TPU v7x, 32 devices: a whole 2x2x4 slice. The times are simulated.
32 devices in a mesh: seq: 16 (over z, x, core), head: 2 (over y).
Axes of the slice: x: 2, y: 2, z: 4, core: 2. Of those that a mesh axis runs over, the one named last changes fastest.
Arguments:
- queries: bfloat16 [4096, 8192], P('seq', 'head'), may hold values from -4.6 to 4.6
- keys: bfloat16 [4096, 1024], P('seq', 'head'), may hold values from -4.6 to 4.6
- values: bfloat16 [4096, 1024], P('seq', 'head'), may hold values from -4 to 4
- key_keep: int32 [4096], P('seq'), may hold values 0 or 1
- global_positions: int32 [384], replicated, may hold values from 0 to 4095
- gain: bfloat16 [8192], P('head'), may hold values from 0.5 to 1.5
- cotangent: bfloat16 [4096, 8192], P('seq', 'head'), may hold values from -6 to 6
Outputs:
- normed: bfloat16 [4096, 8192], P('seq', 'head')
- query_grad: bfloat16 [4096, 8192], P('seq', 'head')
- key_grad: bfloat16 [4096, 1024], P('seq', 'head')
- value_grad: bfloat16 [4096, 1024], P('seq', 'head')
All inputs are finite; a program needn't handle non-finite values. No bound on the sum of `key_keep` on one device may be relied on, other than what follows from the above.
Results may differ from a plain program's by a relative error of at most 0.018.
Values may be sent and summed in bfloat16 or wider, within the bound.
No kernel may reach another device: no remote copies, remote signals or barrier semaphores. Data moves between devices by JAX's collectives and lax.ppermute only.
A program may use at most 64 MiB of HBM per device.

v0:
```python
import jax
import jax.numpy as jnp
from jax import lax
from jax.sharding import PartitionSpec as P

QH = 64
KVH = 8
HD = 128


NEG_FILL = -1e30
NORM_EPS = 1e-06


def from_partner(block, axis, distance):
    count = lax.axis_size(axis)
    route = []
    for low in range(count):
        high = low | 1 << distance
        if high != low and high < count:
            route += [(low, high), (high, low)]
    return lax.ppermute(block, axis, route)


def dot_rows(left, right):
    return lax.dot_general(
        left, right, (((1,), (1,)), ((), ())), preferred_element_type=jnp.float32
    )


def dot_columns(left, right):
    return lax.dot_general(
        left, right, (((0,), (0,)), ((), ())), preferred_element_type=jnp.float32
    )


def per_device(queries, keys, values, key_keep, global_positions, gain, cotangent):
    rows_dev = queries.shape[0]
    kv_heads = keys.shape[1] // HD
    q_heads = queries.shape[1] // HD
    group_size = QH // KVH
    scaling = HD ** (-0.5)
    global_count = global_positions.shape[0]
    bit_count = lax.axis_size("seq").bit_length() - 1
    offset_rows = lax.axis_index("seq") * rows_dev
    bit_order = list(range(bit_count))
    positions = jnp.arange(rows_dev, dtype=jnp.int32)
    key_blocks = [keys]
    value_blocks = [values]
    masks = [(key_keep[None, :] == 1) | (positions[:, None] == positions[None, :])]
    for bit_number in bit_order:
        partner_keys, partner_values, partner_keep = from_partner(
            (keys, values, key_keep), "seq", bit_number
        )
        key_blocks.append(partner_keys)
        value_blocks.append(partner_values)
        masks.append(jnp.broadcast_to(partner_keep[None, :] == 1, (rows_dev, rows_dev)))
    selector = (global_positions[:, None] - offset_rows == positions[None, :]).astype(jnp.float32)
    selector_bf = selector.astype(jnp.bfloat16)
    picked = (
        lax.psum(
            jnp.dot(selector_bf, keys, preferred_element_type=jnp.float32).astype(jnp.bfloat16),
            "seq",
        ).astype(jnp.float32),
        lax.psum(
            jnp.dot(selector_bf, values, preferred_element_type=jnp.float32).astype(jnp.bfloat16),
            "seq",
        ).astype(jnp.float32),
        lax.psum(
            jnp.dot(selector, key_keep.astype(jnp.float32), precision=lax.Precision.HIGHEST).astype(
                jnp.bfloat16
            ),
            "seq",
        ).astype(jnp.float32),
    )
    key_blocks.append(picked[0].astype(jnp.bfloat16))
    value_blocks.append(picked[1].astype(jnp.bfloat16))
    masks.append(jnp.broadcast_to(picked[2][None, :] > 0.5, (rows_dev, global_count)))
    all_keys = jnp.concatenate(key_blocks, 0)
    all_values = jnp.concatenate(value_blocks, 0)
    visible = jnp.concatenate(masks, 1)
    slots = all_keys.shape[0]
    key_stack = all_keys.reshape(slots, kv_heads, HD).transpose(1, 0, 2)
    value_stack = all_values.reshape(slots, kv_heads, HD).transpose(1, 0, 2)
    query_stack = queries.reshape(rows_dev, q_heads, HD).transpose(1, 0, 2)
    heads_order = jnp.arange(q_heads, dtype=jnp.int32)

    def head_scores(head_number, query_rows):
        owner = head_number // group_size
        key_rows = lax.dynamic_index_in_dim(key_stack, owner, 0, keepdims=False)
        value_rows = lax.dynamic_index_in_dim(value_stack, owner, 0, keepdims=False)
        scores = dot_rows(query_rows, key_rows) * scaling
        return (jnp.where(visible, scores, NEG_FILL), owner, key_rows, value_rows)

    def forward_head(operands):
        head_number, query_rows = operands
        scores, owner, key_rows, value_rows = head_scores(head_number, query_rows)
        peak = jnp.max(scores, -1, keepdims=True)
        expo = jnp.exp(scores - peak)
        total = jnp.sum(expo, -1, keepdims=True)
        mixed = (
            jnp.dot(expo.astype(jnp.bfloat16), value_rows, preferred_element_type=jnp.float32)
            / total
        )
        return (mixed, peak[:, 0], total[:, 0])

    attended, peaks, totals = lax.map(forward_head, (heads_order, query_stack))
    attn = attended.transpose(1, 0, 2).reshape(rows_dev, q_heads * HD)
    feature_count = QH * HD
    squares = lax.psum(jnp.sum(attn * attn, -1), "head")
    inverse = lax.rsqrt(squares / feature_count + NORM_EPS)
    gain_wide = gain.astype(jnp.float32)
    normed = (attn * inverse[:, None] * gain_wide).astype(jnp.bfloat16)
    upstream = cotangent.astype(jnp.float32) * gain_wide
    crossed = lax.psum(jnp.sum(upstream * attn, -1), "head")
    d_attn = inverse[:, None] * upstream - attn * (inverse**3 * crossed / feature_count)[:, None]
    d_stack = d_attn.reshape(rows_dev, q_heads, HD).transpose(1, 0, 2)
    d_stack_bf = d_stack.astype(jnp.bfloat16)

    def backward_head(carry, operands):
        head_number, query_rows, grad_rows, grad_rows_bf, attn_rows, peak, total = operands
        scores, owner, key_rows, value_rows = head_scores(head_number, query_rows)
        probs = jnp.exp(scores - peak[:, None]) / total[:, None]
        d_probs = dot_rows(grad_rows_bf, value_rows)
        diag_term = jnp.sum(grad_rows * attn_rows, -1, keepdims=True)
        d_scores = (probs * (d_probs - diag_term)).astype(jnp.bfloat16)
        d_query = jnp.dot(d_scores, key_rows, preferred_element_type=jnp.float32) * scaling
        d_key = dot_columns(d_scores, query_rows) * scaling
        d_value = dot_columns(probs.astype(jnp.bfloat16), grad_rows_bf)
        key_accum, value_accum = carry
        key_accum = lax.dynamic_update_index_in_dim(
            key_accum,
            lax.dynamic_index_in_dim(key_accum, owner, 0, keepdims=False) + d_key,
            owner,
            0,
        )
        value_accum = lax.dynamic_update_index_in_dim(
            value_accum,
            lax.dynamic_index_in_dim(value_accum, owner, 0, keepdims=False) + d_value,
            owner,
            0,
        )
        return ((key_accum, value_accum), d_query)

    zeros_stack = jnp.zeros((kv_heads, slots, HD), jnp.float32)
    (key_accum, value_accum), d_query_stack = lax.scan(
        backward_head,
        (zeros_stack, zeros_stack),
        (heads_order, query_stack, d_stack, d_stack_bf, attended, peaks, totals),
    )
    query_grad = (
        d_query_stack.transpose(1, 0, 2).reshape(rows_dev, q_heads * HD).astype(jnp.bfloat16)
    )
    key_slots = key_accum.transpose(1, 0, 2).reshape(slots, kv_heads * HD)
    value_slots = value_accum.transpose(1, 0, 2).reshape(slots, kv_heads * HD)
    key_running = key_slots[:rows_dev]
    value_running = value_slots[:rows_dev]
    for slot_number, bit_number in enumerate(bit_order):
        lower = rows_dev * (slot_number + 1)
        back_keys, back_values = (
            from_partner(
                key_slots[lower : lower + rows_dev].astype(jnp.bfloat16), "seq", bit_number
            ).astype(jnp.float32),
            from_partner(
                value_slots[lower : lower + rows_dev].astype(jnp.bfloat16), "seq", bit_number
            ).astype(jnp.float32),
        )
        key_running = key_running + back_keys
        value_running = value_running + back_values
    global_start = rows_dev * (len(bit_order) + 1)
    global_keys, global_values = (
        lax.psum(key_slots[global_start:].astype(jnp.bfloat16), "seq").astype(jnp.float32),
        lax.psum(value_slots[global_start:].astype(jnp.bfloat16), "seq").astype(jnp.float32),
    )
    key_running = key_running + lax.dot_general(
        selector, global_keys, (((0,), (0,)), ((), ())), precision=lax.Precision.HIGHEST
    )
    value_running = value_running + lax.dot_general(
        selector, global_values, (((0,), (0,)), ((), ())), precision=lax.Precision.HIGHEST
    )
    return (
        normed,
        query_grad,
        key_running.astype(jnp.bfloat16),
        value_running.astype(jnp.bfloat16),
    )


def solution(mesh):
    placed = (
        P("seq", "head"),
        P("seq", "head"),
        P("seq", "head"),
        P("seq"),
        P(),
        P("head"),
        P("seq", "head"),
    )
    return jax.shard_map(
        per_device,
        mesh=mesh,
        in_specs=placed,
        out_specs=(P("seq", "head"), P("seq", "head"), P("seq", "head"), P("seq", "head")),
        check_vma=False,
    )
```

profile of v0, /device:TPU:0, one launch (start us, length us, event | category | flops | bytes accessed | tf_op | source)
XLA Modules:
  0.0 1053.8 jit_solution(13176667561894845022)
XLA Ops:
  7.2 3.1 collective-permute-start.6
  11.8 2.6 collective-permute-start.7
  22.5 31.7 %psum.50 = bf16[384]{0:T(512)(128)(2,1)S(1)} all-reduce(bf16[384]{0:T(512)(128)(2,1)S(1)} %convolution_reduce_fusion), channel_id=1, replica_groups=mesh['seq'=16,'head'=2] {'seq'}, use_global_device_ids=true, to_apply=%region_2.0 | all-reduce | flops 384 | bytes 1536 | tf_op jit(solution)/shard_map/psum | solution.py:69
  55.0 3.3 copy.26
  58.3 2.9 copy.29
  68.4 2.5 collective-permute-done.2
  72.3 5.4 collective-permute-done.9
  79.7 34.8 %all-reduce.8.cloned.1.call-done = (bf16[384,512]{1,0:T(8,128)(2,1)}, bf16[384,512]{1,0:T(8,128)(2,1)}) async-done(((bf16[384,512]{1,0:T(8,128)(2,1)}, bf16[384,512]{1,0:T(8,128)(2,1)}), (bf16[384,512]{1,0:T(8,128)(2,1)}, bf16[384,512]{1,0:T(8,128)(2,1)})) %all-reduce.8.cloned.1.call-update) | async-done | bytes 786448 | tf_op jit(solution)/shard_map/psum | solution.py:61
  116.5 2.9 bitcast_bitcast_fusion.2
  120.9 235.7 %while.34 = (s32[]{:T(128)}, f32[32,256,128]{2,1,0:T(8,128)}, f32[32,256]{1,0:T(8,128)S(1)}, f32[32,256]{1,0:T(8,128)S(1)}, bf16[32,256,128]{2,1,0:T(8,128)(2,1)...) while((s32[]{:T(128)}, f32[32,256,128]{2,1,0:T(8,128)}, ...), condition=%wide.region_6.7_spmd.clone, body=%wide.region_3.6_spmd.sunk.clone | while | flops 221117968 | bytes 6595905 | solution.py:107
  126.1 2.1 fusion.130
  133.5 2.1 fusion.130
  140.9 2.1 fusion.130
  148.2 2.1 fusion.130
  155.6 2.1 fusion.130
  163.0 2.1 fusion.130
  170.4 2.1 fusion.130
  177.7 2.1 fusion.130
  185.1 2.1 fusion.130
  192.5 2.1 fusion.130
  199.8 2.1 fusion.130
  207.2 2.1 fusion.130
  214.6 2.1 fusion.130
  221.9 2.1 fusion.130
  229.3 2.1 fusion.130
  236.6 2.1 fusion.130
  244.0 2.1 fusion.130
  251.4 2.1 fusion.130
  258.7 2.1 fusion.130
  266.1 2.1 fusion.130
  273.5 2.1 fusion.130
  280.8 2.1 fusion.130
  288.2 2.1 fusion.130
  295.5 2.1 fusion.130
  302.9 2.1 fusion.130
  310.3 2.1 fusion.130
  317.6 2.1 fusion.130
  325.0 2.1 fusion.130
  332.4 2.1 fusion.130
  339.7 2.1 fusion.130
  347.1 2.1 fusion.130
  354.5 2.1 fusion.130
  356.6 2.7 fusion.51
  360.0 2.4 fusion.48
  362.4 5.1 all-reduce
  367.6 4.8 fusion.50
  374.2 2.5 copy.78
  380.6 547.9 %while.35 = (s32[]{:T(128)}, f32[4,1664,128]{1,2,0:T(8,128)}, f32[4,1664,128]{1,2,0:T(8,128)}, bf16[32,256,128]{2,1,0:T(8,128)(2,1)}, s32[32]{0:T(128)S(1)}, /*i...) while((s32[]{:T(128)}, f32[4,1664,128]{1,2,0:T(8,128)}, ...), condition=%wide.region_13.14_spmd.clone, body=%wide.region_11.13_spmd.sunk.clone | while | flops 549404416 | bytes 27074952 | solution.py:146
  411.6 2.0 fusion.145
  445.9 2.0 fusion.145
  463.1 2.0 fusion.145
  480.3 2.0 fusion.145
  531.8 2.0 fusion.145
  548.9 2.0 fusion.145
  668.8 2.0 fusion.145
  702.9 2.0 fusion.145
  822.5 2.0 fusion.145
  873.8 2.0 fusion.145
  890.9 2.0 fusion.145
  928.5 2.1 bitcast_convert_fusion.1
  932.4 2.2 copy.47
  945.8 3.2 copy_bitcast_fusion
  958.5 84.8 %all-reduce.6.cloned.1.call-done = (bf16[384,512]{0,1:T(8,128)(2,1)}, bf16[384,512]{0,1:T(8,128)(2,1)}) async-done(((bf16[384,512]{0,1:T(8,128)(2,1)}, bf16[384,512]{0,1:T(8,128)(2,1)}), (bf16[384,512]{0,1:T(8,128)(2,1)}, bf16[384,512]{0,1:T(8,128)(2,1)})) %all-reduce.6.cloned.1.call-update) | async-done | bytes 786448 | tf_op jit(solution)/shard_map/psum | solution.py:172
  1043.2 2.5 add_convert_fusion.1
  (782 shorter events, 579.1 us)
Async XLA Ops:
  7.2 12.4 %copy-start.10 = (s32[256]{0:T(256)S(1)}, s32[256]{0:T(256)}, u32[]{:S(2)}) copy-start(s32[256]{0:T(256)} %param.14) | copy-start | bytes 3076
  7.2 12.4 %copy-start.6 = (bf16[256,512]{1,0:T(8,128)(2,1)S(1)}, bf16[256,512]{1,0:T(8,128)(2,1)}, u32[]{:S(2)}) copy-start(bf16[256,512]{1,0:T(8,128)(2,1)} %param.12) | copy-start | bytes 786436
  7.2 107.4 %all-reduce.8.cloned.1.call-start = ((), (), s32[]{:S(2)}) async-start(), calls=%async_computation.1 | async-start | bytes 1572864 | tf_op jit(solution)/shard_map/psum | solution.py:61
  7.2 54.1 %collective-permute-start.6 = (s32[256]{0:T(256)}, s32[256]{0:T(256)S(1)}, u32[]{:S(2)}, u32[]{:S(2)}) collective-permute-start(s32[256]{0:T(256)} %param.14), channel_id=1, source_target_pairs={{0,8},{8,0},{2,10},{10,2},{4,12},{12,4},{6,14},{14,6},{16,24},{24,... | collective-permute-start | bytes 3080 | tf_op jit(solution)/shard_map/ppermute | solution.py:22
  10.3 50.9 %collective-permute-start.5 = (s32[256]{0:T(256)}, s32[256]{0:T(256)S(1)}, u32[]{:S(2)}, u32[]{:S(2)}) collective-permute-start(s32[256]{0:T(256)} %param.14), channel_id=1, source_target_pairs={{0,4},{4,0},{2,6},{6,2},{8,12},{12,8},{10,14},{14,10},{16,20},{20,... | collective-permute-start | bytes 3080 | tf_op jit(solution)/shard_map/ppermute | solution.py:22
  11.8 49.3 %collective-permute-start.4 = (s32[256]{0:T(256)}, s32[256]{0:T(256)S(1)}, u32[]{:S(2)}, u32[]{:S(2)}) collective-permute-start(s32[256]{0:T(256)} %param.14), channel_id=1, source_target_pairs={{0,2},{2,0},{4,6},{6,4},{8,10},{10,8},{12,14},{14,12},{16,18},{18,... | collective-permute-start | bytes 3080 | tf_op jit(solution)/shard_map/ppermute | solution.py:22
  11.8 49.7 %collective-permute-start.7 = (s32[256]{0:T(256)}, s32[256]{0:T(256)S(1)}, u32[]{:S(2)}, u32[]{:S(2)}) collective-permute-start(s32[256]{0:T(256)} %param.14), channel_id=1, source_target_pairs={{0,16},{16,0},{2,18},{18,2},{4,20},{20,4},{6,22},{22,6},{8,24},{24... | collective-permute-start | bytes 3080 | tf_op jit(solution)/shard_map/ppermute | solution.py:22
  14.4 57.2 %collective-permute-start.3 = (bf16[256,512]{1,0:T(8,128)(2,1)}, bf16[256,512]{1,0:T(8,128)(2,1)S(1)}, u32[]{:S(2)}, u32[]{:S(2)}) collective-permute-start(bf16[256,512]{1,0:T(8,128)(2,1)} %param.12), channel_id=1, source_target_pairs={{0,16},{16,0},{2,18},{18,2},{4,20},{20,4},{6,22},{22,6},{8,24},{24... | collective-permute-start | bytes 786440 | tf_op jit(solution)/shard_map/ppermute | solution.py:22
  19.4 34.8 %copy-start.7 = (bf16[256,512]{1,0:T(8,128)(2,1)S(1)}, bf16[256,512]{1,0:T(8,128)(2,1)}, u32[]{:S(2)}) copy-start(bf16[256,512]{1,0:T(8,128)(2,1)} %param.13) | copy-start | bytes 786436
  19.5 35.5 %copy-start.9 = (bf16[4096]{0:T(1024)(128)(2,1)S(1)}, bf16[4096]{0:T(1024)(128)(2,1)}, u32[]{:S(2)}) copy-start(bf16[4096]{0:T(1024)(128)(2,1)} %param.16) | copy-start | bytes 24580
  19.5 1023.8 %all-reduce.6.cloned.1.call-start = ((), (), s32[]{:S(2)}) async-start(), calls=%async_computation | async-start | bytes 1572864 | tf_op jit(solution)/shard_map/psum | solution.py:172
  61.1 9.7 collective-permute-start.2
  61.2 6.4 collective-permute-start.1
  61.3 1.7 collective-permute-start
  61.5 18.2 %collective-permute-start.11 = (bf16[256,512]{1,0:T(8,128)(2,1)S(1)}, bf16[256,512]{1,0:T(8,128)(2,1)S(1)}, u32[]{:S(2)}, u32[]{:S(2)}) collective-permute-start(bf16[256,512]{1,0:T(8,128)(2,1)S(1)} %copy-done.7), channel_id=1, source_target_pairs={{0,16},{16,0},{2,18},{18,2},{4,20},{20,4},{6,22},{22,6},{8,24},{24... | collective-permute-start | bytes 786440 | tf_op jit(solution)/shard_map/ppermute | solution.py:22
  62.0 10.4 copy-start.5
  63.0 16.6 %collective-permute-start.10 = (bf16[256,512]{1,0:T(8,128)(2,1)S(1)}, bf16[256,512]{1,0:T(8,128)(2,1)S(1)}, u32[]{:S(2)}, u32[]{:S(2)}) collective-permute-start(bf16[256,512]{1,0:T(8,128)(2,1)S(1)} %copy-done.7), channel_id=1, source_target_pairs={{0,8},{8,0},{2,10},{10,2},{4,12},{12,4},{6,14},{14,6},{16,24},{24,... | collective-permute-start | bytes 786440 | tf_op jit(solution)/shard_map/ppermute | solution.py:22
  67.6 4.7 collective-permute-start.8
  70.9 6.8 collective-permute-start.9
  356.6 3.4 copy-start
  360.0 7.5 copy-start.2
  931.5 12.0 %copy-start.1 = (f32[4,1664,128]{1,2,0:T(8,128)S(1)}, f32[4,1664,128]{1,2,0:T(8,128)}, u32[]{:S(2)}) copy-start(f32[4,1664,128]{1,2,0:T(8,128)} %get-tuple-element.301) | copy-start | bytes 10223620
  940.0 16.3 %collective-permute-start.13 = (bf16[256,512]{1,0:T(8,128)(2,1)}, bf16[256,512]{1,0:T(8,128)(2,1)}, u32[]{:S(2)}, u32[]{:S(2)}) collective-permute-start(bf16[256,512]{1,0:T(8,128)(2,1)} %copy.48), channel_id=1, source_target_pairs={{0,4},{4,0},{2,6},{6,2},{8,12},{12,8},{10,14},{14,10},{16,20},{20,... | collective-permute-start | bytes 786440 | tf_op jit(solution)/shard_map/ppermute | solution.py:22
  941.5 15.5 %collective-permute-start.14 = (bf16[256,512]{1,0:T(8,128)(2,1)}, bf16[256,512]{1,0:T(8,128)(2,1)}, u32[]{:S(2)}, u32[]{:S(2)}) collective-permute-start(bf16[256,512]{1,0:T(8,128)(2,1)} %copy.49), channel_id=1, source_target_pairs={{0,8},{8,0},{2,10},{10,2},{4,12},{12,4},{6,14},{14,6},{16,24},{24,... | collective-permute-start | bytes 786440 | tf_op jit(solution)/shard_map/ppermute | solution.py:22
  942.0 16.4 %collective-permute-start.15 = (bf16[256,512]{1,0:T(8,128)(2,1)}, bf16[256,512]{1,0:T(8,128)(2,1)}, u32[]{:S(2)}, u32[]{:S(2)}) collective-permute-start(bf16[256,512]{1,0:T(8,128)(2,1)} %copy.50), channel_id=1, source_target_pairs={{0,16},{16,0},{2,18},{18,2},{4,20},{20,4},{6,22},{22,6},{8,24},{24... | collective-permute-start | bytes 786440 | tf_op jit(solution)/shard_map/ppermute | solution.py:22
  943.4 15.0 %collective-permute-start.12 = (bf16[256,512]{1,0:T(8,128)(2,1)}, bf16[256,512]{1,0:T(8,128)(2,1)}, u32[]{:S(2)}, u32[]{:S(2)}) collective-permute-start(bf16[256,512]{1,0:T(8,128)(2,1)} %copy.47), channel_id=1, source_target_pairs={{0,2},{2,0},{4,6},{6,4},{8,10},{10,8},{12,14},{14,12},{16,18},{18,... | collective-permute-start | bytes 786440 | tf_op jit(solution)/shard_map/ppermute | solution.py:22
  943.6 1.3 copy-start.3
  949.8 2.7 copy-start.4
  954.9 90.9 %collective-permute-start.17 = (bf16[256,512]{1,0:T(8,128)(2,1)S(1)}, bf16[256,512]{1,0:T(8,128)(2,1)S(1)}, u32[]{:S(2)}, u32[]{:S(2)}) collective-permute-start(bf16[256,512]{1,0:T(8,128)(2,1)S(1)} %copy.53), channel_id=1, source_target_pairs={{0,4},{4,0},{2,6},{6,2},{8,12},{12,8},{10,14},{14,10},{16,20},{20,... | collective-permute-start | bytes 786440 | tf_op jit(solution)/shard_map/ppermute | solution.py:22
  956.3 89.5 %collective-permute-start.18 = (bf16[256,512]{1,0:T(8,128)(2,1)S(1)}, bf16[256,512]{1,0:T(8,128)(2,1)S(1)}, u32[]{:S(2)}, u32[]{:S(2)}) collective-permute-start(bf16[256,512]{1,0:T(8,128)(2,1)S(1)} %copy.54), channel_id=1, source_target_pairs={{0,8},{8,0},{2,10},{10,2},{4,12},{12,4},{6,14},{14,6},{16,24},{24,... | collective-permute-start | bytes 786440 | tf_op jit(solution)/shard_map/ppermute | solution.py:22
  957.0 88.8 %collective-permute-start.19 = (bf16[256,512]{1,0:T(8,128)(2,1)S(1)}, bf16[256,512]{1,0:T(8,128)(2,1)S(1)}, u32[]{:S(2)}, u32[]{:S(2)}) collective-permute-start(bf16[256,512]{1,0:T(8,128)(2,1)S(1)} %copy.55), channel_id=1, source_target_pairs={{0,16},{16,0},{2,18},{18,2},{4,20},{20,4},{6,22},{22,6},{8,24},{24... | collective-permute-start | bytes 786440 | tf_op jit(solution)/shard_map/ppermute | solution.py:22
  958.5 87.3 %collective-permute-start.16 = (bf16[256,512]{1,0:T(8,128)(2,1)S(1)}, bf16[256,512]{1,0:T(8,128)(2,1)S(1)}, u32[]{:S(2)}, u32[]{:S(2)}) collective-permute-start(bf16[256,512]{1,0:T(8,128)(2,1)S(1)} %copy.52), channel_id=1, source_target_pairs={{0,2},{2,0},{4,6},{6,4},{8,10},{10,8},{12,14},{14,12},{16,18},{18,... | collective-permute-start | bytes 786440 | tf_op jit(solution)/shard_map/ppermute | solution.py:22
  1043.2 2.5 copy-start.8
Sparse Core Ops, SparseCore 0:
  19.6 94.9 all-reduce.7
  945.9 97.3 all-reduce.5
where the time goes:
time: 1070 us; the launch traced here: 1050 us
  matrix products  376 us (35%)
  local copies, waits for them, and re-layouts  247 us (23%)
  loops' own time  169 us (16%)
  waiting for transfers between devices  131 us (12%)
  other arithmetic  61.7 us (6%)
  blocking collectives  36.9 us (3%)
  starting transfers between devices  17.1 us (2%)
  between operations  14.4 us (1%)
    dot_general x96, matrix products, dot_rows(): lax.dot_general(left, right, (((1,), (1,)), ((), ())), preferred_element_...  154 us
    another operation x1, loops' own time, per_device(): lax.scan(backward_head, (zeros_stack, zeros_stack), (heads_order, query_s...  85.1 us
    psum x1, waiting for transfers between devices, per_device(): lax.psum(key_slots[global_start:].astype(jnp.bfloat16), 'seq')  84.8 us
    another operation x1, loops' own time, per_device(): attended, peaks, totals = lax.map(forward_head, (heads_order, query_stack))  84.1 us
    dot_general x64, matrix products, dot_columns(): lax.dot_general(left, right, (((0,), (0,)), ((), ())), preferred_element_...  82 us
    dot_general x32, matrix products, forward_head(): jnp.dot(expo.astype(jnp.bfloat16), value_rows, preferred_element_type=jnp...  67.4 us
    dot_general x32, matrix products, backward_head(): jnp.dot(d_scores, key_rows, preferred_element_type=jnp.float32) * scaling  64.5 us
    dynamic_update_slice x64, local copies, waits for them, and re-layouts, backward_head(): lax.dynamic_update_index_in_dim(value_accum, lax.dynamic_index_in_dim(val...  52.2 us
  transfers between devices with their start and end apart: 22, of which 6 were waited for; matrix products, arithmetic and copies ran while one was open for 3% of the time, Pallas kernels for 0%

commit v1 on v0

v1 whole, which is shorter than its diff:
```python
import functools
import math

import jax
import jax.numpy as jnp
from jax import lax
from jax.experimental import pallas as pl
from jax.experimental.pallas import tpu as pltpu
from jax.sharding import PartitionSpec as P

QH = 64
KVH = 8
HD = 128
GROUP = QH // KVH

NEG_FILL = -1e30
NORM_EPS = 1e-06
HIDDEN = 256.0
HIDDEN_ABOVE = 100.0
SCALING = HD ** (-0.5)
EXPONENT = SCALING * math.log2(math.e)
VMEM_BYTES = 56 * 2**20

F32 = jnp.float32
BF16 = jnp.bfloat16


def dot_nt(left, right):
    return lax.dot_general(left, right, (((1,), (1,)), ((), ())), preferred_element_type=F32)


def dot_nn(left, right):
    return lax.dot_general(left, right, (((1,), (0,)), ((), ())), preferred_element_type=F32)


def dot_tn(left, right):
    return lax.dot_general(left, right, (((0,), (0,)), ((), ())), preferred_element_type=F32)


def swap(block, axis, mask):
    count = lax.axis_size(axis)
    return lax.ppermute(block, axis, [(i, i ^ mask) for i in range(count)])


def params():
    return pltpu.CompilerParams(vmem_limit_bytes=VMEM_BYTES)


def cost(flops, moved, expos=0):
    return pl.CostEstimate(flops=int(flops), bytes_accessed=int(moved), transcendentals=int(expos))


def lane_of(shape):
    return lax.broadcasted_iota(jnp.int32, shape, 1)


def read_global(refs, core_ref):
    count = len(refs) // 2
    mine = jnp.concatenate([r[...] for r in refs[:count]], 0)
    other = jnp.concatenate([r[...] for r in refs[count:]], 0)
    first = core_ref[0] == 0
    return jnp.where(first, mine, other), jnp.where(first, other, mine)


def forward_kernel(blocks, own, is_global, first, last, *refs):
    refs = list(refs)
    take = refs.pop
    q_ref = take(0)
    if is_global:
        core_ref = take(0)
        parts = [take(0) for _ in range(blocks)]
        key_list, value_list = [[x] for x in read_global(parts, core_ref)]
    else:
        key_list, value_list = [], []
        for _ in range(blocks):
            key_list.append(take(0)[...])
            value_list.append(take(0)[...])
    bias_ref = take(0) if own else None
    if not first:
        sum_ref, peak_ref, total_ref = take(0), take(0), take(0)
    if last:
        cot_ref, gain_ref = take(0), take(0)
    p_ref, out_ref, peak_out, total_out = take(0), take(0), take(0), take(0)
    if last:
        rows_ref, square_acc, cross_acc = take(0), take(0), take(0)
        step = pl.program_id(0)

        @pl.when(step == 0)
        def _():
            square_acc[...] = jnp.zeros_like(square_acc)
            cross_acc[...] = jnp.zeros_like(cross_acc)

    rows = q_ref.shape[0]
    unit = (lane_of((rows, HD)) == 0).astype(BF16)
    lanes = lane_of((rows, HD))
    wide_keys, wide_values = [], []
    for number, (k, v) in enumerate(zip(key_list, value_list)):
        if own and number == 0:
            extra = jnp.zeros_like(k)
        else:
            hidden = (lane_of(k.shape) == 0) & (k.astype(F32) > HIDDEN_ABOVE)
            extra = jnp.where(hidden, NEG_FILL, 0.0).astype(BF16)
        wide_keys.append(jnp.concatenate([k, extra], 1))
        wide_values.append(jnp.concatenate([v, jnp.ones_like(v)], 1))

    def scores_of(head):
        q = jnp.concatenate([q_ref[:, head * HD : (head + 1) * HD], unit], 1)
        out = []
        for number, k in enumerate(wide_keys):
            s = dot_nt(q, k)
            if own and number == 0:
                s = s + bias_ref[...]
            out.append(s)
        return out

    peaks = jnp.zeros((rows, HD), F32)
    totals = jnp.ones((rows, HD), F32)
    ahead = scores_of(0)
    for head in range(GROUP):
        scores = ahead
        if head + 1 < GROUP:
            ahead = scores_of(head + 1)
        peak = functools.reduce(
            jnp.maximum, [jnp.max(s, -1, keepdims=True) for s in scores]
        )
        if not first:
            before = peak_ref[:, head : head + 1]
            peak = jnp.maximum(peak, before)
        mixed = None
        start = 0
        for s, v in zip(scores, wide_values):
            e = jnp.exp2((s - peak) * EXPONENT).astype(BF16)
            p_ref[head * rows : (head + 1) * rows, start : start + s.shape[1]] = e
            start += s.shape[1]
            part = dot_nn(e, v)
            mixed = part if mixed is None else mixed + part
        value_sum = mixed[:, :HD]
        total = mixed[:, HD:]
        here = slice(head * HD, (head + 1) * HD)
        if not first:
            shrink = jnp.exp2((before - peak) * EXPONENT)
            value_sum = value_sum + sum_ref[:, here] * shrink
            total = total + total_ref[:, head : head + 1] * shrink
        if last:
            inverse_total = 1.0 / total
            attn = value_sum * inverse_total
            out_ref[:, here] = attn
            totals = jnp.where(lanes == head, inverse_total, totals)
            upstream = cot_ref[:, here].astype(F32) * gain_ref[:, here].astype(F32)
            square_acc[...] += attn * attn
            cross_acc[...] += upstream * attn
        else:
            out_ref[:, here] = value_sum
            totals = jnp.where(lanes == head, total, totals)
        peaks = jnp.where(lanes == head, peak, peaks)
    peak_out[...] = peaks
    total_out[...] = totals
    if last:

        @pl.when(step == pl.num_programs(0) - 1)
        def _():
            squares = jnp.sum(square_acc[...].T, 0, keepdims=True)
            crosses = jnp.sum(cross_acc[...].T, 0, keepdims=True)
            rows_ref[...] = jnp.concatenate([squares, crosses], 0)


def column_block(rows, width):
    return pl.BlockSpec((rows, width), lambda a: (0, a))


def fixed_block(shape):
    return pl.BlockSpec(shape, lambda a: (0,) * len(shape))


SCALAR = pl.BlockSpec(memory_space=pltpu.SMEM)


def forward_phase(name, queries, pairs, core=None, bias=None, before=None, norm=None):
    rows, width = queries.shape
    steps = width // (GROUP * HD)
    wide = GROUP * HD
    args, specs = [queries], [column_block(rows, wide)]
    is_global = core is not None
    if is_global:
        args.append(core)
        specs.append(SCALAR)
        flat = pairs
        slots = sum(x.shape[0] for x in pairs) // 2
    else:
        flat = [x for pair in pairs for x in pair]
        slots = sum(k.shape[0] for k, _ in pairs)
    for x in flat:
        args.append(x)
        specs.append(column_block(x.shape[0], HD))
    if bias is not None:
        args.append(bias)
        specs.append(fixed_block(bias.shape))
    if before is not None:
        args += list(before)
        specs += [column_block(rows, wide), column_block(rows, HD), column_block(rows, HD)]
    if norm is not None:
        cotangent, gain = norm
        args += [cotangent, gain]
        specs += [column_block(rows, wide), column_block(1, wide)]
    out_shapes = [
        jax.ShapeDtypeStruct((steps * GROUP * rows, slots), BF16),
        jax.ShapeDtypeStruct((rows, width), F32),
        jax.ShapeDtypeStruct((rows, steps * HD), F32),
        jax.ShapeDtypeStruct((rows, steps * HD), F32),
    ]
    out_specs = [
        pl.BlockSpec((GROUP * rows, slots), lambda a: (a, 0)),
        column_block(rows, wide),
        column_block(rows, HD),
        column_block(rows, HD),
    ]
    scratch = []
    if norm is not None:
        out_shapes.append(jax.ShapeDtypeStruct((2, rows), F32))
        out_specs.append(fixed_block((2, rows)))
        scratch = [pltpu.VMEM((rows, HD), F32), pltpu.VMEM((rows, HD), F32)]
    elements = rows * slots * steps * GROUP
    return pl.pallas_call(
        functools.partial(
            forward_kernel,
            len(pairs),
            bias is not None,
            is_global,
            before is None,
            norm is not None,
        ),
        grid=(steps,),
        in_specs=specs,
        out_specs=out_specs,
        out_shape=out_shapes,
        scratch_shapes=scratch,
        compiler_params=params(),
        cost_estimate=cost(8 * elements * HD, 2 * elements, elements),
        name=name,
    )(*args)


def backward_kernel(blocks, own, is_global, first, last, features, *refs):
    refs = list(refs)
    take = refs.pop
    q_ref, p_ref = take(0), take(0)
    if is_global:
        core_ref = take(0)
        parts = [take(0) for _ in range(blocks)]
        sizes = [r.shape[0] for r in parts[: blocks // 2]]
        key_list, value_list = [[x] for x in read_global(parts, core_ref)]
    else:
        key_list, value_list = [], []
        for _ in range(blocks):
            key_list.append(take(0)[...])
            value_list.append(take(0)[...])
    peak_ref, last_peak_ref, inverse_ref = take(0), take(0), take(0)
    if first:
        norm_ref, attn_ref, cot_ref, gain_ref = take(0), take(0), take(0), take(0)
    else:
        grad_ref, diag_ref, dq_ref = take(0), take(0), take(0)
    outs = [take(0) for _ in range(blocks if is_global else 2 * blocks)]
    dq_out = take(0)
    if first:
        normed_out, grad_out, diag_out = take(0), take(0), take(0)
    ds_ref, q_stack, grad_stack = take(0), take(0), take(0)

    rows = q_ref.shape[0]
    lanes = lane_of((rows, HD))
    factors = jnp.exp2((peak_ref[...] - last_peak_ref[...]) * EXPONENT) * inverse_ref[...]
    if first:
        squares = norm_ref[0:1, :]
        crossed = norm_ref[1:2, :]
        inverse_row = lax.rsqrt(squares / features + NORM_EPS)
        coefficient_row = inverse_row * inverse_row * inverse_row * crossed / features
        inverse_wide = jnp.broadcast_to(inverse_row, (HD, rows)).T
        coefficient_wide = jnp.broadcast_to(coefficient_row, (HD, rows)).T
        diags = jnp.zeros((rows, HD), F32)
    for head in range(GROUP):
        here = slice(head * HD, (head + 1) * HD)
        stack = slice(head * rows, (head + 1) * rows)
        factor = factors[:, head : head + 1]
        if first:
            attn = attn_ref[:, here]
            gain = gain_ref[:, here].astype(F32)
            normed_out[:, here] = (attn * inverse_wide * gain).astype(BF16)
            upstream = cot_ref[:, here].astype(F32) * gain
            grad = inverse_wide * upstream - attn * coefficient_wide
            grad_out[:, here] = grad
            diag = jnp.sum(grad * attn, -1, keepdims=True)
            diags = jnp.where(lanes == head, diag, diags)
        else:
            grad = grad_ref[:, here]
            diag = diag_ref[:, head : head + 1]
        grad_bf = (grad * factor).astype(BF16)
        scaled_diag = diag * factor
        grad_stack[stack, :] = grad_bf
        q_stack[stack, :] = q_ref[:, here]
        start = 0
        d_query = None
        for k, v in zip(key_list, value_list):
            columns = slice(start, start + k.shape[0])
            d_probs = dot_nt(grad_bf, v)
            d_scores = (p_ref[stack, columns].astype(F32) * (d_probs - scaled_diag)).astype(BF16)
            ds_ref[stack, columns] = d_scores
            part = dot_nn(d_scores, k)
            d_query = part if d_query is None else d_query + part
            start += k.shape[0]
        if not first:
            d_query = d_query + dq_ref[:, here]
        if last:
            d_query = d_query * SCALING
        dq_out[:, here] = d_query.astype(dq_out.dtype)
    if first:
        diag_out[...] = diags
    q_all, grad_all = q_stack[...], grad_stack[...]
    if is_global:
        d_key = (dot_tn(q_all, ds_ref[...]) * SCALING).T.astype(BF16)
        d_value = dot_tn(grad_all, p_ref[...]).T.astype(BF16)
        core_first = core_ref[0] == 0
        mine = jnp.where(core_first, d_key, d_value)
        other = jnp.where(core_first, d_value, d_key)
        start = 0
        for number, size in enumerate(sizes):
            outs[number][...] = mine[start : start + size]
            outs[number + blocks // 2][...] = other[start : start + size]
            start += size
    else:
        start = 0
        for number, k in enumerate(key_list):
            columns = slice(start, start + k.shape[0])
            start += k.shape[0]
            d_key = (dot_tn(q_all, ds_ref[:, columns]) * SCALING).T
            d_value = dot_tn(grad_all, p_ref[:, columns]).T
            outs[2 * number][...] = d_key.astype(outs[2 * number].dtype)
            outs[2 * number + 1][...] = d_value.astype(outs[2 * number + 1].dtype)


def backward_phase(
    name, queries, probs, pairs, peaks, last_peaks, inverse, own=False, core=None,
    norm=None, grads=None, last=False,
):
    rows, width = queries.shape
    steps = width // (GROUP * HD)
    wide = GROUP * HD
    slots = probs.shape[1]
    args = [queries, probs]
    specs = [column_block(rows, wide), pl.BlockSpec((GROUP * rows, slots), lambda a: (a, 0))]
    is_global = core is not None
    if is_global:
        args.append(core)
        specs.append(SCALAR)
        flat = pairs
    else:
        flat = [x for pair in pairs for x in pair]
    out_shapes, out_specs = [], []
    for number, x in enumerate(flat):
        args.append(x)
        specs.append(column_block(x.shape[0], HD))
        kind = F32 if own and number < 2 else BF16
        out_shapes.append(jax.ShapeDtypeStruct(x.shape, kind))
        out_specs.append(column_block(x.shape[0], HD))
    args += [peaks, last_peaks, inverse]
    specs += [column_block(rows, HD)] * 3
    if norm is not None:
        sums, attn, cotangent, gain = norm
        args += [sums, attn, cotangent, gain]
        specs += [
            fixed_block(sums.shape),
            column_block(rows, wide),
            column_block(rows, wide),
            column_block(1, wide),
        ]
    else:
        args += list(grads)
        specs += [column_block(rows, wide), column_block(rows, HD), column_block(rows, wide)]
    out_shapes.append(jax.ShapeDtypeStruct((rows, width), BF16 if last else F32))
    out_specs.append(column_block(rows, wide))
    if norm is not None:
        out_shapes += [
            jax.ShapeDtypeStruct((rows, width), BF16),
            jax.ShapeDtypeStruct((rows, width), F32),
            jax.ShapeDtypeStruct((rows, steps * HD), F32),
        ]
        out_specs += [
            column_block(rows, wide),
            column_block(rows, wide),
            column_block(rows, HD),
        ]
    elements = rows * slots * steps * GROUP
    return pl.pallas_call(
        functools.partial(
            backward_kernel, len(pairs), own, is_global, norm is not None, last, QH * HD
        ),
        grid=(steps,),
        in_specs=specs,
        out_specs=out_specs,
        out_shape=out_shapes,
        scratch_shapes=[
            pltpu.VMEM((GROUP * rows, slots), BF16),
            pltpu.VMEM((GROUP * rows, HD), BF16),
            pltpu.VMEM((GROUP * rows, HD), BF16),
        ],
        compiler_params=params(),
        cost_estimate=cost(12 * elements * HD, 2 * elements),
        name=name,
    )(*args)


def pick_kernel(core_ref, spots_ref, k_ref, v_ref, pk_ref, pv_ref, out_ref):
    rows = k_ref.shape[0]
    count = spots_ref.shape[1]
    first = core_ref[0] == 0
    row_ids = lax.broadcasted_iota(jnp.int32, (rows, count), 0)
    total = None
    for number, (k, v) in enumerate(((k_ref, v_ref), (pk_ref, pv_ref))):
        source = jnp.where(first, k[...], v[...])
        chosen = jnp.where(row_ids == spots_ref[number : number + 1, :], 1.0, 0.0).astype(BF16)
        part = dot_tn(chosen, source)
        total = part if total is None else total + part
    out_ref[...] = total.astype(BF16)


def pick(core, spots, keys, values, partner_keys, partner_values):
    full = pl.BlockSpec(memory_space=pltpu.VMEM)
    shape = (spots.shape[1], keys.shape[1])
    return pl.pallas_call(
        pick_kernel,
        in_specs=[SCALAR] + [full] * 5,
        out_specs=full,
        out_shape=jax.ShapeDtypeStruct(shape, BF16),
        compiler_params=params(),
        cost_estimate=cost(4 * shape[0] * shape[1] * keys.shape[0], 3 * 2**20),
        name="pick_globals",
    )(core, spots, keys, values, partner_keys, partner_values)


def finish_kernel(partners, parts, *refs):
    core_ref, spots_ref = refs[0], refs[1]
    own = refs[2:4]
    back = refs[4 : 4 + 2 * partners]
    total = refs[4 + 2 * partners : 4 + 2 * partners + 2 * parts]
    outs = refs[4 + 2 * partners + 2 * parts :]
    rows = own[0].shape[0]
    count = spots_ref.shape[1]
    row_ids = lax.broadcasted_iota(jnp.int32, (rows, count), 0)
    chosen = jnp.where(row_ids == spots_ref[0:1, :], 1.0, 0.0).astype(BF16)
    global_grads = read_global(total, core_ref)
    for kind in range(2):
        running = own[kind][...]
        for number in range(partners):
            running = running + back[2 * number + kind][...].astype(F32)
        running = running + dot_nn(chosen, global_grads[kind])
        outs[kind][...] = running.astype(BF16)


def finish(core, spots, own, back, total):
    full = pl.BlockSpec(memory_space=pltpu.VMEM)
    args = list(own) + list(back) + list(total)
    return pl.pallas_call(
        functools.partial(finish_kernel, len(back) // 2, len(total) // 2),
        in_specs=[SCALAR] + [full] * (len(args) + 1),
        out_specs=[full] * 2,
        out_shape=[jax.ShapeDtypeStruct(own[0].shape, BF16)] * 2,
        compiler_params=params(),
        cost_estimate=cost(2**28, 4 * 2**20),
        name="finish_key_value_grads",
    )(core, spots, *args)


def levels_of(bit_count):
    bits = list(range(1, bit_count))
    levels = []
    while bits:
        levels.insert(0, bits[-2:])
        bits = bits[:-2]
    return levels


def masks_of(level):
    return [
        sum(1 << bit for place, bit in enumerate(level) if number >> place & 1)
        for number in range(1 << len(level))
    ]


def reduce_level(block, masks):
    size = block.shape[0] // len(masks)
    running = block[:size].astype(F32)
    for number, mask in enumerate(masks):
        if number:
            moved = swap(block[number * size : (number + 1) * size], "seq", mask)
            running = running + moved.astype(F32)
    return running.astype(BF16)


def gather_level(block, masks):
    return [block if mask == 0 else swap(block, "seq", mask) for mask in masks]


def per_device(queries, keys, values, key_keep, global_positions, gain, cotangent):
    rows = queries.shape[0]
    bit_count = lax.axis_size("seq").bit_length() - 1
    place = lax.axis_index("seq")
    core = (place & 1).reshape(1)
    global_count = global_positions.shape[0]

    marked = jnp.where(key_keep[:, None] == 1, keys, jnp.asarray(HIDDEN, BF16))
    near = [(swap(marked, "seq", 1 << bit), swap(values, "seq", 1 << bit)) for bit in range(bit_count)]

    levels = [masks_of(level) for level in levels_of(bit_count)]
    order = [0]
    for masks in levels:
        order = [base ^ mask for base in order for mask in masks]
    pieces = len(order)
    chunk_ids = (place >> 1) ^ jnp.array([mask >> 1 for mask in order], jnp.int32)
    chunks = global_positions.reshape(pieces, global_count // pieces)
    match = chunk_ids[:, None] == jnp.arange(pieces, dtype=jnp.int32)[None, :]
    ordered = jnp.sum(jnp.where(match[:, :, None], chunks[None], 0), 1).reshape(global_count)
    spots = jnp.stack([ordered - place * rows, ordered - (place ^ 1) * rows])

    picked = pick(core, spots, marked, values, near[0][0], near[0][1])
    for masks in levels:
        picked = reduce_level(picked, masks)
    mine = [picked]
    for masks in reversed(levels):
        block = mine[0] if len(mine) == 1 else jnp.concatenate(mine, 0)
        mine = gather_level(block, masks)
    global_parts = mine + [swap(part, "seq", 1) for part in mine]

    positions = jnp.arange(rows, dtype=jnp.int32)
    visible = (key_keep[None, :] == 1) | (positions[:, None] == positions[None, :])
    bias = jnp.where(visible, 0.0, NEG_FILL).astype(F32)
    gain_row = gain.reshape(1, -1)

    groups = [[(keys, values), near[0]]]
    if bit_count > 2:
        groups.append(near[1:-1])
    if bit_count > 1:
        groups.append(near[-1:])
    state = None
    probs, peaks = [], []
    for number, group in enumerate(groups):
        p, *state = forward_phase(
            f"forward_slots_{number}", queries, group, bias=bias if number == 0 else None, before=state
        )
        probs.append(p)
        peaks.append(state[1])
    p_global, attn, last_peaks, inverse, sums = forward_phase(
        "forward_globals", queries, global_parts, core=core, before=state, norm=(cotangent, gain_row)
    )
    head_bits = lax.axis_size("head").bit_length() - 1
    for bit in range(head_bits):
        sums = sums + swap(sums, "head", 1 << bit)

    *global_grads, d_query, normed, grad, diag = backward_phase(
        "backward_globals", queries, p_global, global_parts, last_peaks, last_peaks, inverse,
        core=core, norm=(sums, attn, cotangent, gain_row),
    )
    half = len(global_grads) // 2
    reduced = [
        (a.astype(F32) + swap(b, "seq", 1).astype(F32)).astype(BF16)
        for a, b in zip(global_grads[:half], global_grads[half:])
    ]
    block = reduced
    for masks in levels:
        running = block[0].astype(F32) if isinstance(block, list) else None
        if isinstance(block, list):
            for part, mask in zip(block[1:], masks[1:]):
                running = running + swap(part, "seq", mask).astype(F32)
            block = running.astype(BF16)
        else:
            block = reduce_level(block, masks)
    mine = [block]
    for masks in reversed(levels):
        block = mine[0] if len(mine) == 1 else jnp.concatenate(mine, 0)
        mine = gather_level(block, masks)
    total_parts = mine + [swap(part, "seq", 1) for part in mine]

    back = []
    own_grads = None
    bits_of = [[0], list(range(1, bit_count - 1)), [bit_count - 1]]
    bits_of = [bits_of[0]] + [b for b in bits_of[1:] if b and b != [0]]
    for number in reversed(range(len(groups))):
        *slot_grads, d_query = backward_phase(
            f"backward_slots_{number}", queries, probs[number], groups[number], peaks[number],
            last_peaks, inverse, own=number == 0, grads=(grad, diag, d_query), last=number == 0,
        )
        if number == 0:
            own_grads, slot_grads = slot_grads[:2], slot_grads[2:]
        for place_in, bit in enumerate(bits_of[number]):
            back += [swap(x, "seq", 1 << bit) for x in slot_grads[2 * place_in : 2 * place_in + 2]]
    key_grad, value_grad = finish(core, spots, own_grads, back, total_parts)
    return normed, d_query, key_grad, value_grad


def solution(mesh):
    placed = (
        P("seq", "head"),
        P("seq", "head"),
        P("seq", "head"),
        P("seq"),
        P(),
        P("head"),
        P("seq", "head"),
    )
    return jax.shard_map(
        per_device,
        mesh=mesh,
        in_specs=placed,
        out_specs=(P("seq", "head"), P("seq", "head"), P("seq", "head"), P("seq", "head")),
        check_vma=False,
    )
```

time: 1070 us -> 213 us (0.20); the launches traced: 1050 us -> 213 us
  matrix products: 376 us -> 0 us
  local copies, waits for them, and re-layouts: 247 us -> 7 us
  loops' own time: 169 us -> 0 us
  Pallas kernels: 0 us -> 113 us
  waiting for transfers between devices: 131 us -> 48.4 us
  other arithmetic: 61.7 us -> 6.34 us
  blocking collectives: 36.9 us -> 0 us
  starting transfers between devices: 17.1 us -> 36.6 us
  between operations: 14.4 us -> 1.15 us
    dot_general x229 -> x0, matrix products: 376 us -> none  [the longest x96 154 us: dot_rows(): lax.dot_general(left, right, (((1,), (1,)), ((), ())), preferred_element_...]
    another operation x2 -> x0, loops' own time: 169 us -> none  [the longest x1 85.1 us: per_device(): lax.scan(backward_head, (zeros_stack, zeros_stack), (heads_order, query_s...]
    dynamic_slice x256 -> x0, local copies, waits for them, and re-layouts: 135 us -> none  [the longest x64 48.5 us: backward_head(): lax.dynamic_index_in_dim(key_accum, owner, 0, keepdims=False) + d_key]
    psum x2 -> x0, waiting for transfers between devices: 120 us -> none  [the longest x1 84.8 us: per_device(): lax.psum(key_slots[global_start:].astype(jnp.bfloat16), 'seq')]
    pallas_call x0 -> x10, Pallas kernels: none -> 113 us  [the longest x4 55.5 us: backward_phase(): pl.pallas_call(functools.partial(backward_kernel, len(pairs), own, is_glo...]
    dynamic_update_slice x160 -> x0, local copies, waits for them, and re-layouts: 64.4 us -> none  [the longest x64 52.2 us: backward_head(): lax.dynamic_update_index_in_dim(value_accum, lax.dynamic_index_in_dim(val...]
    reduce_sum x66 -> x1, other arithmetic: 52 us -> 0.09 us  [per_device(): jnp.sum(jnp.where(match[:, :, None], chunks[None], 0), 1)]
    psum x2 -> x0, blocking collectives: 36.9 us -> none  [the longest x1 31.7 us: per_device(): lax.psum(jnp.dot(selector, key_keep.astype(jnp.float32), precision=lax.Pr...]
  transfers between devices with their start and end apart: 22 -> 39, of which waited for: 6 -> 14; matrix products, arithmetic and copies ran while one was open for 3% -> 2% of each run, Pallas kernels for 0% -> 36%
where the time goes in v1:
time: 213 us
  Pallas kernels  113 us (53%)
  waiting for transfers between devices  48.4 us (23%)
  starting transfers between devices  36.6 us (17%)
  local copies, waits for them, and re-layouts  7 us (3%)
  other arithmetic  6.34 us (3%)
    pallas_call x4, Pallas kernels, backward_phase(): pl.pallas_call(functools.partial(backward_kernel, len(pairs), own, is_glo...  55.5 us
    pallas_call x4, Pallas kernels, forward_phase(): pl.pallas_call(functools.partial(forward_kernel, len(pairs), bias is not...  52.3 us
    ppermute x39, waiting for transfers between devices, swap(): return lax.ppermute(block, axis, [(i, i ^ mask) for i in range(count)])  48.4 us
    ppermute x39, starting transfers between devices, swap(): return lax.ppermute(block, axis, [(i, i ^ mask) for i in range(count)])  36.6 us
  transfers between devices with their start and end apart: 39, of which 14 were waited for; matrix products, arithmetic and copies ran while one was open for 2% of the time, Pallas kernels for 36%

profile of v1, /device:TPU:0, one launch (start us, length us, event | category | flops | bytes accessed | tf_op | source)
XLA Modules:
  0.0 212.8 jit_solution(16904692771801980907)
XLA Ops:
  0.6 0.7 broadcast_compare_fusion
  1.3 1.0 broadcast_select_fusion.k_ref
  2.4 0.5 collective-permute-start
  3.0 0.7 broadcast_xor_fusion
  3.7 0.8 broadcast_in_dim.50
  4.7 0.6 pad_add_fusion.spots_ref.refs_1_
  5.4 0.7 copy-done.14
  6.1 2.3 %pick_globals.1 = bf16[384,512]{1,0:T(8,128)(2,1)} custom-call(s32[1]{0:T(128)} %bitcast.core_ref.refs_1_.refs_2_.refs_0_, s32[2,384]{1,0:T(2,128)} %pad_add_fusion.spots_ref.refs_1_, bf16[256,512]{1,0:T(8,128)(2,1)} %copy-done, bf16[256,512]{1,0:T(8,128)(2,1)} %refs_3_.1, bf16[256,512]{1,0:T(8,128)(2,1)} %copy-done.14, bf16[256,512]{1,0:T(8,128)(2,1)} %copy-done.15), custom_call_target="tpu_custom_call" | custom-call | flops 201326592 | bytes 3145728 | tf_op jit(solution)/shard_map/pick_globals/pallas_call | solution.py:427
  8.5 0.9 slice.41
  9.4 3.0 %collective-permute-start.2 = (bf16[192,512]{1,0:T(8,128)(2,1)S(1)}, bf16[192,512]{1,0:T(8,128)(2,1)S(1)}, u32[]{:S(2)}, u32[]{:S(2)}) collective-permute-start(bf16[192,512]{1,0:T(8,128)(2,1)S(1)} %slice.41), channel_id=1, source_target_pairs={{0,4},{2,6},{4,0},{6,2},{8,12},{10,14},{12,8},{14,10},{16,20},{18,... | collective-permute-start | bytes 589832 | tf_op jit(solution)/shard_map/ppermute | solution.py:42
  12.4 5.1 %collective-permute-done.2 = bf16[192,512]{1,0:T(8,128)(2,1)S(1)} collective-permute-done((bf16[192,512]{1,0:T(8,128)(2,1)S(1)}, bf16[192,512]{1,0:T(8,128)(2,1)S(1)}, u32[]{:S(2)}, u32[]{:S(2)}) %collective-permute-start.2) | collective-permute-done | bytes 196640 | tf_op jit(solution)/shard_map/ppermute | solution.py:42
  17.6 1.0 add_convert_fusion.3
  18.6 1.9 collective-permute-start.3
  20.4 2.5 %collective-permute-start.5 = (bf16[48,512]{1,0:T(8,128)(2,1)S(1)}, bf16[48,512]{1,0:T(8,128)(2,1)S(1)}, u32[]{:S(2)}, u32[]{:S(2)}) collective-permute-start(bf16[48,512]{1,0:T(8,128)(2,1)S(1)} %get-tuple-element.88), channel_id=1, source_target_pairs={{0,24},{2,26},{4,28},{6,30},{8,16},{10,18},{12,20},{14,22},{16,8},... | collective-permute-start | bytes 147464 | tf_op jit(solution)/shard_map/ppermute | solution.py:42
  23.0 1.8 collective-permute-start.16
  24.8 1.5 collective-permute-start.14
  26.3 0.2 collective-permute-start.17
  26.6 1.8 collective-permute-done.4
  28.4 1.5 collective-permute-start.8
  29.9 0.8 collective-permute-start.7
  30.7 0.7 fusion.1.refs_5_
  31.4 1.3 reshape.66.refs_10_.refs_13_
  32.7 7.1 %collective-permute-done.8 = bf16[48,512]{1,0:T(8,128)(2,1)S(1)} collective-permute-done((bf16[48,512]{1,0:T(8,128)(2,1)S(1)}, bf16[48,512]{1,0:T(8,128)(2,1)S(1)}, u32[]{:S(2)}, u32[]{:S(2)}) %collective-permute-start.8) | collective-permute-done | bytes 49184 | tf_op jit(solution)/shard_map/ppermute | solution.py:42
  39.8 1.5 collective-permute-start.15
  41.3 9.8 %forward_slots_0.1 = (bf16[8192,512]{1,0:T(8,128)(2,1)}, f32[256,4096]{1,0:T(8,128)}, f32[256,512]{1,0:T(8,128)}, f32[256,512]{1,0:T(8,128)}) custom-call(bf16[256,4096]{1,0:T(8,128)(2,1)} %refs_0_.15, bf16[256,512]{1,0:T(8,128)(2,1)} %refs_2_.3, bf16[256,512]{1,0:T(8,128)(2,1)} %refs_3_.1, bf16[256,512]{1,0:T(8,128)(2,1)} %copy-done.14, ...), custom_call_target="tpu_custom_call" | custom-call | flops 4294967296 | bytes 8388608 | tf_op jit(solution)/shard_map/forward_slots_0/pallas_call | solution.py:223
  51.1 2.6 %collective-permute-start.12 = (bf16[256,512]{1,0:T(8,128)(2,1)S(1)}, bf16[256,512]{1,0:T(8,128)(2,1)S(1)}, u32[]{:S(2)}, u32[]{:S(2)}) collective-permute-start(bf16[256,512]{1,0:T(8,128)(2,1)S(1)} %copy-done.1), channel_id=1, source_target_pairs={{0,16},{2,18},{4,20},{6,22},{8,24},{10,26},{12,28},{14,30},{16,0},... | collective-permute-start | bytes 786440 | tf_op jit(solution)/shard_map/ppermute | solution.py:42
  53.8 0.4 collective-permute-start.13
  54.3 1.1 collective-permute-start.9
  55.4 0.7 copy-done.26
  56.2 15.9 %forward_slots_1.1 = (bf16[8192,512]{1,0:T(8,128)(2,1)}, f32[256,4096]{1,0:T(8,128)}, f32[256,512]{1,0:T(8,128)}, f32[256,512]{1,0:T(8,128)}) custom-call(bf16[256,4096]{1,0:T(8,128)(2,1)} %refs_0_.15, bf16[256,512]{1,0:T(8,128)(2,1)} %copy-done.23, bf16[256,512]{1,0:T(8,128)(2,1)} %copy-done.28, bf16[256,512]{1,0:T(8,128)(2,1)} %copy-done.22, ...), custom_call_target="tpu_custom_call" | custom-call | flops 4294967296 | bytes 8388608 | tf_op jit(solution)/shard_map/forward_slots_1/pallas_call | solution.py:223
  72.1 0.5 collective-permute-start.11
  72.6 1.6 collective-permute-done.13.refs_2_.refs_3_
  74.2 0.7 copy-done.4
  74.9 11.6 %forward_slots_2.1 = (bf16[8192,256]{1,0:T(8,128)(2,1)}, f32[256,4096]{1,0:T(8,128)}, f32[256,512]{1,0:T(8,128)}, f32[256,512]{1,0:T(8,128)}) custom-call(bf16[256,4096]{1,0:T(8,128)(2,1)} %refs_0_.15, bf16[256,512]{1,0:T(8,128)(2,1)} %copy-done.3, bf16[256,512]{1,0:T(8,128)(2,1)} %copy-done.4, f32[256,4096]{1,0:T(8,128)} %get-tuple-element.47.refs_3_, ...), custom_call_target="tpu_custom_call" | custom-call | flops 2147483648 | bytes 4194304 | tf_op jit(solution)/shard_map/forward_slots_2/pallas_call | solution.py:223
  86.6 0.6 copy-done.33
  87.3 15.0 %forward_globals.1 = (bf16[8192,384]{1,0:T(8,128)(2,1)}, f32[256,4096]{1,0:T(8,128)}, f32[256,512]{1,0:T(8,128)}, f32[256,512]{1,0:T(8,128)}, f32[2,256]{1,0:T(2,128)}) custom-call(bf16[256,4096]{1,0:T(8,128)(2,1)} %refs_0_.15, s32[1]{0:T(128)} %bitcast.core_ref.refs_1_.refs_2_.refs_0_, bf16[192,512]{1,0:T(8,128)(2,1)} %copy-done.19, ...), custom_call_target="tpu_custom_call" | custom-call | flops 3221225472 | bytes 6291456 | tf_op jit(solution)/shard_map/forward_globals/pallas_call | solution.py:223
  102.2 1.6 collective-permute-start.18
  103.8 2.3 %collective-permute-done.18 = f32[2,256]{1,0:T(2,128)S(1)} collective-permute-done((f32[2,256]{1,0:T(2,128)}, f32[2,256]{1,0:T(2,128)S(1)}, u32[]{:S(2)}, u32[]{:S(2)}) %collective-permute-start.18) | collective-permute-done | bytes 2080 | tf_op jit(solution)/shard_map/ppermute | solution.py:42
  106.1 1.2 add.37.refs_10_
  107.4 15.9 %backward_globals.1 = (bf16[192,512]{1,0:T(8,128)(2,1)}, bf16[192,512]{1,0:T(8,128)(2,1)}, bf16[192,512]{1,0:T(8,128)(2,1)}, bf16[192,512]{1,0:T(8,128)(2,1)}, f...) custom-call(bf16[256,4096]{1,0:T(8,128)(2,1)} %refs_0_.15, ...), custom_call_target="tpu_custom_call" | custom-call | flops 4831838208 | bytes 6291456 | tf_op jit(solution)/shard_map/backward_globals/pallas_call | solution.py:391
  123.3 0.5 collective-permute-start.28
  123.8 10.5 %backward_slots_2.1 = (bf16[256,512]{1,0:T(8,128)(2,1)}, bf16[256,512]{1,0:T(8,128)(2,1)}, f32[256,4096]{1,0:T(8,128)}) custom-call(bf16[256,4096]{1,0:T(8,128)(2,1)} %refs_0_.15, bf16[8192,256]{1,0:T(8,128)(2,1)} %get-tuple-element.63.refs_1_, bf16[256,512]{1,0:T(8,128)(2,1)} %copy-done.3, bf16[256,512]{1,0:T(8,128)(2,1)} %copy-done.4, ...), custom_call_target="tpu_custom_call" | custom-call | flops 3221225472 | bytes 4194304 | tf_op jit(solution)/shard_map/backward_slots_2/pallas_call | solution.py:391
  134.5 1.6 collective-permute-start.29
  136.0 14.7 %backward_slots_1.1 = (bf16[256,512]{1,0:T(8,128)(2,1)}, bf16[256,512]{1,0:T(8,128)(2,1)}, bf16[256,512]{1,0:T(8,128)(2,1)}, bf16[256,512]{1,0:T(8,128)(2,1)}, f32[256,4096]{1,0:T(8,128)}) custom-call(bf16[256,4096]{1,0:T(8,128)(2,1)} %refs_0_.15, bf16[8192,512]{1,0:T(8,128)(2,1)} %get-tuple-element.62.refs_1_, bf16[256,512]{1,0:T(8,128)(2,1)} %copy-done.23, ...), custom_call_target="tpu_custom_call" | custom-call | flops 6442450944 | bytes 8388608 | tf_op jit(solution)/shard_map/backward_slots_1/pallas_call | solution.py:391
  150.9 2.5 %collective-permute-start.32 = (bf16[48,512]{1,0:T(8,128)(2,1)S(1)}, bf16[48,512]{1,0:T(8,128)(2,1)S(1)}, u32[]{:S(2)}, u32[]{:S(2)}) collective-permute-start(bf16[48,512]{1,0:T(8,128)(2,1)S(1)} %get-tuple-element.85), channel_id=1, source_target_pairs={{0,24},{2,26},{4,28},{6,30},{8,16},{10,18},{12,20},{14,22},{16,8},... | collective-permute-start | bytes 147464 | tf_op jit(solution)/shard_map/ppermute | solution.py:42
  153.4 1.0 collective-permute-start.31
  154.4 14.4 %backward_slots_0.1 = (f32[256,512]{1,0:T(8,128)}, f32[256,512]{1,0:T(8,128)}, bf16[256,512]{1,0:T(8,128)(2,1)}, bf16[256,512]{1,0:T(8,128)(2,1)}, bf16[256,4096]{1,0:T(8,128)(2,1)}) custom-call(bf16[256,4096]{1,0:T(8,128)(2,1)} %refs_0_.15, bf16[8192,512]{1,0:T(8,128)(2,1)} %get-tuple-element.59.refs_1_, bf16[256,512]{1,0:T(8,128)(2,1)} %refs_2_.3, ...), custom_call_target="tpu_custom_call" | custom-call | flops 6442450944 | bytes 8388608 | tf_op jit(solution)/shard_map/backward_slots_0/pallas_call | solution.py:391
  169.0 2.5 %collective-permute-start.35 = (bf16[48,512]{1,0:T(8,128)(2,1)S(1)}, bf16[48,512]{1,0:T(8,128)(2,1)S(1)}, u32[]{:S(2)}, u32[]{:S(2)}) collective-permute-start(bf16[48,512]{1,0:T(8,128)(2,1)S(1)} %add_convert_fusion.4), channel_id=1, source_target_pairs={{0,24},{2,26},{4,28},{6,30},{8,16},{10,18},{12,20},{14,22},{16,8},... | collective-permute-start | bytes 147464 | tf_op jit(solution)/shard_map/ppermute | solution.py:42
  171.5 2.0 collective-permute-start.33
  173.4 1.9 collective-permute-done.35
  175.3 0.5 collective-permute-start.21
  175.8 1.2 collective-permute-done.34
  177.1 0.5 collective-permute-start.22
  177.7 1.5 collective-permute-start.36
  179.2 2.1 collective-permute-start.24
  181.3 3.2 %collective-permute-done.21.refs_6_ = bf16[256,512]{1,0:T(8,128)(2,1)S(1)} collective-permute-done((bf16[256,512]{1,0:T(8,128)(2,1)S(1)}, bf16[256,512]{1,0:T(8,128)(2,1)S(1)}, u32[]{:S(2)}, u32[]{:S(2)}) %collective-permute-start.21) | collective-permute-done | bytes 262176 | tf_op jit(solution)/shard_map/ppermute | solution.py:42
  184.5 5.6 %collective-permute-done.22.refs_7_ = bf16[256,512]{1,0:T(8,128)(2,1)S(1)} collective-permute-done((bf16[256,512]{1,0:T(8,128)(2,1)S(1)}, bf16[256,512]{1,0:T(8,128)(2,1)S(1)}, u32[]{:S(2)}, u32[]{:S(2)}) %collective-permute-start.22) | collective-permute-done | bytes 262176 | tf_op jit(solution)/shard_map/ppermute | solution.py:42
  190.2 1.9 collective-permute-done.23.refs_8_
  192.1 0.6 collective-permute-done.36.refs_13_
  192.7 4.2 %collective-permute-done.24.refs_9_ = bf16[256,512]{1,0:T(8,128)(2,1)S(1)} collective-permute-done((bf16[256,512]{1,0:T(8,128)(2,1)S(1)}, bf16[256,512]{1,0:T(8,128)(2,1)S(1)}, u32[]{:S(2)}, u32[]{:S(2)}) %collective-permute-start.24) | collective-permute-done | bytes 262176 | tf_op jit(solution)/shard_map/ppermute | solution.py:42
  196.9 7.5 %collective-permute-done.19.refs_4_ = bf16[256,512]{1,0:T(8,128)(2,1)S(1)} collective-permute-done((bf16[256,512]{1,0:T(8,128)(2,1)S(1)}, bf16[256,512]{1,0:T(8,128)(2,1)S(1)}, u32[]{:S(2)}, u32[]{:S(2)}) %collective-permute-start.19) | collective-permute-done | bytes 262176 | tf_op jit(solution)/shard_map/ppermute | solution.py:42
  204.4 4.3 %collective-permute-done.20.refs_5_ = bf16[256,512]{1,0:T(8,128)(2,1)S(1)} collective-permute-done((bf16[256,512]{1,0:T(8,128)(2,1)S(1)}, bf16[256,512]{1,0:T(8,128)(2,1)S(1)}, u32[]{:S(2)}, u32[]{:S(2)}) %collective-permute-start.20) | collective-permute-done | bytes 262176 | tf_op jit(solution)/shard_map/ppermute | solution.py:42
  208.8 0.6 copy-done.12
  209.6 3.3 %finish_key_value_grads.1 = (bf16[256,512]{1,0:T(8,128)(2,1)}, bf16[256,512]{1,0:T(8,128)(2,1)}) custom-call(s32[1]{0:T(128)} %bitcast.core_ref.refs_1_.refs_2_.refs_0_, s32[2,384]{1,0:T(2,128)} %pad_add_fusion.spots_ref.refs_1_, f32[256,512]{1,0:T(8,128)} %get-tuple-element.68.refs_2_, f32[256,512]{1,0:T(8,128)} %get-tuple-element.69.refs_3_, ...), custom_call_target="tpu_custom_call" | custom-call | flops 268435456 | bytes 4194304 | tf_op jit(solution)/shard_map/finish_key_value_grads/pallas_call | solution.py:460
  (117 shorter events, 1.8 us)
Async XLA Ops:
  2.4 3.0 %copy-start = (bf16[256,512]{1,0:T(8,128)(2,1)}, bf16[256,512]{1,0:T(8,128)(2,1)S(1)}, u32[]{:S(2)}) copy-start(bf16[256,512]{1,0:T(8,128)(2,1)S(1)} %broadcast_select_fusion.k_ref) | copy-start | bytes 786436
  2.4 3.0 %collective-permute-start = (bf16[256,512]{1,0:T(8,128)(2,1)S(1)}, bf16[256,512]{1,0:T(8,128)(2,1)S(1)}, u32[]{:S(2)}, u32[]{:S(2)}) collective-permute-start(bf16[256,512]{1,0:T(8,128)(2,1)S(1)} %broadcast_select_fusion.k_ref), channel_id=1, source_target_pairs={{0,2},{2,0},{4,6},{6,4},{8,10},{10,8},{12,14},{14,12},{16,18},{18,... | collective-permute-start | bytes 786440 | tf_op jit(solution)/shard_map/ppermute | solution.py:42
  2.9 2.5 %collective-permute-start.1 = (bf16[256,512]{1,0:T(8,128)(2,1)}, bf16[256,512]{1,0:T(8,128)(2,1)S(1)}, u32[]{:S(2)}, u32[]{:S(2)}) collective-permute-start(bf16[256,512]{1,0:T(8,128)(2,1)} %refs_3_.1), channel_id=1, source_target_pairs={{0,2},{2,0},{4,6},{6,4},{8,10},{10,8},{12,14},{14,12},{16,18},{18,... | collective-permute-start | bytes 786440 | tf_op jit(solution)/shard_map/ppermute | solution.py:42
  9.4 8.1 %collective-permute-start.2 = (bf16[192,512]{1,0:T(8,128)(2,1)S(1)}, bf16[192,512]{1,0:T(8,128)(2,1)S(1)}, u32[]{:S(2)}, u32[]{:S(2)}) collective-permute-start(bf16[192,512]{1,0:T(8,128)(2,1)S(1)} %slice.41), channel_id=1, source_target_pairs={{0,4},{2,6},{4,0},{6,2},{8,12},{10,14},{12,8},{14,10},{16,20},{18,... | collective-permute-start | bytes 589832 | tf_op jit(solution)/shard_map/ppermute | solution.py:42
  18.6 7.8 %collective-permute-start.3 = (bf16[48,512]{1,0:T(8,128)(2,1)S(1)}, bf16[48,512]{1,0:T(8,128)(2,1)S(1)}, u32[]{:S(2)}, u32[]{:S(2)}) collective-permute-start(bf16[48,512]{1,0:T(8,128)(2,1)S(1)} %get-tuple-element.87), channel_id=1, source_target_pairs={{0,8},{2,10},{4,12},{6,14},{8,0},{10,2},{12,4},{14,6},{16,24},{18,... | collective-permute-start | bytes 147464 | tf_op jit(solution)/shard_map/ppermute | solution.py:42
  20.4 6.1 %collective-permute-start.5 = (bf16[48,512]{1,0:T(8,128)(2,1)S(1)}, bf16[48,512]{1,0:T(8,128)(2,1)S(1)}, u32[]{:S(2)}, u32[]{:S(2)}) collective-permute-start(bf16[48,512]{1,0:T(8,128)(2,1)S(1)} %get-tuple-element.88), channel_id=1, source_target_pairs={{0,24},{2,26},{4,28},{6,30},{8,16},{10,18},{12,20},{14,22},{16,8},... | collective-permute-start | bytes 147464 | tf_op jit(solution)/shard_map/ppermute | solution.py:42
  22.9 5.4 %collective-permute-start.4 = (bf16[48,512]{1,0:T(8,128)(2,1)S(1)}, bf16[48,512]{1,0:T(8,128)(2,1)S(1)}, u32[]{:S(2)}, u32[]{:S(2)}) collective-permute-start(bf16[48,512]{1,0:T(8,128)(2,1)S(1)} %get-tuple-element.89), channel_id=1, source_target_pairs={{0,16},{2,18},{4,20},{6,22},{8,24},{10,26},{12,28},{14,30},{16,0},... | collective-permute-start | bytes 147464 | tf_op jit(solution)/shard_map/ppermute | solution.py:42
  23.0 30.7 %collective-permute-start.16 = (bf16[256,512]{1,0:T(8,128)(2,1)}, bf16[256,512]{1,0:T(8,128)(2,1)S(1)}, u32[]{:S(2)}, u32[]{:S(2)}) collective-permute-start(bf16[256,512]{1,0:T(8,128)(2,1)} %copy-done), channel_id=1, source_target_pairs={{0,8},{2,10},{4,12},{6,14},{8,0},{10,2},{12,4},{14,6},{16,24},{18,... | collective-permute-start | bytes 786440 | tf_op jit(solution)/shard_map/ppermute | solution.py:42
  24.8 29.4 %collective-permute-start.14 = (bf16[256,512]{1,0:T(8,128)(2,1)}, bf16[256,512]{1,0:T(8,128)(2,1)S(1)}, u32[]{:S(2)}, u32[]{:S(2)}) collective-permute-start(bf16[256,512]{1,0:T(8,128)(2,1)} %copy-done), channel_id=1, source_target_pairs={{0,4},{2,6},{4,0},{6,2},{8,12},{10,14},{12,8},{14,10},{16,20},{18,... | collective-permute-start | bytes 786440 | tf_op jit(solution)/shard_map/ppermute | solution.py:42
  26.3 29.0 %collective-permute-start.17 = (bf16[256,512]{1,0:T(8,128)(2,1)}, bf16[256,512]{1,0:T(8,128)(2,1)S(1)}, u32[]{:S(2)}, u32[]{:S(2)}) collective-permute-start(bf16[256,512]{1,0:T(8,128)(2,1)} %refs_3_.1), channel_id=1, source_target_pairs={{0,8},{2,10},{4,12},{6,14},{8,0},{10,2},{12,4},{14,6},{16,24},{18,... | collective-permute-start | bytes 786440 | tf_op jit(solution)/shard_map/ppermute | solution.py:42
  28.4 11.5 %collective-permute-start.8 = (bf16[48,512]{1,0:T(8,128)(2,1)S(1)}, bf16[48,512]{1,0:T(8,128)(2,1)S(1)}, u32[]{:S(2)}, u32[]{:S(2)}) collective-permute-start(bf16[48,512]{1,0:T(8,128)(2,1)S(1)} %add_convert_fusion.5), channel_id=1, source_target_pairs={{0,24},{2,26},{4,28},{6,30},{8,16},{10,18},{12,20},{14,22},{16,8},... | collective-permute-start | bytes 147464 | tf_op jit(solution)/shard_map/ppermute | solution.py:42
  29.9 11.4 %collective-permute-start.7 = (bf16[48,512]{1,0:T(8,128)(2,1)S(1)}, bf16[48,512]{1,0:T(8,128)(2,1)S(1)}, u32[]{:S(2)}, u32[]{:S(2)}) collective-permute-start(bf16[48,512]{1,0:T(8,128)(2,1)S(1)} %add_convert_fusion.5), channel_id=1, source_target_pairs={{0,16},{2,18},{4,20},{6,22},{8,24},{10,26},{12,28},{14,30},{16,0},... | collective-permute-start | bytes 147464 | tf_op jit(solution)/shard_map/ppermute | solution.py:42
  32.7 18.4 %copy-start.1 = (bf16[256,512]{1,0:T(8,128)(2,1)S(1)}, bf16[256,512]{1,0:T(8,128)(2,1)}, u32[]{:S(2)}) copy-start(bf16[256,512]{1,0:T(8,128)(2,1)} %copy-done) | copy-start | bytes 786436
  32.7 21.1 %copy-start.13 = (bf16[256,512]{1,0:T(8,128)(2,1)S(1)}, bf16[256,512]{1,0:T(8,128)(2,1)}, u32[]{:S(2)}) copy-start(bf16[256,512]{1,0:T(8,128)(2,1)} %refs_3_.1) | copy-start | bytes 786436
  39.8 15.5 %collective-permute-start.15 = (bf16[256,512]{1,0:T(8,128)(2,1)}, bf16[256,512]{1,0:T(8,128)(2,1)S(1)}, u32[]{:S(2)}, u32[]{:S(2)}) collective-permute-start(bf16[256,512]{1,0:T(8,128)(2,1)} %refs_3_.1), channel_id=1, source_target_pairs={{0,4},{2,6},{4,0},{6,2},{8,12},{10,14},{12,8},{14,10},{16,20},{18,... | collective-permute-start | bytes 786440 | tf_op jit(solution)/shard_map/ppermute | solution.py:42
  41.3 9.8 %collective-permute-start.6 = (bf16[48,512]{1,0:T(8,128)(2,1)S(1)}, bf16[48,512]{1,0:T(8,128)(2,1)S(1)}, u32[]{:S(2)}, u32[]{:S(2)}) collective-permute-start(bf16[48,512]{1,0:T(8,128)(2,1)S(1)} %add_convert_fusion.5), channel_id=1, source_target_pairs={{0,8},{2,10},{4,12},{6,14},{8,0},{10,2},{12,4},{14,6},{16,24},{18,... | collective-permute-start | bytes 147464 | tf_op jit(solution)/shard_map/ppermute | solution.py:42
  51.1 21.5 %collective-permute-start.12 = (bf16[256,512]{1,0:T(8,128)(2,1)S(1)}, bf16[256,512]{1,0:T(8,128)(2,1)S(1)}, u32[]{:S(2)}, u32[]{:S(2)}) collective-permute-start(bf16[256,512]{1,0:T(8,128)(2,1)S(1)} %copy-done.1), channel_id=1, source_target_pairs={{0,16},{2,18},{4,20},{6,22},{8,24},{10,26},{12,28},{14,30},{16,0},... | collective-permute-start | bytes 786440 | tf_op jit(solution)/shard_map/ppermute | solution.py:42
  53.8 18.3 %copy-start.19 = (bf16[192,512]{1,0:T(8,128)(2,1)}, bf16[192,512]{1,0:T(8,128)(2,1)S(1)}, u32[]{:S(2)}) copy-start(bf16[192,512]{1,0:T(8,128)(2,1)S(1)} %pad_maximum_fusion.refs_2_.refs_3_) | copy-start | bytes 589828
  53.8 1.6 copy-start.22
  53.8 20.4 %collective-permute-start.13 = (bf16[256,512]{1,0:T(8,128)(2,1)S(1)}, bf16[256,512]{1,0:T(8,128)(2,1)S(1)}, u32[]{:S(2)}, u32[]{:S(2)}) collective-permute-start(bf16[256,512]{1,0:T(8,128)(2,1)S(1)} %copy-done.13), channel_id=1, source_target_pairs={{0,16},{2,18},{4,20},{6,22},{8,24},{10,26},{12,28},{14,30},{16,0},... | collective-permute-start | bytes 786440 | tf_op jit(solution)/shard_map/ppermute | solution.py:42
  54.2 1.1 copy-start.23
  54.3 17.9 %collective-permute-start.9 = (bf16[192,512]{1,0:T(8,128)(2,1)S(1)}, bf16[192,512]{1,0:T(8,128)(2,1)S(1)}, u32[]{:S(2)}, u32[]{:S(2)}) collective-permute-start(bf16[192,512]{1,0:T(8,128)(2,1)S(1)} %pad_maximum_fusion.refs_2_.refs_3_), channel_id=1, source_target_pairs={{0,4},{2,6},{4,0},{6,2},{8,12},{10,14},{12,8},{14,10},{16,20},{18,... | collective-permute-start | bytes 589832 | tf_op jit(solution)/shard_map/ppermute | solution.py:42
  72.0 14.5 %collective-permute-start.10 = (bf16[192,512]{1,0:T(8,128)(2,1)S(1)}, bf16[192,512]{1,0:T(8,128)(2,1)S(1)}, u32[]{:S(2)}, u32[]{:S(2)}) collective-permute-start(bf16[192,512]{1,0:T(8,128)(2,1)S(1)} %pad_maximum_fusion.refs_2_.refs_3_), channel_id=1, source_target_pairs={{0,2},{2,0},{4,6},{6,4},{8,10},{10,8},{12,14},{14,12},{16,18},{18,... | collective-permute-start | bytes 589832 | tf_op jit(solution)/shard_map/ppermute | solution.py:42
  72.1 14.4 %copy-start.32 = (bf16[192,512]{1,0:T(8,128)(2,1)}, bf16[192,512]{1,0:T(8,128)(2,1)S(1)}, u32[]{:S(2)}) copy-start(bf16[192,512]{1,0:T(8,128)(2,1)S(1)} %collective-permute-done.9.refs_3_.refs_4_) | copy-start | bytes 589828
  72.1 14.4 %collective-permute-start.11 = (bf16[192,512]{1,0:T(8,128)(2,1)S(1)}, bf16[192,512]{1,0:T(8,128)(2,1)S(1)}, u32[]{:S(2)}, u32[]{:S(2)}) collective-permute-start(bf16[192,512]{1,0:T(8,128)(2,1)S(1)} %collective-permute-done.9.refs_3_.refs_4_), channel_id=1, source_target_pairs={{0,2},{2,0},{4,6},{6,4},{8,10},{10,8},{12,14},{14,12},{16,18},{18,... | collective-permute-start | bytes 589832 | tf_op jit(solution)/shard_map/ppermute | solution.py:42
  72.6 1.6 copy-start.3
  102.2 3.9 %collective-permute-start.18 = (f32[2,256]{1,0:T(2,128)}, f32[2,256]{1,0:T(2,128)S(1)}, u32[]{:S(2)}, u32[]{:S(2)}) collective-permute-start(f32[2,256]{1,0:T(2,128)} %get-tuple-element.56), channel_id=1, source_target_pairs={{0,1},{1,0},{2,3},{3,2},{4,5},{5,4},{6,7},{7,6},{8,9},{9,8},{10,11... | collective-permute-start | bytes 6152 | tf_op jit(solution)/shard_map/ppermute | solution.py:42
  123.3 27.4 %collective-permute-start.27 = (bf16[192,512]{1,0:T(8,128)(2,1)}, bf16[192,512]{1,0:T(8,128)(2,1)S(1)}, u32[]{:S(2)}, u32[]{:S(2)}) collective-permute-start(bf16[192,512]{1,0:T(8,128)(2,1)} %get-tuple-element.79), channel_id=1, source_target_pairs={{0,2},{2,0},{4,6},{6,4},{8,10},{10,8},{12,14},{14,12},{16,18},{18,... | collective-permute-start | bytes 589832 | tf_op jit(solution)/shard_map/ppermute | solution.py:42
  123.3 11.0 %collective-permute-start.28 = (bf16[192,512]{1,0:T(8,128)(2,1)}, bf16[192,512]{1,0:T(8,128)(2,1)S(1)}, u32[]{:S(2)}, u32[]{:S(2)}) collective-permute-start(bf16[192,512]{1,0:T(8,128)(2,1)} %get-tuple-element.81), channel_id=1, source_target_pairs={{0,2},{2,0},{4,6},{6,4},{8,10},{10,8},{12,14},{14,12},{16,18},{18,... | collective-permute-start | bytes 589832 | tf_op jit(solution)/shard_map/ppermute | solution.py:42
  123.8 10.6 %copy-start.21 = (bf16[192,512]{1,0:T(8,128)(2,1)S(1)}, bf16[192,512]{1,0:T(8,128)(2,1)}, u32[]{:S(2)}) copy-start(bf16[192,512]{1,0:T(8,128)(2,1)} %get-tuple-element.80) | copy-start | bytes 589828
  134.5 16.2 %collective-permute-start.29 = (bf16[192,512]{1,0:T(8,128)(2,1)S(1)}, bf16[192,512]{1,0:T(8,128)(2,1)S(1)}, u32[]{:S(2)}, u32[]{:S(2)}) collective-permute-start(bf16[192,512]{1,0:T(8,128)(2,1)S(1)} %add_convert_fusion.1), channel_id=1, source_target_pairs={{0,4},{2,6},{4,0},{6,2},{8,12},{10,14},{12,8},{14,10},{16,20},{18,... | collective-permute-start | bytes 589832 | tf_op jit(solution)/shard_map/ppermute | solution.py:42
  136.0 14.7 %copy-start.20 = (bf16[192,512]{1,0:T(8,128)(2,1)S(1)}, bf16[192,512]{1,0:T(8,128)(2,1)}, u32[]{:S(2)}) copy-start(bf16[192,512]{1,0:T(8,128)(2,1)} %get-tuple-element.78) | copy-start | bytes 589828
  150.8 18.1 %collective-permute-start.30 = (bf16[48,512]{1,0:T(8,128)(2,1)S(1)}, bf16[48,512]{1,0:T(8,128)(2,1)S(1)}, u32[]{:S(2)}, u32[]{:S(2)}) collective-permute-start(bf16[48,512]{1,0:T(8,128)(2,1)S(1)} %get-tuple-element.84), channel_id=1, source_target_pairs={{0,8},{2,10},{4,12},{6,14},{8,0},{10,2},{12,4},{14,6},{16,24},{18,... | collective-permute-start | bytes 147464 | tf_op jit(solution)/shard_map/ppermute | solution.py:42
  150.9 18.0 %collective-permute-start.32 = (bf16[48,512]{1,0:T(8,128)(2,1)S(1)}, bf16[48,512]{1,0:T(8,128)(2,1)S(1)}, u32[]{:S(2)}, u32[]{:S(2)}) collective-permute-start(bf16[48,512]{1,0:T(8,128)(2,1)S(1)} %get-tuple-element.85), channel_id=1, source_target_pairs={{0,24},{2,26},{4,28},{6,30},{8,16},{10,18},{12,20},{14,22},{16,8},... | collective-permute-start | bytes 147464 | tf_op jit(solution)/shard_map/ppermute | solution.py:42
  153.4 15.6 %collective-permute-start.31 = (bf16[48,512]{1,0:T(8,128)(2,1)S(1)}, bf16[48,512]{1,0:T(8,128)(2,1)S(1)}, u32[]{:S(2)}, u32[]{:S(2)}) collective-permute-start(bf16[48,512]{1,0:T(8,128)(2,1)S(1)} %get-tuple-element.86), channel_id=1, source_target_pairs={{0,16},{2,18},{4,20},{6,22},{8,24},{10,26},{12,28},{14,30},{16,0},... | collective-permute-start | bytes 147464 | tf_op jit(solution)/shard_map/ppermute | solution.py:42
  154.4 20.9 %copy-start.31 = (bf16[256,512]{1,0:T(8,128)(2,1)S(1)}, bf16[256,512]{1,0:T(8,128)(2,1)}, u32[]{:S(2)}) copy-start(bf16[256,512]{1,0:T(8,128)(2,1)} %get-tuple-element.72) | copy-start | bytes 786436
  154.4 22.7 %copy-start.30 = (bf16[256,512]{1,0:T(8,128)(2,1)S(1)}, bf16[256,512]{1,0:T(8,128)(2,1)}, u32[]{:S(2)}) copy-start(bf16[256,512]{1,0:T(8,128)(2,1)} %get-tuple-element.73) | copy-start | bytes 786436
  154.4 23.2 %copy-start.29 = (bf16[256,512]{1,0:T(8,128)(2,1)S(1)}, bf16[256,512]{1,0:T(8,128)(2,1)}, u32[]{:S(2)}) copy-start(bf16[256,512]{1,0:T(8,128)(2,1)} %get-tuple-element.74) | copy-start | bytes 786436
  154.4 24.9 %copy-start.27 = (bf16[256,512]{1,0:T(8,128)(2,1)S(1)}, bf16[256,512]{1,0:T(8,128)(2,1)}, u32[]{:S(2)}) copy-start(bf16[256,512]{1,0:T(8,128)(2,1)} %get-tuple-element.75) | copy-start | bytes 786436
  154.4 30.2 %copy-start.25 = (bf16[256,512]{1,0:T(8,128)(2,1)S(1)}, bf16[256,512]{1,0:T(8,128)(2,1)}, u32[]{:S(2)}) copy-start(bf16[256,512]{1,0:T(8,128)(2,1)} %get-tuple-element.70) | copy-start | bytes 786436
  154.4 35.8 %copy-start.24 = (bf16[256,512]{1,0:T(8,128)(2,1)S(1)}, bf16[256,512]{1,0:T(8,128)(2,1)}, u32[]{:S(2)}) copy-start(bf16[256,512]{1,0:T(8,128)(2,1)} %get-tuple-element.71) | copy-start | bytes 786436
  168.8 8.9 %collective-permute-start.25 = (bf16[256,512]{1,0:T(8,128)(2,1)}, bf16[256,512]{1,0:T(8,128)(2,1)S(1)}, u32[]{:S(2)}, u32[]{:S(2)}) collective-permute-start(bf16[256,512]{1,0:T(8,128)(2,1)} %get-tuple-element.76), channel_id=1, source_target_pairs={{0,2},{2,0},{4,6},{6,4},{8,10},{10,8},{12,14},{14,12},{16,18},{18,... | collective-permute-start | bytes 786440 | tf_op jit(solution)/shard_map/ppermute | solution.py:42
  169.0 6.3 %collective-permute-start.35 = (bf16[48,512]{1,0:T(8,128)(2,1)S(1)}, bf16[48,512]{1,0:T(8,128)(2,1)S(1)}, u32[]{:S(2)}, u32[]{:S(2)}) collective-permute-start(bf16[48,512]{1,0:T(8,128)(2,1)S(1)} %add_convert_fusion.4), channel_id=1, source_target_pairs={{0,24},{2,26},{4,28},{6,30},{8,16},{10,18},{12,20},{14,22},{16,8},... | collective-permute-start | bytes 147464 | tf_op jit(solution)/shard_map/ppermute | solution.py:42
  171.4 5.6 %collective-permute-start.34 = (bf16[48,512]{1,0:T(8,128)(2,1)S(1)}, bf16[48,512]{1,0:T(8,128)(2,1)S(1)}, u32[]{:S(2)}, u32[]{:S(2)}) collective-permute-start(bf16[48,512]{1,0:T(8,128)(2,1)S(1)} %add_convert_fusion.4), channel_id=1, source_target_pairs={{0,16},{2,18},{4,20},{6,22},{8,24},{10,26},{12,28},{14,30},{16,0},... | collective-permute-start | bytes 147464 | tf_op jit(solution)/shard_map/ppermute | solution.py:42
  171.5 6.1 %collective-permute-start.33 = (bf16[48,512]{1,0:T(8,128)(2,1)S(1)}, bf16[48,512]{1,0:T(8,128)(2,1)S(1)}, u32[]{:S(2)}, u32[]{:S(2)}) collective-permute-start(bf16[48,512]{1,0:T(8,128)(2,1)S(1)} %add_convert_fusion.4), channel_id=1, source_target_pairs={{0,8},{2,10},{4,12},{6,14},{8,0},{10,2},{12,4},{14,6},{16,24},{18,... | collective-permute-start | bytes 147464 | tf_op jit(solution)/shard_map/ppermute | solution.py:42
  173.4 5.8 %collective-permute-start.26 = (bf16[256,512]{1,0:T(8,128)(2,1)}, bf16[256,512]{1,0:T(8,128)(2,1)S(1)}, u32[]{:S(2)}, u32[]{:S(2)}) collective-permute-start(bf16[256,512]{1,0:T(8,128)(2,1)} %get-tuple-element.77), channel_id=1, source_target_pairs={{0,2},{2,0},{4,6},{6,4},{8,10},{10,8},{12,14},{14,12},{16,18},{18,... | collective-permute-start | bytes 786440 | tf_op jit(solution)/shard_map/ppermute | solution.py:42
  175.3 9.2 %collective-permute-start.21 = (bf16[256,512]{1,0:T(8,128)(2,1)S(1)}, bf16[256,512]{1,0:T(8,128)(2,1)S(1)}, u32[]{:S(2)}, u32[]{:S(2)}) collective-permute-start(bf16[256,512]{1,0:T(8,128)(2,1)S(1)} %copy-done.31), channel_id=1, source_target_pairs={{0,4},{2,6},{4,0},{6,2},{8,12},{10,14},{12,8},{14,10},{16,20},{18,... | collective-permute-start | bytes 786440 | tf_op jit(solution)/shard_map/ppermute | solution.py:42
  177.1 13.1 %collective-permute-start.22 = (bf16[256,512]{1,0:T(8,128)(2,1)S(1)}, bf16[256,512]{1,0:T(8,128)(2,1)S(1)}, u32[]{:S(2)}, u32[]{:S(2)}) collective-permute-start(bf16[256,512]{1,0:T(8,128)(2,1)S(1)} %copy-done.30), channel_id=1, source_target_pairs={{0,4},{2,6},{4,0},{6,2},{8,12},{10,14},{12,8},{14,10},{16,20},{18,... | collective-permute-start | bytes 786440 | tf_op jit(solution)/shard_map/ppermute | solution.py:42
  177.6 14.5 %collective-permute-start.23 = (bf16[256,512]{1,0:T(8,128)(2,1)S(1)}, bf16[256,512]{1,0:T(8,128)(2,1)S(1)}, u32[]{:S(2)}, u32[]{:S(2)}) collective-permute-start(bf16[256,512]{1,0:T(8,128)(2,1)S(1)} %copy-done.29), channel_id=1, source_target_pairs={{0,8},{2,10},{4,12},{6,14},{8,0},{10,2},{12,4},{14,6},{16,24},{18,... | collective-permute-start | bytes 786440 | tf_op jit(solution)/shard_map/ppermute | solution.py:42
  177.7 31.0 %copy-start.2 = (bf16[192,512]{1,0:T(8,128)(2,1)}, bf16[192,512]{1,0:T(8,128)(2,1)S(1)}, u32[]{:S(2)}) copy-start(bf16[192,512]{1,0:T(8,128)(2,1)S(1)} %pad_maximum_fusion.1.refs_12_) | copy-start | bytes 589828
  177.7 31.0 %copy-start.5 = (bf16[256,512]{1,0:T(8,128)(2,1)}, bf16[256,512]{1,0:T(8,128)(2,1)S(1)}, u32[]{:S(2)}) copy-start(bf16[256,512]{1,0:T(8,128)(2,1)S(1)} %collective-permute-done.25.refs_10_) | copy-start | bytes 786436
  177.7 15.0 %collective-permute-start.36 = (bf16[192,512]{1,0:T(8,128)(2,1)S(1)}, bf16[192,512]{1,0:T(8,128)(2,1)S(1)}, u32[]{:S(2)}, u32[]{:S(2)}) collective-permute-start(bf16[192,512]{1,0:T(8,128)(2,1)S(1)} %pad_maximum_fusion.1.refs_12_), channel_id=1, source_target_pairs={{0,4},{2,6},{4,0},{6,2},{8,12},{10,14},{12,8},{14,10},{16,20},{18,... | collective-permute-start | bytes 589832 | tf_op jit(solution)/shard_map/ppermute | solution.py:42
  179.2 29.5 %copy-start.6 = (bf16[256,512]{1,0:T(8,128)(2,1)}, bf16[256,512]{1,0:T(8,128)(2,1)S(1)}, u32[]{:S(2)}) copy-start(bf16[256,512]{1,0:T(8,128)(2,1)S(1)} %collective-permute-done.26.refs_11_) | copy-start | bytes 786436
  179.2 17.7 %collective-permute-start.24 = (bf16[256,512]{1,0:T(8,128)(2,1)S(1)}, bf16[256,512]{1,0:T(8,128)(2,1)S(1)}, u32[]{:S(2)}, u32[]{:S(2)}) collective-permute-start(bf16[256,512]{1,0:T(8,128)(2,1)S(1)} %copy-done.27), channel_id=1, source_target_pairs={{0,8},{2,10},{4,12},{6,14},{8,0},{10,2},{12,4},{14,6},{16,24},{18,... | collective-permute-start | bytes 786440 | tf_op jit(solution)/shard_map/ppermute | solution.py:42
  184.5 24.2 %copy-start.7 = (bf16[256,512]{1,0:T(8,128)(2,1)}, bf16[256,512]{1,0:T(8,128)(2,1)S(1)}, u32[]{:S(2)}) copy-start(bf16[256,512]{1,0:T(8,128)(2,1)S(1)} %collective-permute-done.21.refs_6_) | copy-start | bytes 786436
  184.5 19.9 %collective-permute-start.19 = (bf16[256,512]{1,0:T(8,128)(2,1)S(1)}, bf16[256,512]{1,0:T(8,128)(2,1)S(1)}, u32[]{:S(2)}, u32[]{:S(2)}) collective-permute-start(bf16[256,512]{1,0:T(8,128)(2,1)S(1)} %copy-done.25), channel_id=1, source_target_pairs={{0,16},{2,18},{4,20},{6,22},{8,24},{10,26},{12,28},{14,30},{16,0},... | collective-permute-start | bytes 786440 | tf_op jit(solution)/shard_map/ppermute | solution.py:42
  190.1 18.6 %copy-start.8 = (bf16[256,512]{1,0:T(8,128)(2,1)}, bf16[256,512]{1,0:T(8,128)(2,1)S(1)}, u32[]{:S(2)}) copy-start(bf16[256,512]{1,0:T(8,128)(2,1)S(1)} %collective-permute-done.22.refs_7_) | copy-start | bytes 786436
  190.1 18.6 %collective-permute-start.20 = (bf16[256,512]{1,0:T(8,128)(2,1)S(1)}, bf16[256,512]{1,0:T(8,128)(2,1)S(1)}, u32[]{:S(2)}, u32[]{:S(2)}) collective-permute-start(bf16[256,512]{1,0:T(8,128)(2,1)S(1)} %copy-done.24), channel_id=1, source_target_pairs={{0,16},{2,18},{4,20},{6,22},{8,24},{10,26},{12,28},{14,30},{16,0},... | collective-permute-start | bytes 786440 | tf_op jit(solution)/shard_map/ppermute | solution.py:42
  192.1 16.7 %copy-start.9 = (bf16[256,512]{1,0:T(8,128)(2,1)}, bf16[256,512]{1,0:T(8,128)(2,1)S(1)}, u32[]{:S(2)}) copy-start(bf16[256,512]{1,0:T(8,128)(2,1)S(1)} %collective-permute-done.23.refs_8_) | copy-start | bytes 786436
  192.1 16.6 %collective-permute-start.37 = (bf16[192,512]{1,0:T(8,128)(2,1)S(1)}, bf16[192,512]{1,0:T(8,128)(2,1)S(1)}, u32[]{:S(2)}, u32[]{:S(2)}) collective-permute-start(bf16[192,512]{1,0:T(8,128)(2,1)S(1)} %pad_maximum_fusion.1.refs_12_), channel_id=1, source_target_pairs={{0,2},{2,0},{4,6},{6,4},{8,10},{10,8},{12,14},{14,12},{16,18},{18,... | collective-permute-start | bytes 589832 | tf_op jit(solution)/shard_map/ppermute | solution.py:42
  192.7 16.1 %copy-start.16 = (bf16[192,512]{1,0:T(8,128)(2,1)}, bf16[192,512]{1,0:T(8,128)(2,1)S(1)}, u32[]{:S(2)}) copy-start(bf16[192,512]{1,0:T(8,128)(2,1)S(1)} %collective-permute-done.36.refs_13_) | copy-start | bytes 589828
  192.7 16.0 %collective-permute-start.38 = (bf16[192,512]{1,0:T(8,128)(2,1)S(1)}, bf16[192,512]{1,0:T(8,128)(2,1)S(1)}, u32[]{:S(2)}, u32[]{:S(2)}) collective-permute-start(bf16[192,512]{1,0:T(8,128)(2,1)S(1)} %collective-permute-done.36.refs_13_), channel_id=1, source_target_pairs={{0,2},{2,0},{4,6},{6,4},{8,10},{10,8},{12,14},{14,12},{16,18},{18,... | collective-permute-start | bytes 589832 | tf_op jit(solution)/shard_map/ppermute | solution.py:42
  196.9 11.9 %copy-start.10 = (bf16[256,512]{1,0:T(8,128)(2,1)}, bf16[256,512]{1,0:T(8,128)(2,1)S(1)}, u32[]{:S(2)}) copy-start(bf16[256,512]{1,0:T(8,128)(2,1)S(1)} %collective-permute-done.24.refs_9_) | copy-start | bytes 786436
  204.4 4.4 %copy-start.11 = (bf16[256,512]{1,0:T(8,128)(2,1)}, bf16[256,512]{1,0:T(8,128)(2,1)S(1)}, u32[]{:S(2)}) copy-start(bf16[256,512]{1,0:T(8,128)(2,1)S(1)} %collective-permute-done.19.refs_4_) | copy-start | bytes 786436
  (10 other events, 7.5 us)

commit v2 on v1

v2 whole, which is shorter than its diff:
```python
import functools
import math

import jax
import jax.numpy as jnp
from jax import lax
from jax.experimental import pallas as pl
from jax.experimental.pallas import tpu as pltpu
from jax.sharding import PartitionSpec as P

QH = 64
KVH = 8
HD = 128
GROUP = QH // KVH

NEG_FILL = -1e30
NORM_EPS = 1e-06
HIDDEN = 256.0
HIDDEN_ABOVE = 100.0
SCALING = HD ** (-0.5)
EXPONENT = SCALING * math.log2(math.e)
VMEM_BYTES = 56 * 2**20
TOTAL_LEAST = 2.0**-80
TOTAL_MOST = 2.0**100

F32 = jnp.float32
BF16 = jnp.bfloat16


def dot_nt(left, right):
    return lax.dot_general(left, right, (((1,), (1,)), ((), ())), preferred_element_type=F32)


def dot_nn(left, right):
    return lax.dot_general(left, right, (((1,), (0,)), ((), ())), preferred_element_type=F32)


def dot_tn(left, right):
    return lax.dot_general(left, right, (((0,), (0,)), ((), ())), preferred_element_type=F32)


def swap(block, axis, mask):
    count = lax.axis_size(axis)
    return lax.ppermute(block, axis, [(i, i ^ mask) for i in range(count)])


def params():
    return pltpu.CompilerParams(vmem_limit_bytes=VMEM_BYTES)


def cost(flops, moved, expos=0):
    return pl.CostEstimate(flops=int(flops), bytes_accessed=int(moved), transcendentals=int(expos))


def lane_of(shape):
    return lax.broadcasted_iota(jnp.int32, shape, 1)


def column_block(rows, width, row=0):
    return pl.BlockSpec((rows, width), lambda a: (row, a))


def fixed_block(shape):
    return pl.BlockSpec(shape, lambda a: (0,) * len(shape))


SCALAR = pl.BlockSpec(memory_space=pltpu.SMEM)
WHOLE = pl.BlockSpec(memory_space=pltpu.VMEM)


def read_global(refs, core_ref):
    count = len(refs) // 2
    mine = jnp.concatenate([r[...] for r in refs[:count]], 0)
    other = jnp.concatenate([r[...] for r in refs[count:]], 0)
    first = core_ref[0] == 0
    return jnp.where(first, mine, other), jnp.where(first, other, mine)


def read_slots(take, near, parts):
    keys, values = [], []
    for _ in range(near):
        keys.append(take(0)[...])
        values.append(take(0)[...])
    core_ref = None
    if parts:
        core_ref = take(0)
        refs = [take(0) for _ in range(parts)]
        k, v = read_global(refs, core_ref)
        keys.append(k)
        values.append(v)
    return keys, values, core_ref


def slot_operands(near, parts, core):
    args, specs = [], []
    for k, v, row in near:
        rows = k.shape[0] if row == 0 else k.shape[0] // 2
        args += [k, v]
        specs += [column_block(rows, HD), column_block(rows, HD, row)]
    if parts:
        args += [core] + list(parts)
        specs += [SCALAR] + [column_block(x.shape[0], HD) for x in parts]
    slots = sum(k.shape[0] if row == 0 else k.shape[0] // 2 for k, _, row in near)
    return args, specs, slots + sum(x.shape[0] for x in parts) // 2


def prepare_kernel(keep_ref, k_ref, v_ref, out_ref):
    rows, width = k_ref.shape
    keep = jnp.broadcast_to(keep_ref[...].astype(F32), (HD, rows)).T
    for start in range(0, width, HD):
        here = slice(start, start + HD)
        k = jnp.where(keep == 1.0, k_ref[:, here].astype(F32), HIDDEN)
        out_ref[:rows, here] = k.astype(BF16)
    out_ref[rows:, :] = v_ref[...]


def prepare(keep_row, keys, values):
    rows, width = keys.shape
    return pl.pallas_call(
        prepare_kernel,
        in_specs=[WHOLE] * 3,
        out_specs=WHOLE,
        out_shape=jax.ShapeDtypeStruct((2 * rows, width), BF16),
        compiler_params=params(),
        cost_estimate=cost(2**20, 4 * rows * width * 2),
        name="prepare_keys_values",
    )(keep_row, keys, values)


def forward_kernel(near, parts, own, first, last, *refs):
    refs = list(refs)
    take = refs.pop
    q_ref = take(0)
    key_list, value_list, _ = read_slots(take, near, parts)
    keep_ref = take(0) if own else None
    if not first:
        sum_ref, peak_ref, total_ref = take(0), take(0), take(0)
    if last:
        cot_ref, gain_ref = take(0), take(0)
    p_ref, out_ref, peak_out, total_out = take(0), take(0), take(0), take(0)
    if last:
        rows_ref, square_acc, cross_acc = take(0), take(0), take(0)
        step = pl.program_id(0)

    rows = q_ref.shape[0]
    lanes = lane_of((rows, HD))
    unit = (lanes == 0).astype(BF16)
    wide_keys, wide_values = [], []
    for number, (k, v) in enumerate(zip(key_list, value_list)):
        if own and number == 0:
            extra = jnp.zeros_like(k)
        else:
            hidden = (lane_of(k.shape) == 0) & (k.astype(F32) > HIDDEN_ABOVE)
            extra = jnp.where(hidden, NEG_FILL, 0.0).astype(BF16)
        wide_keys.append(jnp.concatenate([k, extra], 1))
        wide_values.append(jnp.concatenate([v, jnp.ones_like(v)], 1))
    if own:
        square = (rows, rows)
        itself = lax.broadcasted_iota(jnp.int32, square, 0) == lane_of(square)
        visible = itself | (jnp.broadcast_to(keep_ref[...], square) == 1)

    def scores_of(head, number):
        q = jnp.concatenate([q_ref[:, head * HD : (head + 1) * HD], unit], 1)
        return dot_nt(q, wide_keys[number])

    def keep_exponentials(head, number, value):
        start = sum(k.shape[0] for k in wide_keys[:number])
        stop = start + wide_keys[number].shape[0]
        p_ref[head * rows : (head + 1) * rows, start:stop] = value
        return dot_nn(value, wide_values[number])

    totals = jnp.ones((rows, HD), F32)
    order = [(head, number) for head in range(GROUP) for number in range(len(wide_keys))]
    ahead = scores_of(*order[0])
    mixed = None
    for place, (head, number) in enumerate(order):
        scores = ahead
        if place + 1 < len(order):
            ahead = scores_of(*order[place + 1])
        expo = jnp.exp2(scores * EXPONENT)
        if own and number == 0:
            expo = jnp.where(visible, expo, 0.0)
        part = keep_exponentials(head, number, expo.astype(BF16))
        mixed = part if number == 0 else mixed + part
        if number + 1 == len(wide_keys):
            here = slice(head * HD, (head + 1) * HD)
            value_sum, total = mixed[:, :HD], mixed[:, HD:]
            if not first:
                value_sum = value_sum + sum_ref[:, here]
                total = total + total_ref[:, head : head + 1]
            if last:
                total = 1.0 / total
                value_sum = value_sum * total
            out_ref[:, here] = value_sum
            totals = jnp.where(lanes == head, total, totals)
    total_out[...] = totals
    peak_out[...] = jnp.zeros((rows, HD), F32)
    if last:
        good = (totals >= 1.0 / TOTAL_MOST) & (totals <= 1.0 / TOTAL_LEAST)
    else:
        good = (totals >= TOTAL_LEAST) & (totals <= TOTAL_MOST)
    if not first:
        good = good & (peak_ref[...] == 0.0)
    in_range = jnp.min(jnp.where(good, 1.0, 0.0)) > 0.5

    @pl.when(jnp.logical_not(in_range))
    def _():
        peaks = jnp.zeros((rows, HD), F32)
        safe_totals = jnp.ones((rows, HD), F32)
        for head in range(GROUP):
            scores = [scores_of(head, number) for number in range(len(wide_keys))]
            if own:
                scores[0] = jnp.where(visible, scores[0], NEG_FILL)
            peak = functools.reduce(jnp.maximum, [jnp.max(s, -1, keepdims=True) for s in scores])
            if not first:
                before = peak_ref[:, head : head + 1]
                peak = jnp.maximum(peak, before)
            mix = None
            for number, s in enumerate(scores):
                e = jnp.exp2((s - peak) * EXPONENT).astype(BF16)
                part = keep_exponentials(head, number, e)
                mix = part if mix is None else mix + part
            here = slice(head * HD, (head + 1) * HD)
            value_sum, total = mix[:, :HD], mix[:, HD:]
            if not first:
                shrink = jnp.exp2((before - peak) * EXPONENT)
                value_sum = value_sum + sum_ref[:, here] * shrink
                total = total + total_ref[:, head : head + 1] * shrink
            if last:
                total = 1.0 / total
                value_sum = value_sum * total
            out_ref[:, here] = value_sum
            safe_totals = jnp.where(lanes == head, total, safe_totals)
            peaks = jnp.where(lanes == head, peak, peaks)
        peak_out[...] = peaks
        total_out[...] = safe_totals

    if last:

        @pl.when(step == 0)
        def _():
            square_acc[...] = jnp.zeros_like(square_acc)
            cross_acc[...] = jnp.zeros_like(cross_acc)

        squares, crosses = square_acc[...], cross_acc[...]
        for head in range(GROUP):
            here = slice(head * HD, (head + 1) * HD)
            attn = out_ref[:, here]
            upstream = cot_ref[:, here].astype(F32) * gain_ref[:, here].astype(F32)
            squares = squares + attn * attn
            crosses = crosses + upstream * attn
        square_acc[...] = squares
        cross_acc[...] = crosses

        @pl.when(step == pl.num_programs(0) - 1)
        def _():
            square_row = jnp.sum(square_acc[...].T, 0, keepdims=True)
            cross_row = jnp.sum(cross_acc[...].T, 0, keepdims=True)
            rows_ref[...] = jnp.concatenate([square_row, cross_row], 0)


def forward_phase(name, queries, near, parts=(), core=None, keep_row=None, before=None, norm=None):
    rows, width = queries.shape
    steps = width // (GROUP * HD)
    wide = GROUP * HD
    args, specs, slots = slot_operands(near, parts, core)
    args.insert(0, queries)
    specs.insert(0, column_block(rows, wide))
    if keep_row is not None:
        args.append(keep_row)
        specs.append(fixed_block(keep_row.shape))
    if before is not None:
        args += list(before)
        specs += [column_block(rows, wide), column_block(rows, HD), column_block(rows, HD)]
    if norm is not None:
        args += list(norm)
        specs += [column_block(rows, wide), column_block(1, wide)]
    out_shapes = [
        jax.ShapeDtypeStruct((steps * GROUP * rows, slots), BF16),
        jax.ShapeDtypeStruct((rows, width), F32),
        jax.ShapeDtypeStruct((rows, steps * HD), F32),
        jax.ShapeDtypeStruct((rows, steps * HD), F32),
    ]
    out_specs = [
        pl.BlockSpec((GROUP * rows, slots), lambda a: (a, 0)),
        column_block(rows, wide),
        column_block(rows, HD),
        column_block(rows, HD),
    ]
    scratch = []
    if norm is not None:
        out_shapes.append(jax.ShapeDtypeStruct((2, rows), F32))
        out_specs.append(fixed_block((2, rows)))
        scratch = [pltpu.VMEM((rows, HD), F32), pltpu.VMEM((rows, HD), F32)]
    elements = rows * slots * steps * GROUP
    return pl.pallas_call(
        functools.partial(
            forward_kernel, len(near), len(parts), keep_row is not None, before is None, norm is not None
        ),
        grid=(steps,),
        in_specs=specs,
        out_specs=out_specs,
        out_shape=out_shapes,
        scratch_shapes=scratch,
        compiler_params=params(),
        cost_estimate=cost(8 * elements * HD, 2 * elements, elements),
        name=name,
    )(*args)


def backward_kernel(near, parts, own, later, last, features, *refs):
    refs = list(refs)
    take = refs.pop
    first = later is not None
    q_ref, p_ref = take(0), take(0)
    key_list, value_list, core_ref = read_slots(take, near, parts)
    if first:
        peak_refs = [take(0) for _ in range(later + 1)]
        inverse_ref, norm_ref, attn_ref, cot_ref, gain_ref = [take(0) for _ in range(5)]
    else:
        grad_ref, diag_ref, dq_ref = take(0), take(0), take(0)
    outs = [take(0) for _ in range(near + parts)]
    dq_out = take(0)
    if first:
        normed_out = take(0)
        later_outs = [(take(0), take(0)) for _ in range(later)]
    ds_ref, q_stack, grad_stack = take(0), take(0), take(0)

    rows = q_ref.shape[0]
    lanes = lane_of((rows, HD))
    if first:
        inverse_total = inverse_ref[...]
        factors = [inverse_total] + [
            jnp.exp2((r[...] - peak_refs[0][...]) * EXPONENT) * inverse_total for r in peak_refs[1:]
        ]
        squares = norm_ref[0:1, :]
        crossed = norm_ref[1:2, :]
        inverse_row = lax.rsqrt(squares / features + NORM_EPS)
        coefficient_row = inverse_row * inverse_row * inverse_row * crossed / features
        inverse_wide = jnp.broadcast_to(inverse_row, (HD, rows)).T
        coefficient_wide = jnp.broadcast_to(coefficient_row, (HD, rows)).T
        diags = [jnp.zeros((rows, HD), F32)] * later

    gradients, diagonals = [], []
    for head in range(GROUP):
        here = slice(head * HD, (head + 1) * HD)
        stack = slice(head * rows, (head + 1) * rows)
        if first:
            attn = attn_ref[:, here]
            gain = gain_ref[:, here].astype(F32)
            normed_out[:, here] = (attn * inverse_wide * gain).astype(BF16)
            upstream = cot_ref[:, here].astype(F32) * gain
            grad = inverse_wide * upstream - attn * coefficient_wide
            diag = jnp.sum(grad * attn, -1, keepdims=True)
            factor = factors[0][:, head : head + 1]
            grad_bf = (grad * factor).astype(BF16)
            scaled_diag = diag * factor
            for number, (grad_out, _) in enumerate(later_outs):
                factor = factors[number + 1][:, head : head + 1]
                grad_out[:, here] = (grad * factor).astype(BF16)
                diags[number] = jnp.where(lanes == head, diag * factor, diags[number])
        else:
            grad_bf = grad_ref[:, here]
            scaled_diag = diag_ref[:, head : head + 1]
        grad_stack[stack, :] = grad_bf
        q_stack[stack, :] = q_ref[:, here]
        start = 0
        d_query = None
        for k, v in zip(key_list, value_list):
            columns = slice(start, start + k.shape[0])
            d_probs = dot_nt(grad_bf, v)
            d_scores = (p_ref[stack, columns].astype(F32) * (d_probs - scaled_diag)).astype(BF16)
            ds_ref[stack, columns] = d_scores
            part = dot_nn(d_scores, k)
            d_query = part if d_query is None else d_query + part
            start += k.shape[0]
        if not first:
            d_query = d_query + dq_ref[:, here]
        if last:
            d_query = d_query * SCALING
        dq_out[:, here] = d_query.astype(dq_out.dtype)
    if first:
        for (_, diag_out), diag in zip(later_outs, diags):
            diag_out[...] = diag
    q_all, grad_all = q_stack[...], grad_stack[...]
    start = 0
    for number, k in enumerate(key_list):
        size = k.shape[0]
        columns = slice(start, start + size)
        start += size
        d_key = (dot_tn(q_all, ds_ref[:, columns]) * SCALING).T
        d_value = dot_tn(grad_all, p_ref[:, columns]).T
        if number < near:
            out = outs[number]
            out[:size, :] = d_key.astype(out.dtype)
            out[size:, :] = d_value.astype(out.dtype)
        else:
            d_key, d_value = d_key.astype(BF16), d_value.astype(BF16)
            core_first = core_ref[0] == 0
            mine = jnp.where(core_first, d_key, d_value)
            other = jnp.where(core_first, d_value, d_key)
            begin = 0
            for part in range(parts // 2):
                mine_out, other_out = outs[near + part], outs[near + parts // 2 + part]
                length = mine_out.shape[0]
                mine_out[...] = mine[begin : begin + length]
                other_out[...] = other[begin : begin + length]
                begin += length


def backward_phase(
    name, queries, probs, near, parts=(), core=None, own=False, peaks=None, norm=None,
    grads=None, last=False,
):
    rows, width = queries.shape
    steps = width // (GROUP * HD)
    wide = GROUP * HD
    slots = probs.shape[1]
    args, specs, _ = slot_operands(near, parts, core)
    args = [queries, probs] + args
    specs = [column_block(rows, wide), pl.BlockSpec((GROUP * rows, slots), lambda a: (a, 0))] + specs
    out_shapes, out_specs = [], []
    for number, (k, _, row) in enumerate(near):
        size = k.shape[0] if row == 0 else k.shape[0] // 2
        kind = F32 if own and number == 0 else BF16
        out_shapes.append(jax.ShapeDtypeStruct((2 * size, k.shape[1]), kind))
        out_specs.append(column_block(2 * size, HD))
    for x in parts:
        out_shapes.append(jax.ShapeDtypeStruct(x.shape, BF16))
        out_specs.append(column_block(x.shape[0], HD))
    later = None
    if norm is not None:
        later = len(peaks) - 1
        inverse, sums, attn, cotangent, gain = norm
        args += list(peaks) + [inverse, sums, attn, cotangent, gain]
        specs += [column_block(rows, HD)] * (len(peaks) + 1) + [
            fixed_block(sums.shape),
            column_block(rows, wide),
            column_block(rows, wide),
            column_block(1, wide),
        ]
    else:
        args += list(grads)
        specs += [column_block(rows, wide), column_block(rows, HD), column_block(rows, wide)]
    out_shapes.append(jax.ShapeDtypeStruct((rows, width), BF16 if last else F32))
    out_specs.append(column_block(rows, wide))
    if norm is not None:
        out_shapes.append(jax.ShapeDtypeStruct((rows, width), BF16))
        out_specs.append(column_block(rows, wide))
        for _ in range(later):
            out_shapes += [
                jax.ShapeDtypeStruct((rows, width), BF16),
                jax.ShapeDtypeStruct((rows, steps * HD), F32),
            ]
            out_specs += [column_block(rows, wide), column_block(rows, HD)]
    elements = rows * slots * steps * GROUP
    return pl.pallas_call(
        functools.partial(backward_kernel, len(near), len(parts), own, later, last, QH * HD),
        grid=(steps,),
        in_specs=specs,
        out_specs=out_specs,
        out_shape=out_shapes,
        scratch_shapes=[
            pltpu.VMEM((GROUP * rows, slots), BF16),
            pltpu.VMEM((GROUP * rows, HD), BF16),
            pltpu.VMEM((GROUP * rows, HD), BF16),
        ],
        compiler_params=params(),
        cost_estimate=cost(12 * elements * HD, 2 * elements),
        name=name,
    )(*args)


def pick_kernel(core_ref, spots_ref, own_ref, partner_ref, out_ref):
    rows = own_ref.shape[0] // 2
    count = spots_ref.shape[1]
    first = core_ref[0] == 0
    row_ids = lax.broadcasted_iota(jnp.int32, (rows, count), 0)
    total = None
    for number, ref in enumerate((own_ref, partner_ref)):
        source = jnp.where(first, ref[:rows, :], ref[rows:, :])
        chosen = jnp.where(row_ids == spots_ref[number : number + 1, :], 1.0, 0.0).astype(BF16)
        part = dot_tn(chosen, source)
        total = part if total is None else total + part
    out_ref[...] = total.astype(BF16)


def pick(core, spots, own, partner):
    shape = (spots.shape[1], own.shape[1])
    return pl.pallas_call(
        pick_kernel,
        in_specs=[SCALAR] + [WHOLE] * 3,
        out_specs=WHOLE,
        out_shape=jax.ShapeDtypeStruct(shape, BF16),
        compiler_params=params(),
        cost_estimate=cost(2 * shape[0] * shape[1] * own.shape[0], 3 * 2**20),
        name="pick_globals",
    )(core, spots, own, partner)


def finish_kernel(partners, parts, *refs):
    core_ref, spots_ref, own = refs[:3]
    back = refs[3 : 3 + partners]
    total = refs[3 + partners : 3 + partners + parts]
    outs = refs[3 + partners + parts :]
    rows = own.shape[0] // 2
    count = spots_ref.shape[1]
    row_ids = lax.broadcasted_iota(jnp.int32, (rows, count), 0)
    chosen = jnp.where(row_ids == spots_ref[0:1, :], 1.0, 0.0).astype(BF16)
    global_grads = read_global(total, core_ref)
    for kind in range(2):
        here = slice(kind * rows, (kind + 1) * rows)
        running = own[here, :]
        for ref in back:
            running = running + ref[here, :].astype(F32)
        running = running + dot_nn(chosen, global_grads[kind])
        outs[kind][...] = running.astype(BF16)


def finish(core, spots, own, back, total):
    args = [own] + list(back) + list(total)
    rows, width = own.shape
    return pl.pallas_call(
        functools.partial(finish_kernel, len(back), len(total)),
        in_specs=[SCALAR] + [WHOLE] * (len(args) + 1),
        out_specs=[WHOLE] * 2,
        out_shape=[jax.ShapeDtypeStruct((rows // 2, width), BF16)] * 2,
        compiler_params=params(),
        cost_estimate=cost(2**28, 4 * 2**20),
        name="finish_key_value_grads",
    )(core, spots, *args)


def levels_of(bit_count):
    bits = list(range(1, bit_count))
    levels = []
    while bits:
        levels.insert(0, bits[-2:])
        bits = bits[:-2]
    return levels


def masks_of(level):
    return [
        sum(1 << bit for place, bit in enumerate(level) if number >> place & 1)
        for number in range(1 << len(level))
    ]


def reduce_level(block, masks):
    size = block.shape[0] // len(masks)
    running = block[:size].astype(F32)
    for number, mask in enumerate(masks):
        if number:
            moved = swap(block[number * size : (number + 1) * size], "seq", mask)
            running = running + moved.astype(F32)
    return running.astype(BF16)


def gather_level(block, masks):
    return [block if mask == 0 else swap(block, "seq", mask) for mask in masks]


def gather_parts(block, levels):
    mine = [block]
    for masks in reversed(levels):
        block = mine[0] if len(mine) == 1 else jnp.concatenate(mine, 0)
        mine = gather_level(block, masks)
    return mine + [swap(part, "seq", 1) for part in mine]


def reduce_parts(blocks, masks):
    running = blocks[0].astype(F32)
    for part, mask in zip(blocks[1:], masks[1:]):
        running = running + swap(part, "seq", mask).astype(F32)
    return running.astype(BF16)


def per_device(queries, keys, values, key_keep, global_positions, gain, cotangent):
    rows = queries.shape[0]
    bit_count = lax.axis_size("seq").bit_length() - 1
    place = lax.axis_index("seq")
    core = (place & 1).reshape(1)
    global_count = global_positions.shape[0]
    keep_row = key_keep.reshape(1, rows)
    gain_row = gain.reshape(1, -1)

    packed = prepare(keep_row, keys, values)
    near = [swap(packed, "seq", 1 << bit) for bit in range(bit_count)]

    levels = [masks_of(level) for level in levels_of(bit_count)]
    order = [0]
    for masks in levels:
        order = [base ^ mask for base in order for mask in masks]
    pieces = len(order)
    chunk_ids = (place >> 1) ^ jnp.array([mask >> 1 for mask in order], jnp.int32)
    chunks = global_positions.reshape(pieces, global_count // pieces)
    match = chunk_ids[:, None] == jnp.arange(pieces, dtype=jnp.int32)[None, :]
    ordered = jnp.sum(jnp.where(match[:, :, None], chunks[None], 0), 1).reshape(global_count)
    spots = jnp.stack([ordered - place * rows, ordered - (place ^ 1) * rows])

    picked = pick(core, spots, packed, near[0])
    for masks in levels:
        picked = reduce_level(picked, masks)
    global_parts = gather_parts(picked, levels)

    group_a = [(keys, values, 0)] + [(x, x, 1) for x in near[:-1]]
    group_b = [(x, x, 1) for x in near[-1:]]
    p_a, *state = forward_phase("forward_a", queries, group_a, keep_row=keep_row)
    peak_a = state[1]
    p_b, attn, peak_b, inverse, sums = forward_phase(
        "forward_b", queries, group_b, global_parts, core, before=state, norm=(cotangent, gain_row)
    )
    head_bits = lax.axis_size("head").bit_length() - 1
    for bit in range(head_bits):
        sums = sums + swap(sums, "head", 1 << bit)

    back_b, *rest = backward_phase(
        "backward_b", queries, p_b, group_b, global_parts, core, peaks=[peak_b, peak_a],
        norm=(inverse, sums, attn, cotangent, gain_row),
    )
    part_count = len(global_parts)
    global_grads, (d_query, normed, grad_a, diag_a) = rest[:part_count], rest[part_count:]
    half = part_count // 2
    reduced = [
        (a.astype(F32) + swap(b, "seq", 1).astype(F32)).astype(BF16)
        for a, b in zip(global_grads[:half], global_grads[half:])
    ]
    total = reduce_parts(reduced, levels[0]) if levels else reduced[0]
    for masks in levels[1:]:
        total = reduce_level(total, masks)
    total_parts = gather_parts(total, levels)

    own, *back_a, d_query = backward_phase(
        "backward_a", queries, p_a, group_a, own=True, grads=(grad_a, diag_a, d_query), last=True
    )
    back = [swap(x, "seq", 1 << bit) for bit, x in enumerate(back_a + [back_b])]
    key_grad, value_grad = finish(core, spots, own, back, total_parts)
    return normed, d_query, key_grad, value_grad


def solution(mesh):
    placed = (
        P("seq", "head"),
        P("seq", "head"),
        P("seq", "head"),
        P("seq"),
        P(),
        P("head"),
        P("seq", "head"),
    )
    return jax.shard_map(
        per_device,
        mesh=mesh,
        in_specs=placed,
        out_specs=(P("seq", "head"), P("seq", "head"), P("seq", "head"), P("seq", "head")),
        check_vma=False,
    )
```

time: 213 us -> 207 us (0.972)
  Pallas kernels: 113 us -> 106 us
    pallas_call x10 -> x7, Pallas kernels: 113 us -> 106 us  [the longest x2 57.2 us: forward_phase(): pl.pallas_call(functools.partial(forward_kernel, len(near), len(parts), k...]
    ppermute x39 -> x31, waiting for transfers between devices: 48.4 us -> 50.3 us  [swap(): return lax.ppermute(block, axis, [(i, i ^ mask) for i in range(count)])]
    ppermute x39 -> x31, starting transfers between devices: 36.6 us -> 36.4 us  [swap(): return lax.ppermute(block, axis, [(i, i ^ mask) for i in range(count)])]
  transfers between devices with their start and end apart: 39 -> 31, of which waited for: 14 -> 14; matrix products, arithmetic and copies ran while one was open for 2% -> 2% of each run, Pallas kernels for 36% -> 25%
where the time goes in v2:
time: 207 us; the launch traced here: 206 us
  Pallas kernels  106 us (51%)
  waiting for transfers between devices  50.3 us (24%)
  starting transfers between devices  36.4 us (18%)
  local copies, waits for them, and re-layouts  6.67 us (3%)
  other arithmetic  5.71 us (3%)
    pallas_call x2, Pallas kernels, forward_phase(): pl.pallas_call(functools.partial(forward_kernel, len(near), len(parts), k...  57.2 us
    ppermute x31, waiting for transfers between devices, swap(): return lax.ppermute(block, axis, [(i, i ^ mask) for i in range(count)])  50.3 us
    pallas_call x2, Pallas kernels, backward_phase(): pl.pallas_call(functools.partial(backward_kernel, len(near), len(parts),...  41.7 us
    ppermute x31, starting transfers between devices, swap(): return lax.ppermute(block, axis, [(i, i ^ mask) for i in range(count)])  36.4 us
    unnamed x36, local copies, waits for them, and re-layouts  4.17 us
  transfers between devices with their start and end apart: 31, of which 14 were waited for; matrix products, arithmetic and copies ran while one was open for 2% of the time, Pallas kernels for 25%

profile of v2, /device:TPU:0, one launch (start us, length us, event | category | flops | bytes accessed | tf_op | source)
XLA Modules:
  0.0 206.5 jit_solution(15549196801726218137)
XLA Ops:
  0.6 2.0 prepare_keys_values.1.own_ref
  2.6 0.5 collective-permute-start.1
  3.1 0.7 broadcast_xor_fusion
  3.7 0.1 iota_compare_fusion
  3.8 0.8 broadcast_in_dim.26
  4.6 0.1 select_reduce_fusion
  4.7 0.1 sub.34
  4.7 0.1 sub.37
  4.8 0.6 pad_add_fusion.spots_ref.refs_1_
  5.4 0.8 copy-done.5
  6.2 2.4 %pick_globals.1 = bf16[384,512]{1,0:T(8,128)(2,1)} custom-call(s32[1]{0:T(128)} %bitcast.1.core_ref.refs_3_.refs_4_.refs_0_, s32[2,384]{1,0:T(2,128)} %pad_add_fusion.spots_ref.refs_1_, bf16[512,512]{1,0:T(8,128)(2,1)} %prepare_keys_values.1.own_ref, bf16[512,512]{1,0:T(8,128)(2,1)} %copy-done.5), custom_call_target="tpu_custom_call" | custom-call | flops 201326592 | bytes 3145728 | tf_op jit(solution)/shard_map/pick_globals/pallas_call | solution.py:490
  8.6 0.9 slice.41
  9.5 2.6 %collective-permute-start.2 = (bf16[192,512]{1,0:T(8,128)(2,1)S(1)}, bf16[192,512]{1,0:T(8,128)(2,1)S(1)}, u32[]{:S(2)}, u32[]{:S(2)}) collective-permute-start(bf16[192,512]{1,0:T(8,128)(2,1)S(1)} %slice.41), channel_id=1, source_target_pairs={{0,4},{2,6},{4,0},{6,2},{8,12},{10,14},{12,8},{14,10},{16,20},{18,... | collective-permute-start | bytes 589832 | tf_op jit(solution)/shard_map/ppermute | solution.py:44
  12.1 5.6 %collective-permute-done.2 = bf16[192,512]{1,0:T(8,128)(2,1)S(1)} collective-permute-done((bf16[192,512]{1,0:T(8,128)(2,1)S(1)}, bf16[192,512]{1,0:T(8,128)(2,1)S(1)}, u32[]{:S(2)}, u32[]{:S(2)}) %collective-permute-start.2) | collective-permute-done | bytes 196640 | tf_op jit(solution)/shard_map/ppermute | solution.py:44
  17.7 1.0 add_convert_fusion.3
  18.7 1.9 collective-permute-start.3
  20.6 2.5 %collective-permute-start.5 = (bf16[48,512]{1,0:T(8,128)(2,1)S(1)}, bf16[48,512]{1,0:T(8,128)(2,1)S(1)}, u32[]{:S(2)}, u32[]{:S(2)}) collective-permute-start(bf16[48,512]{1,0:T(8,128)(2,1)S(1)} %get-tuple-element.58), channel_id=1, source_target_pairs={{0,24},{2,26},{4,28},{6,30},{8,16},{10,18},{12,20},{14,22},{16,8},... | collective-permute-start | bytes 147464 | tf_op jit(solution)/shard_map/ppermute | solution.py:44
  23.0 0.1 collective-permute-start.4
  23.2 1.8 collective-permute-start.13
  25.0 1.5 collective-permute-start.12
  26.4 0.5 collective-permute-done.5
  27.0 1.5 collective-permute-done.4
  28.5 2.1 %collective-permute-start.8 = (bf16[48,512]{1,0:T(8,128)(2,1)S(1)}, bf16[48,512]{1,0:T(8,128)(2,1)S(1)}, u32[]{:S(2)}, u32[]{:S(2)}) collective-permute-start(bf16[48,512]{1,0:T(8,128)(2,1)S(1)} %add_convert_fusion.5), channel_id=1, source_target_pairs={{0,24},{2,26},{4,28},{6,30},{8,16},{10,18},{12,20},{14,22},{16,8},... | collective-permute-start | bytes 147464 | tf_op jit(solution)/shard_map/ppermute | solution.py:44
  30.7 2.3 %collective-permute-start.6 = (bf16[48,512]{1,0:T(8,128)(2,1)S(1)}, bf16[48,512]{1,0:T(8,128)(2,1)S(1)}, u32[]{:S(2)}, u32[]{:S(2)}) collective-permute-start(bf16[48,512]{1,0:T(8,128)(2,1)S(1)} %add_convert_fusion.5), channel_id=1, source_target_pairs={{0,8},{2,10},{4,12},{6,14},{8,0},{10,2},{12,4},{14,6},{16,24},{18,... | collective-permute-start | bytes 147464 | tf_op jit(solution)/shard_map/ppermute | solution.py:44
  33.0 8.1 %collective-permute-done.8 = bf16[48,512]{1,0:T(8,128)(2,1)S(1)} collective-permute-done((bf16[48,512]{1,0:T(8,128)(2,1)S(1)}, bf16[48,512]{1,0:T(8,128)(2,1)S(1)}, u32[]{:S(2)}, u32[]{:S(2)}) %collective-permute-start.8) | collective-permute-done | bytes 49184 | tf_op jit(solution)/shard_map/ppermute | solution.py:44
  41.1 0.1 collective-permute-done.6
  41.2 1.6 collective-permute-start.9
  42.8 1.4 collective-permute-start
  44.2 0.6 reshape.66.refs_12_.refs_15_
  44.8 2.2 %collective-permute-done.9.refs_5_.refs_6_ = bf16[192,512]{1,0:T(8,128)(2,1)S(1)} collective-permute-done((bf16[192,512]{1,0:T(8,128)(2,1)S(1)}, bf16[192,512]{1,0:T(8,128)(2,1)S(1)}, u32[]{:S(2)}, u32[]{:S(2)}) %collective-permute-start.9) | collective-permute-done | bytes 196640 | tf_op jit(solution)/shard_map/ppermute | solution.py:44
  47.0 0.8 copy-done.11
  47.8 0.8 copy-done.12
  48.6 26.9 %forward_a.1 = (bf16[8192,1024]{1,0:T(8,128)(2,1)}, f32[256,4096]{1,0:T(8,128)}, f32[256,512]{1,0:T(8,128)}, f32[256,512]{1,0:T(8,128)}) custom-call(bf16[256,4096]{1,0:T(8,128)(2,1)} %refs_0_.7, bf16[256,512]{1,0:T(8,128)(2,1)} %refs_2_.3, bf16[256,512]{1,0:T(8,128)(2,1)} %refs_3_.1, bf16[512,512]{1,0:T(8,128)(2,1)} %copy-done.5, ...), custom_call_target="tpu_custom_call" | custom-call | flops 8589934592 | bytes 16777216 | tf_op jit(solution)/shard_map/forward_a/pallas_call | solution.py:296
  75.5 0.7 copy-done.14
  76.4 30.3 %forward_b.1 = (bf16[8192,640]{1,0:T(8,128)(2,1)}, f32[256,4096]{1,0:T(8,128)}, f32[256,512]{1,0:T(8,128)}, f32[256,512]{1,0:T(8,128)}, f32[2,256]{1,0:T(2,128)}) custom-call(bf16[256,4096]{1,0:T(8,128)(2,1)} %refs_0_.7, bf16[512,512]{1,0:T(8,128)(2,1)} %copy-done.14, bf16[512,512]{1,0:T(8,128)(2,1)} %copy-done.14, ...), custom_call_target="tpu_custom_call" | custom-call | flops 5368709120 | bytes 10485760 | tf_op jit(solution)/shard_map/forward_b/pallas_call | solution.py:296
  106.7 1.6 collective-permute-start.14
  108.3 2.3 %collective-permute-done.14 = f32[2,256]{1,0:T(2,128)S(1)} collective-permute-done((f32[2,256]{1,0:T(2,128)}, f32[2,256]{1,0:T(2,128)S(1)}, u32[]{:S(2)}, u32[]{:S(2)}) %collective-permute-start.14) | collective-permute-done | bytes 2080 | tf_op jit(solution)/shard_map/ppermute | solution.py:44
  110.6 1.2 add.37.refs_12_
  111.8 17.5 %backward_b.1 = (bf16[512,512]{1,0:T(8,128)(2,1)}, bf16[192,512]{1,0:T(8,128)(2,1)}, bf16[192,512]{1,0:T(8,128)(2,1)}, bf16[192,512]{1,0:T(8,128)(2,1)}, bf16[19...) custom-call(bf16[256,4096]{1,0:T(8,128)(2,1)} %refs_0_.7, ...), custom_call_target="tpu_custom_call" | custom-call | flops 8053063680 | bytes 10485760 | tf_op jit(solution)/shard_map/backward_b/pallas_call | solution.py:457
  129.4 0.5 collective-permute-start.19
  129.9 1.1 collective-permute-done.20
  131.1 1.0 add_convert_fusion.1
  132.0 1.6 collective-permute-start.21
  133.6 5.4 %collective-permute-done.21 = bf16[192,512]{1,0:T(8,128)(2,1)S(1)} collective-permute-done((bf16[192,512]{1,0:T(8,128)(2,1)S(1)}, bf16[192,512]{1,0:T(8,128)(2,1)S(1)}, u32[]{:S(2)}, u32[]{:S(2)}) %collective-permute-start.21) | collective-permute-done | bytes 196640 | tf_op jit(solution)/shard_map/ppermute | solution.py:44
  139.1 1.0 add_convert_fusion
  140.1 0.9 collective-permute-start.22
  141.0 2.0 collective-permute-start.24
  143.0 0.6 collective-permute-start.23
  143.6 24.2 %backward_a.1 = (f32[512,512]{1,0:T(8,128)}, bf16[512,512]{1,0:T(8,128)(2,1)}, bf16[512,512]{1,0:T(8,128)(2,1)}, bf16[512,512]{1,0:T(8,128)(2,1)}, bf16[256,4096]{1,0:T(8,128)(2,1)}) custom-call(bf16[256,4096]{1,0:T(8,128)(2,1)} %refs_0_.7, bf16[8192,1024]{1,0:T(8,128)(2,1)} %get-tuple-element.38.refs_1_, bf16[256,512]{1,0:T(8,128)(2,1)} %refs_2_.3, ...), custom_call_target="tpu_custom_call" | custom-call | flops 12884901888 | bytes 16777216 | tf_op jit(solution)/shard_map/backward_a/pallas_call | solution.py:457
  167.9 2.6 %collective-permute-start.27 = (bf16[48,512]{1,0:T(8,128)(2,1)S(1)}, bf16[48,512]{1,0:T(8,128)(2,1)S(1)}, u32[]{:S(2)}, u32[]{:S(2)}) collective-permute-start(bf16[48,512]{1,0:T(8,128)(2,1)S(1)} %add_convert_fusion.4), channel_id=1, source_target_pairs={{0,24},{2,26},{4,28},{6,30},{8,16},{10,18},{12,20},{14,22},{16,8},... | collective-permute-start | bytes 147464 | tf_op jit(solution)/shard_map/ppermute | solution.py:44
  170.5 0.7 collective-permute-start.26
  171.2 1.1 collective-permute-start.25
  172.4 1.5 collective-permute-start.16
  173.9 0.2 collective-permute-done.27
  174.1 2.3 %collective-permute-start.17 = (bf16[512,512]{1,0:T(8,128)(2,1)}, bf16[512,512]{1,0:T(8,128)(2,1)S(1)}, u32[]{:S(2)}, u32[]{:S(2)}) collective-permute-start(bf16[512,512]{1,0:T(8,128)(2,1)} %get-tuple-element.46), channel_id=1, source_target_pairs={{0,8},{2,10},{4,12},{6,14},{8,0},{10,2},{12,4},{14,6},{16,24},{18,... | collective-permute-start | bytes 1572872 | tf_op jit(solution)/shard_map/ppermute | solution.py:44
  176.4 0.1 collective-permute-done.26
  176.5 1.0 collective-permute-start.18
  177.6 1.6 collective-permute-start.28
  179.1 11.2 %collective-permute-done.28.refs_8_ = bf16[192,512]{1,0:T(8,128)(2,1)S(1)} collective-permute-done((bf16[192,512]{1,0:T(8,128)(2,1)S(1)}, bf16[192,512]{1,0:T(8,128)(2,1)S(1)}, u32[]{:S(2)}, u32[]{:S(2)}) %collective-permute-start.28) | collective-permute-done | bytes 196640 | tf_op jit(solution)/shard_map/ppermute | solution.py:44
  190.3 6.2 %collective-permute-done.17.refs_5_ = bf16[512,512]{1,0:T(8,128)(2,1)S(1)} collective-permute-done((bf16[512,512]{1,0:T(8,128)(2,1)}, bf16[512,512]{1,0:T(8,128)(2,1)S(1)}, u32[]{:S(2)}, u32[]{:S(2)}) %collective-permute-start.17) | collective-permute-done | bytes 524320 | tf_op jit(solution)/shard_map/ppermute | solution.py:44
  196.5 5.8 %collective-permute-done.18.refs_6_ = bf16[512,512]{1,0:T(8,128)(2,1)S(1)} collective-permute-done((bf16[512,512]{1,0:T(8,128)(2,1)S(1)}, bf16[512,512]{1,0:T(8,128)(2,1)S(1)}, u32[]{:S(2)}, u32[]{:S(2)}) %collective-permute-start.18) | collective-permute-done | bytes 524320 | tf_op jit(solution)/shard_map/ppermute | solution.py:44
  202.3 0.7 copy-done.4
  203.1 0.1 copy-done.7
  203.2 3.3 %finish_key_value_grads.1 = (bf16[256,512]{1,0:T(8,128)(2,1)}, bf16[256,512]{1,0:T(8,128)(2,1)}) custom-call(s32[1]{0:T(128)} %bitcast.1.core_ref.refs_3_.refs_4_.refs_0_, s32[2,384]{1,0:T(2,128)} %pad_add_fusion.spots_ref.refs_1_, f32[512,512]{1,0:T(8,128)} %get-tuple-element.43.refs_2_, bf16[512,512]{1,0:T(8,128)(2,1)} %copy-done.1, ...), custom_call_target="tpu_custom_call" | custom-call | flops 268435456 | bytes 4194304 | tf_op jit(solution)/shard_map/finish_key_value_grads/pallas_call | solution.py:523
  (61 shorter events, 0.6 us)
Async XLA Ops:
  0.6 43.5 %copy-start.10 = (bf16[4096]{0:T(1024)(128)(2,1)S(1)}, bf16[4096]{0:T(1024)(128)(2,1)}, u32[]{:S(2)}) copy-start(bf16[4096]{0:T(1024)(128)(2,1)} %param.13) | copy-start | bytes 24580
  2.6 2.8 %collective-permute-start.1 = (bf16[512,512]{1,0:T(8,128)(2,1)}, bf16[512,512]{1,0:T(8,128)(2,1)S(1)}, u32[]{:S(2)}, u32[]{:S(2)}) collective-permute-start(bf16[512,512]{1,0:T(8,128)(2,1)} %prepare_keys_values.1.own_ref), channel_id=1, source_target_pairs={{0,2},{2,0},{4,6},{6,4},{8,10},{10,8},{12,14},{14,12},{16,18},{18,... | collective-permute-start | bytes 1572872 | tf_op jit(solution)/shard_map/ppermute | solution.py:44
  5.4 0.8 copy-start.5
  9.5 8.1 %collective-permute-start.2 = (bf16[192,512]{1,0:T(8,128)(2,1)S(1)}, bf16[192,512]{1,0:T(8,128)(2,1)S(1)}, u32[]{:S(2)}, u32[]{:S(2)}) collective-permute-start(bf16[192,512]{1,0:T(8,128)(2,1)S(1)} %slice.41), channel_id=1, source_target_pairs={{0,4},{2,6},{4,0},{6,2},{8,12},{10,14},{12,8},{14,10},{16,20},{18,... | collective-permute-start | bytes 589832 | tf_op jit(solution)/shard_map/ppermute | solution.py:44
  18.7 7.8 %collective-permute-start.3 = (bf16[48,512]{1,0:T(8,128)(2,1)S(1)}, bf16[48,512]{1,0:T(8,128)(2,1)S(1)}, u32[]{:S(2)}, u32[]{:S(2)}) collective-permute-start(bf16[48,512]{1,0:T(8,128)(2,1)S(1)} %get-tuple-element.57), channel_id=1, source_target_pairs={{0,8},{2,10},{4,12},{6,14},{8,0},{10,2},{12,4},{14,6},{16,24},{18,... | collective-permute-start | bytes 147464 | tf_op jit(solution)/shard_map/ppermute | solution.py:44
  20.6 6.4 %collective-permute-start.5 = (bf16[48,512]{1,0:T(8,128)(2,1)S(1)}, bf16[48,512]{1,0:T(8,128)(2,1)S(1)}, u32[]{:S(2)}, u32[]{:S(2)}) collective-permute-start(bf16[48,512]{1,0:T(8,128)(2,1)S(1)} %get-tuple-element.58), channel_id=1, source_target_pairs={{0,24},{2,26},{4,28},{6,30},{8,16},{10,18},{12,20},{14,22},{16,8},... | collective-permute-start | bytes 147464 | tf_op jit(solution)/shard_map/ppermute | solution.py:44
  23.0 5.5 %collective-permute-start.4 = (bf16[48,512]{1,0:T(8,128)(2,1)S(1)}, bf16[48,512]{1,0:T(8,128)(2,1)S(1)}, u32[]{:S(2)}, u32[]{:S(2)}) collective-permute-start(bf16[48,512]{1,0:T(8,128)(2,1)S(1)} %get-tuple-element.59), channel_id=1, source_target_pairs={{0,16},{2,18},{4,20},{6,22},{8,24},{10,26},{12,28},{14,30},{16,0},... | collective-permute-start | bytes 147464 | tf_op jit(solution)/shard_map/ppermute | solution.py:44
  23.2 23.8 %collective-permute-start.13 = (bf16[512,512]{1,0:T(8,128)(2,1)}, bf16[512,512]{1,0:T(8,128)(2,1)S(1)}, u32[]{:S(2)}, u32[]{:S(2)}) collective-permute-start(bf16[512,512]{1,0:T(8,128)(2,1)} %prepare_keys_values.1.own_ref), channel_id=1, source_target_pairs={{0,8},{2,10},{4,12},{6,14},{8,0},{10,2},{12,4},{14,6},{16,24},{18,... | collective-permute-start | bytes 1572872 | tf_op jit(solution)/shard_map/ppermute | solution.py:44
  25.0 22.0 %collective-permute-start.12 = (bf16[512,512]{1,0:T(8,128)(2,1)}, bf16[512,512]{1,0:T(8,128)(2,1)S(1)}, u32[]{:S(2)}, u32[]{:S(2)}) collective-permute-start(bf16[512,512]{1,0:T(8,128)(2,1)} %prepare_keys_values.1.own_ref), channel_id=1, source_target_pairs={{0,4},{2,6},{4,0},{6,2},{8,12},{10,14},{12,8},{14,10},{16,20},{18,... | collective-permute-start | bytes 1572872 | tf_op jit(solution)/shard_map/ppermute | solution.py:44
  28.5 12.5 %collective-permute-start.8 = (bf16[48,512]{1,0:T(8,128)(2,1)S(1)}, bf16[48,512]{1,0:T(8,128)(2,1)S(1)}, u32[]{:S(2)}, u32[]{:S(2)}) collective-permute-start(bf16[48,512]{1,0:T(8,128)(2,1)S(1)} %add_convert_fusion.5), channel_id=1, source_target_pairs={{0,24},{2,26},{4,28},{6,30},{8,16},{10,18},{12,20},{14,22},{16,8},... | collective-permute-start | bytes 147464 | tf_op jit(solution)/shard_map/ppermute | solution.py:44
  30.7 10.4 %collective-permute-start.7 = (bf16[48,512]{1,0:T(8,128)(2,1)S(1)}, bf16[48,512]{1,0:T(8,128)(2,1)S(1)}, u32[]{:S(2)}, u32[]{:S(2)}) collective-permute-start(bf16[48,512]{1,0:T(8,128)(2,1)S(1)} %add_convert_fusion.5), channel_id=1, source_target_pairs={{0,16},{2,18},{4,20},{6,22},{8,24},{10,26},{12,28},{14,30},{16,0},... | collective-permute-start | bytes 147464 | tf_op jit(solution)/shard_map/ppermute | solution.py:44
  30.7 10.5 %collective-permute-start.6 = (bf16[48,512]{1,0:T(8,128)(2,1)S(1)}, bf16[48,512]{1,0:T(8,128)(2,1)S(1)}, u32[]{:S(2)}, u32[]{:S(2)}) collective-permute-start(bf16[48,512]{1,0:T(8,128)(2,1)S(1)} %add_convert_fusion.5), channel_id=1, source_target_pairs={{0,8},{2,10},{4,12},{6,14},{8,0},{10,2},{12,4},{14,6},{16,24},{18,... | collective-permute-start | bytes 147464 | tf_op jit(solution)/shard_map/ppermute | solution.py:44
  41.2 34.2 %copy-start.9 = (bf16[192,512]{1,0:T(8,128)(2,1)}, bf16[192,512]{1,0:T(8,128)(2,1)S(1)}, u32[]{:S(2)}) copy-start(bf16[192,512]{1,0:T(8,128)(2,1)S(1)} %pad_maximum_fusion.refs_4_.refs_5_) | copy-start | bytes 589828
  41.2 5.7 %collective-permute-start.9 = (bf16[192,512]{1,0:T(8,128)(2,1)S(1)}, bf16[192,512]{1,0:T(8,128)(2,1)S(1)}, u32[]{:S(2)}, u32[]{:S(2)}) collective-permute-start(bf16[192,512]{1,0:T(8,128)(2,1)S(1)} %pad_maximum_fusion.refs_4_.refs_5_), channel_id=1, source_target_pairs={{0,4},{2,6},{4,0},{6,2},{8,12},{10,14},{12,8},{14,10},{16,20},{18,... | collective-permute-start | bytes 589832 | tf_op jit(solution)/shard_map/ppermute | solution.py:44
  42.8 32.7 %collective-permute-start = (bf16[512,512]{1,0:T(8,128)(2,1)}, bf16[512,512]{1,0:T(8,128)(2,1)S(1)}, u32[]{:S(2)}, u32[]{:S(2)}) collective-permute-start(bf16[512,512]{1,0:T(8,128)(2,1)} %prepare_keys_values.1.own_ref), channel_id=1, source_target_pairs={{0,16},{2,18},{4,20},{6,22},{8,24},{10,26},{12,28},{14,30},{16,0},... | collective-permute-start | bytes 1572872 | tf_op jit(solution)/shard_map/ppermute | solution.py:44
  44.8 30.7 %collective-permute-start.10 = (bf16[192,512]{1,0:T(8,128)(2,1)S(1)}, bf16[192,512]{1,0:T(8,128)(2,1)S(1)}, u32[]{:S(2)}, u32[]{:S(2)}) collective-permute-start(bf16[192,512]{1,0:T(8,128)(2,1)S(1)} %pad_maximum_fusion.refs_4_.refs_5_), channel_id=1, source_target_pairs={{0,2},{2,0},{4,6},{6,4},{8,10},{10,8},{12,14},{14,12},{16,18},{18,... | collective-permute-start | bytes 589832 | tf_op jit(solution)/shard_map/ppermute | solution.py:44
  46.9 28.5 %copy-start.15 = (bf16[192,512]{1,0:T(8,128)(2,1)}, bf16[192,512]{1,0:T(8,128)(2,1)S(1)}, u32[]{:S(2)}) copy-start(bf16[192,512]{1,0:T(8,128)(2,1)S(1)} %collective-permute-done.9.refs_5_.refs_6_) | copy-start | bytes 589828
  46.9 28.5 %collective-permute-start.11 = (bf16[192,512]{1,0:T(8,128)(2,1)S(1)}, bf16[192,512]{1,0:T(8,128)(2,1)S(1)}, u32[]{:S(2)}, u32[]{:S(2)}) collective-permute-start(bf16[192,512]{1,0:T(8,128)(2,1)S(1)} %collective-permute-done.9.refs_5_.refs_6_), channel_id=1, source_target_pairs={{0,2},{2,0},{4,6},{6,4},{8,10},{10,8},{12,14},{14,12},{16,18},{18,... | collective-permute-start | bytes 589832 | tf_op jit(solution)/shard_map/ppermute | solution.py:44
  47.0 0.8 copy-start.11
  47.8 0.8 copy-start.12
  75.5 0.8 copy-start.14
  75.5 0.8 copy-start.16
  75.5 0.9 copy-start.17
  106.7 3.9 %collective-permute-start.14 = (f32[2,256]{1,0:T(2,128)}, f32[2,256]{1,0:T(2,128)S(1)}, u32[]{:S(2)}, u32[]{:S(2)}) collective-permute-start(f32[2,256]{1,0:T(2,128)} %get-tuple-element.35), channel_id=1, source_target_pairs={{0,1},{1,0},{2,3},{3,2},{4,5},{5,4},{6,7},{7,6},{8,9},{9,8},{10,11... | collective-permute-start | bytes 6152 | tf_op jit(solution)/shard_map/ppermute | solution.py:44
  129.3 1.7 collective-permute-start.20
  129.4 4.2 %collective-permute-start.19 = (bf16[192,512]{1,0:T(8,128)(2,1)}, bf16[192,512]{1,0:T(8,128)(2,1)S(1)}, u32[]{:S(2)}, u32[]{:S(2)}) collective-permute-start(bf16[192,512]{1,0:T(8,128)(2,1)} %get-tuple-element.49), channel_id=1, source_target_pairs={{0,2},{2,0},{4,6},{6,4},{8,10},{10,8},{12,14},{14,12},{16,18},{18,... | collective-permute-start | bytes 589832 | tf_op jit(solution)/shard_map/ppermute | solution.py:44
  132.0 7.0 %collective-permute-start.21 = (bf16[192,512]{1,0:T(8,128)(2,1)S(1)}, bf16[192,512]{1,0:T(8,128)(2,1)S(1)}, u32[]{:S(2)}, u32[]{:S(2)}) collective-permute-start(bf16[192,512]{1,0:T(8,128)(2,1)S(1)} %add_convert_fusion.1), channel_id=1, source_target_pairs={{0,4},{2,6},{4,0},{6,2},{8,12},{10,14},{12,8},{14,10},{16,20},{18,... | collective-permute-start | bytes 589832 | tf_op jit(solution)/shard_map/ppermute | solution.py:44
  140.1 27.8 %collective-permute-start.22 = (bf16[48,512]{1,0:T(8,128)(2,1)S(1)}, bf16[48,512]{1,0:T(8,128)(2,1)S(1)}, u32[]{:S(2)}, u32[]{:S(2)}) collective-permute-start(bf16[48,512]{1,0:T(8,128)(2,1)S(1)} %get-tuple-element.54), channel_id=1, source_target_pairs={{0,8},{2,10},{4,12},{6,14},{8,0},{10,2},{12,4},{14,6},{16,24},{18,... | collective-permute-start | bytes 147464 | tf_op jit(solution)/shard_map/ppermute | solution.py:44
  141.0 26.9 %collective-permute-start.24 = (bf16[48,512]{1,0:T(8,128)(2,1)S(1)}, bf16[48,512]{1,0:T(8,128)(2,1)S(1)}, u32[]{:S(2)}, u32[]{:S(2)}) collective-permute-start(bf16[48,512]{1,0:T(8,128)(2,1)S(1)} %get-tuple-element.55), channel_id=1, source_target_pairs={{0,24},{2,26},{4,28},{6,30},{8,16},{10,18},{12,20},{14,22},{16,8},... | collective-permute-start | bytes 147464 | tf_op jit(solution)/shard_map/ppermute | solution.py:44
  143.0 24.9 %collective-permute-start.23 = (bf16[48,512]{1,0:T(8,128)(2,1)S(1)}, bf16[48,512]{1,0:T(8,128)(2,1)S(1)}, u32[]{:S(2)}, u32[]{:S(2)}) collective-permute-start(bf16[48,512]{1,0:T(8,128)(2,1)S(1)} %get-tuple-element.56), channel_id=1, source_target_pairs={{0,16},{2,18},{4,20},{6,22},{8,24},{10,26},{12,28},{14,30},{16,0},... | collective-permute-start | bytes 147464 | tf_op jit(solution)/shard_map/ppermute | solution.py:44
  143.6 32.9 %copy-start.13 = (bf16[512,512]{1,0:T(8,128)(2,1)S(1)}, bf16[512,512]{1,0:T(8,128)(2,1)}, u32[]{:S(2)}) copy-start(bf16[512,512]{1,0:T(8,128)(2,1)} %get-tuple-element.47) | copy-start | bytes 1572868
  167.8 11.3 %collective-permute-start.15 = (bf16[512,512]{1,0:T(8,128)(2,1)}, bf16[512,512]{1,0:T(8,128)(2,1)S(1)}, u32[]{:S(2)}, u32[]{:S(2)}) collective-permute-start(bf16[512,512]{1,0:T(8,128)(2,1)} %get-tuple-element.44), channel_id=1, source_target_pairs={{0,2},{2,0},{4,6},{6,4},{8,10},{10,8},{12,14},{14,12},{16,18},{18,... | collective-permute-start | bytes 1572872 | tf_op jit(solution)/shard_map/ppermute | solution.py:44
  167.9 6.1 %collective-permute-start.27 = (bf16[48,512]{1,0:T(8,128)(2,1)S(1)}, bf16[48,512]{1,0:T(8,128)(2,1)S(1)}, u32[]{:S(2)}, u32[]{:S(2)}) collective-permute-start(bf16[48,512]{1,0:T(8,128)(2,1)S(1)} %add_convert_fusion.4), channel_id=1, source_target_pairs={{0,24},{2,26},{4,28},{6,30},{8,16},{10,18},{12,20},{14,22},{16,8},... | collective-permute-start | bytes 147464 | tf_op jit(solution)/shard_map/ppermute | solution.py:44
  170.5 6.0 %collective-permute-start.26 = (bf16[48,512]{1,0:T(8,128)(2,1)S(1)}, bf16[48,512]{1,0:T(8,128)(2,1)S(1)}, u32[]{:S(2)}, u32[]{:S(2)}) collective-permute-start(bf16[48,512]{1,0:T(8,128)(2,1)S(1)} %add_convert_fusion.4), channel_id=1, source_target_pairs={{0,16},{2,18},{4,20},{6,22},{8,24},{10,26},{12,28},{14,30},{16,0},... | collective-permute-start | bytes 147464 | tf_op jit(solution)/shard_map/ppermute | solution.py:44
  171.2 6.3 %collective-permute-start.25 = (bf16[48,512]{1,0:T(8,128)(2,1)S(1)}, bf16[48,512]{1,0:T(8,128)(2,1)S(1)}, u32[]{:S(2)}, u32[]{:S(2)}) collective-permute-start(bf16[48,512]{1,0:T(8,128)(2,1)S(1)} %add_convert_fusion.4), channel_id=1, source_target_pairs={{0,8},{2,10},{4,12},{6,14},{8,0},{10,2},{12,4},{14,6},{16,24},{18,... | collective-permute-start | bytes 147464 | tf_op jit(solution)/shard_map/ppermute | solution.py:44
  172.4 17.9 %collective-permute-start.16 = (bf16[512,512]{1,0:T(8,128)(2,1)}, bf16[512,512]{1,0:T(8,128)(2,1)S(1)}, u32[]{:S(2)}, u32[]{:S(2)}) collective-permute-start(bf16[512,512]{1,0:T(8,128)(2,1)} %get-tuple-element.45), channel_id=1, source_target_pairs={{0,4},{2,6},{4,0},{6,2},{8,12},{10,14},{12,8},{14,10},{16,20},{18,... | collective-permute-start | bytes 1572872 | tf_op jit(solution)/shard_map/ppermute | solution.py:44
  174.1 22.4 %collective-permute-start.17 = (bf16[512,512]{1,0:T(8,128)(2,1)}, bf16[512,512]{1,0:T(8,128)(2,1)S(1)}, u32[]{:S(2)}, u32[]{:S(2)}) collective-permute-start(bf16[512,512]{1,0:T(8,128)(2,1)} %get-tuple-element.46), channel_id=1, source_target_pairs={{0,8},{2,10},{4,12},{6,14},{8,0},{10,2},{12,4},{14,6},{16,24},{18,... | collective-permute-start | bytes 1572872 | tf_op jit(solution)/shard_map/ppermute | solution.py:44
  176.5 25.8 %collective-permute-start.18 = (bf16[512,512]{1,0:T(8,128)(2,1)S(1)}, bf16[512,512]{1,0:T(8,128)(2,1)S(1)}, u32[]{:S(2)}, u32[]{:S(2)}) collective-permute-start(bf16[512,512]{1,0:T(8,128)(2,1)S(1)} %copy-done.13), channel_id=1, source_target_pairs={{0,16},{2,18},{4,20},{6,22},{8,24},{10,26},{12,28},{14,30},{16,0},... | collective-permute-start | bytes 1572872 | tf_op jit(solution)/shard_map/ppermute | solution.py:44
  177.5 24.8 %copy-start = (bf16[192,512]{1,0:T(8,128)(2,1)}, bf16[192,512]{1,0:T(8,128)(2,1)S(1)}, u32[]{:S(2)}) copy-start(bf16[192,512]{1,0:T(8,128)(2,1)S(1)} %pad_maximum_fusion.1.refs_7_) | copy-start | bytes 589828
  177.6 12.7 %collective-permute-start.28 = (bf16[192,512]{1,0:T(8,128)(2,1)S(1)}, bf16[192,512]{1,0:T(8,128)(2,1)S(1)}, u32[]{:S(2)}, u32[]{:S(2)}) collective-permute-start(bf16[192,512]{1,0:T(8,128)(2,1)S(1)} %pad_maximum_fusion.1.refs_7_), channel_id=1, source_target_pairs={{0,4},{2,6},{4,0},{6,2},{8,12},{10,14},{12,8},{14,10},{16,20},{18,... | collective-permute-start | bytes 589832 | tf_op jit(solution)/shard_map/ppermute | solution.py:44
  179.1 23.2 %copy-start.1 = (bf16[512,512]{1,0:T(8,128)(2,1)}, bf16[512,512]{1,0:T(8,128)(2,1)S(1)}, u32[]{:S(2)}) copy-start(bf16[512,512]{1,0:T(8,128)(2,1)S(1)} %collective-permute-done.15.refs_3_) | copy-start | bytes 1572868
  179.1 23.2 %collective-permute-start.29 = (bf16[192,512]{1,0:T(8,128)(2,1)S(1)}, bf16[192,512]{1,0:T(8,128)(2,1)S(1)}, u32[]{:S(2)}, u32[]{:S(2)}) collective-permute-start(bf16[192,512]{1,0:T(8,128)(2,1)S(1)} %pad_maximum_fusion.1.refs_7_), channel_id=1, source_target_pairs={{0,2},{2,0},{4,6},{6,4},{8,10},{10,8},{12,14},{14,12},{16,18},{18,... | collective-permute-start | bytes 589832 | tf_op jit(solution)/shard_map/ppermute | solution.py:44
  190.3 12.0 %copy-start.6 = (bf16[192,512]{1,0:T(8,128)(2,1)}, bf16[192,512]{1,0:T(8,128)(2,1)S(1)}, u32[]{:S(2)}) copy-start(bf16[192,512]{1,0:T(8,128)(2,1)S(1)} %collective-permute-done.28.refs_8_) | copy-start | bytes 589828
  190.3 12.0 %collective-permute-start.30 = (bf16[192,512]{1,0:T(8,128)(2,1)S(1)}, bf16[192,512]{1,0:T(8,128)(2,1)S(1)}, u32[]{:S(2)}, u32[]{:S(2)}) collective-permute-start(bf16[192,512]{1,0:T(8,128)(2,1)S(1)} %collective-permute-done.28.refs_8_), channel_id=1, source_target_pairs={{0,2},{2,0},{4,6},{6,4},{8,10},{10,8},{12,14},{14,12},{16,18},{18,... | collective-permute-start | bytes 589832 | tf_op jit(solution)/shard_map/ppermute | solution.py:44
  190.3 12.0 %copy-start.2 = (bf16[512,512]{1,0:T(8,128)(2,1)}, bf16[512,512]{1,0:T(8,128)(2,1)S(1)}, u32[]{:S(2)}) copy-start(bf16[512,512]{1,0:T(8,128)(2,1)S(1)} %collective-permute-done.16.refs_4_) | copy-start | bytes 1572868
  196.5 5.9 %copy-start.3 = (bf16[512,512]{1,0:T(8,128)(2,1)}, bf16[512,512]{1,0:T(8,128)(2,1)S(1)}, u32[]{:S(2)}) copy-start(bf16[512,512]{1,0:T(8,128)(2,1)S(1)} %collective-permute-done.17.refs_5_) | copy-start | bytes 1572868
  202.3 0.8 copy-start.4
  202.3 0.9 copy-start.7
  202.3 0.9 copy-start.8

commit v3 on v2

--- a/solution.py
+++ b/solution.py
@@ -19,7 +19,9 @@
 HIDDEN_ABOVE = 100.0
 SCALING = HD ** (-0.5)
 EXPONENT = SCALING * math.log2(math.e)
-VMEM_BYTES = 56 * 2**20
+VMEM_BYTES = 28 * 2**20
+FAR_STAYS = False
+GLOBALS_STAY = False
 TOTAL_LEAST = 2.0**-80
 TOTAL_MOST = 2.0**100
 
@@ -44,6 +46,10 @@
     return lax.ppermute(block, axis, [(i, i ^ mask) for i in range(count)])
 
 
+def off_chip(block):
+    return pltpu.with_memory_space_constraint(block, pltpu.HBM)
+
+
 def params():
     return pltpu.CompilerParams(vmem_limit_bytes=VMEM_BYTES)
 
@@ -66,6 +72,7 @@
 
 SCALAR = pl.BlockSpec(memory_space=pltpu.SMEM)
 WHOLE = pl.BlockSpec(memory_space=pltpu.VMEM)
+ANYWHERE = pl.BlockSpec(memory_space=pl.ANY)
 
 
 def read_global(refs, core_ref):
@@ -127,9 +134,11 @@
     )(keep_row, keys, values)
 
 
-def forward_kernel(near, parts, own, first, last, *refs):
+def forward_kernel(near, parts, own, first, last, kept, resident, waits, *refs):
     refs = list(refs)
     take = refs.pop
+    for _ in range(waits):
+        take(0)
     q_ref = take(0)
     key_list, value_list, _ = read_slots(take, near, parts)
     keep_ref = take(0) if own else None
@@ -137,12 +146,14 @@
         sum_ref, peak_ref, total_ref = take(0), take(0), take(0)
     if last:
         cot_ref, gain_ref = take(0), take(0)
-    p_ref, out_ref, peak_out, total_out = take(0), take(0), take(0), take(0)
+    p_refs = [take(0) for _ in kept]
+    out_ref, peak_out, total_out = take(0), take(0), take(0)
     if last:
         rows_ref, square_acc, cross_acc = take(0), take(0), take(0)
         step = pl.program_id(0)
 
     rows = q_ref.shape[0]
+    base = pl.multiple_of(pl.program_id(0) * (GROUP * rows), GROUP * rows)
     lanes = lane_of((rows, HD))
     unit = (lanes == 0).astype(BF16)
     wide_keys, wide_values = [], []
@@ -164,9 +175,11 @@
         return dot_nt(q, wide_keys[number])
 
     def keep_exponentials(head, number, value):
-        start = sum(k.shape[0] for k in wide_keys[:number])
+        group = next(i for i, members in enumerate(kept) if number in members)
+        start = sum(wide_keys[i].shape[0] for i in kept[group] if i < number)
         stop = start + wide_keys[number].shape[0]
-        p_ref[head * rows : (head + 1) * rows, start:stop] = value
+        lower = base + head * rows if resident[group] else head * rows
+        p_refs[group][pl.ds(lower, rows), start:stop] = value
         return dot_nn(value, wide_values[number])
 
     totals = jnp.ones((rows, HD), F32)
@@ -259,13 +272,19 @@
             rows_ref[...] = jnp.concatenate([square_row, cross_row], 0)
 
 
-def forward_phase(name, queries, near, parts=(), core=None, keep_row=None, before=None, norm=None):
+def forward_phase(
+    name, queries, near, parts=(), core=None, keep_row=None, before=None, norm=None, kept=None,
+    resident=(False, False), after=(),
+):
     rows, width = queries.shape
     steps = width // (GROUP * HD)
     wide = GROUP * HD
     args, specs, slots = slot_operands(near, parts, core)
-    args.insert(0, queries)
-    specs.insert(0, column_block(rows, wide))
+    block_rows = [rows] * len(near) + ([slots - rows * len(near)] if parts else [])
+    sizes = [slots] if kept is None else [sum(block_rows[i] for i in members) for members in kept]
+    kept = [range(len(near) + 1)] if kept is None else kept
+    args = list(after) + [queries] + args
+    specs = [ANYWHERE] * len(after) + [column_block(rows, wide)] + specs
     if keep_row is not None:
         args.append(keep_row)
         specs.append(fixed_block(keep_row.shape))
@@ -275,14 +294,16 @@
     if norm is not None:
         args += list(norm)
         specs += [column_block(rows, wide), column_block(1, wide)]
-    out_shapes = [
-        jax.ShapeDtypeStruct((steps * GROUP * rows, slots), BF16),
-        jax.ShapeDtypeStruct((rows, width), F32),
+    place = jax.ShapeDtypeStruct if norm is None else pltpu.HBM
+    out_shapes = [pltpu.HBM((steps * GROUP * rows, size), BF16) for size in sizes] + [
+        place((rows, width), F32),
         jax.ShapeDtypeStruct((rows, steps * HD), F32),
         jax.ShapeDtypeStruct((rows, steps * HD), F32),
     ]
     out_specs = [
-        pl.BlockSpec((GROUP * rows, slots), lambda a: (a, 0)),
+        WHOLE if stay else pl.BlockSpec((GROUP * rows, size), lambda a: (a, 0))
+        for size, stay in zip(sizes, resident)
+    ] + [
         column_block(rows, wide),
         column_block(rows, HD),
         column_block(rows, HD),
@@ -295,7 +316,8 @@
     elements = rows * slots * steps * GROUP
     return pl.pallas_call(
         functools.partial(
-            forward_kernel, len(near), len(parts), keep_row is not None, before is None, norm is not None
+            forward_kernel, len(near), len(parts), keep_row is not None, before is None,
+            norm is not None, kept, resident, len(after),
         ),
         grid=(steps,),
         in_specs=specs,
@@ -308,17 +330,20 @@
     )(*args)
 
 
-def backward_kernel(near, parts, own, later, last, features, *refs):
+def backward_kernel(near, parts, own, later, last, features, added, resident, waits, *refs):
     refs = list(refs)
     take = refs.pop
+    for _ in range(waits):
+        take(0)
     first = later is not None
     q_ref, p_ref = take(0), take(0)
     key_list, value_list, core_ref = read_slots(take, near, parts)
     if first:
         peak_refs = [take(0) for _ in range(later + 1)]
-        inverse_ref, norm_ref, attn_ref, cot_ref, gain_ref = [take(0) for _ in range(5)]
+        inverse_ref, norm_ref, other_ref, attn_ref, cot_ref, gain_ref = [take(0) for _ in range(6)]
     else:
         grad_ref, diag_ref, dq_ref = take(0), take(0), take(0)
+    add_refs = [take(0) for _ in range(added)]
     outs = [take(0) for _ in range(near + parts)]
     dq_out = take(0)
     if first:
@@ -327,14 +352,17 @@
     ds_ref, q_stack, grad_stack = take(0), take(0), take(0)
 
     rows = q_ref.shape[0]
+    base = 0
+    if resident:
+        base = pl.multiple_of(pl.program_id(0) * (GROUP * rows), GROUP * rows)
     lanes = lane_of((rows, HD))
     if first:
         inverse_total = inverse_ref[...]
         factors = [inverse_total] + [
             jnp.exp2((r[...] - peak_refs[0][...]) * EXPONENT) * inverse_total for r in peak_refs[1:]
         ]
-        squares = norm_ref[0:1, :]
-        crossed = norm_ref[1:2, :]
+        squares = norm_ref[0:1, :] + other_ref[0:1, :]
+        crossed = norm_ref[1:2, :] + other_ref[1:2, :]
         inverse_row = lax.rsqrt(squares / features + NORM_EPS)
         coefficient_row = inverse_row * inverse_row * inverse_row * crossed / features
         inverse_wide = jnp.broadcast_to(inverse_row, (HD, rows)).T
@@ -369,7 +397,7 @@
         for k, v in zip(key_list, value_list):
             columns = slice(start, start + k.shape[0])
             d_probs = dot_nt(grad_bf, v)
-            d_scores = (p_ref[stack, columns].astype(F32) * (d_probs - scaled_diag)).astype(BF16)
+            d_scores = (p_ref[pl.ds(base + head * rows, rows), columns].astype(F32) * (d_probs - scaled_diag)).astype(BF16)
             ds_ref[stack, columns] = d_scores
             part = dot_nn(d_scores, k)
             d_query = part if d_query is None else d_query + part
@@ -389,9 +417,13 @@
         columns = slice(start, start + size)
         start += size
         d_key = (dot_tn(q_all, ds_ref[:, columns]) * SCALING).T
-        d_value = dot_tn(grad_all, p_ref[:, columns]).T
+        d_value = dot_tn(grad_all, p_ref[pl.ds(base, GROUP * rows), columns]).T
         if number < near:
             out = outs[number]
+            if own and number == 0:
+                for ref in add_refs:
+                    d_key = d_key + ref[:size, :].astype(F32)
+                    d_value = d_value + ref[size:, :].astype(F32)
             out[:size, :] = d_key.astype(out.dtype)
             out[size:, :] = d_value.astype(out.dtype)
         else:
@@ -410,15 +442,19 @@
 
 def backward_phase(
     name, queries, probs, near, parts=(), core=None, own=False, peaks=None, norm=None,
-    grads=None, last=False,
+    grads=None, last=False, add=(), resident=False,
+    after=(),
 ):
     rows, width = queries.shape
     steps = width // (GROUP * HD)
     wide = GROUP * HD
     slots = probs.shape[1]
     args, specs, _ = slot_operands(near, parts, core)
-    args = [queries, probs] + args
-    specs = [column_block(rows, wide), pl.BlockSpec((GROUP * rows, slots), lambda a: (a, 0))] + specs
+    args = list(after) + [queries, off_chip(probs)] + args
+    specs = [ANYWHERE] * len(after) + [
+        column_block(rows, wide),
+        WHOLE if resident else pl.BlockSpec((GROUP * rows, slots), lambda a: (a, 0)),
+    ] + specs
     out_shapes, out_specs = [], []
     for number, (k, _, row) in enumerate(near):
         size = k.shape[0] if row == 0 else k.shape[0] // 2
@@ -431,10 +467,11 @@
     later = None
     if norm is not None:
         later = len(peaks) - 1
-        inverse, sums, attn, cotangent, gain = norm
-        args += list(peaks) + [inverse, sums, attn, cotangent, gain]
+        inverse, sums, others, attn, cotangent, gain = norm
+        args += list(peaks) + [inverse, sums, others, off_chip(attn), cotangent, gain]
         specs += [column_block(rows, HD)] * (len(peaks) + 1) + [
             fixed_block(sums.shape),
+            fixed_block(others.shape),
             column_block(rows, wide),
             column_block(rows, wide),
             column_block(1, wide),
@@ -442,6 +479,8 @@
     else:
         args += list(grads)
         specs += [column_block(rows, wide), column_block(rows, HD), column_block(rows, wide)]
+    args += list(add)
+    specs += [column_block(x.shape[0], HD) for x in add]
     out_shapes.append(jax.ShapeDtypeStruct((rows, width), BF16 if last else F32))
     out_specs.append(column_block(rows, wide))
     if norm is not None:
@@ -455,7 +494,10 @@
             out_specs += [column_block(rows, wide), column_block(rows, HD)]
     elements = rows * slots * steps * GROUP
     return pl.pallas_call(
-        functools.partial(backward_kernel, len(near), len(parts), own, later, last, QH * HD),
+        functools.partial(
+            backward_kernel, len(near), len(parts), own, later, last, QH * HD, len(add), resident,
+            len(after),
+        ),
         grid=(steps,),
         in_specs=specs,
         out_specs=out_specs,
@@ -471,7 +513,8 @@
     )(*args)
 
 
-def pick_kernel(core_ref, spots_ref, own_ref, partner_ref, out_ref):
+def pick_kernel(core_ref, spots_ref, own_ref, partner_ref, *refs):
+    out_refs = refs[2:]
     rows = own_ref.shape[0] // 2
     count = spots_ref.shape[1]
     first = core_ref[0] == 0
@@ -482,20 +525,99 @@
         chosen = jnp.where(row_ids == spots_ref[number : number + 1, :], 1.0, 0.0).astype(BF16)
         part = dot_tn(chosen, source)
         total = part if total is None else total + part
-    out_ref[...] = total.astype(BF16)
-
-
-def pick(core, spots, own, partner):
-    shape = (spots.shape[1], own.shape[1])
+    write_pieces(total, out_refs)
+
+
+def write_pieces(total, out_refs):
+    start = 0
+    for ref in out_refs:
+        ref[...] = total[start : start + ref.shape[0]].astype(ref.dtype)
+        start += ref.shape[0]
+
+
+def piece_shapes(count, rows, width):
+    return [jax.ShapeDtypeStruct((rows // count, width), BF16)] * count
+
+
+def pick(core, spots, own, partner, pieces):
+    count, width = spots.shape[1], own.shape[1]
     return pl.pallas_call(
         pick_kernel,
-        in_specs=[SCALAR] + [WHOLE] * 3,
+        in_specs=[SCALAR] + [WHOLE] * 3 + [ANYWHERE],
+        out_specs=[ANYWHERE] + [WHOLE] * pieces,
+        out_shape=[jax.ShapeDtypeStruct(own.shape, own.dtype)] + piece_shapes(pieces, count, width),
+        input_output_aliases={4: 0},
+        compiler_params=params(),
+        cost_estimate=cost(2 * count * width * own.shape[0], 3 * 2**20),
+        name="pick_globals",
+    )(core, spots, own, partner, own)
+
+
+def combine_kernel(waits, blocks, *refs):
+    blocks_in = refs[waits : waits + blocks]
+    running = blocks_in[0][...].astype(F32)
+    for ref in blocks_in[1:]:
+        running = running + ref[...].astype(F32)
+    write_pieces(running, refs[waits + blocks :])
+
+
+def combine(blocks, pieces, after=()):
+    rows, width = blocks[0].shape
+    return pl.pallas_call(
+        functools.partial(combine_kernel, len(after), len(blocks)),
+        in_specs=[ANYWHERE] * len(after) + [WHOLE] * len(blocks),
+        out_specs=[WHOLE] * pieces,
+        out_shape=piece_shapes(pieces, rows, width),
+        compiler_params=params(),
+        cost_estimate=cost(2**20, len(blocks) * rows * width * 4),
+        name="combine_globals",
+    )(*after, *blocks)
+
+
+def join_kernel(waits, blocks, *refs):
+    out_ref = refs[-1]
+    start = 0
+    for ref in refs[waits : waits + blocks]:
+        out_ref[start : start + ref.shape[0], :] = ref[...]
+        start += ref.shape[0]
+
+
+def join(blocks, after=()):
+    rows = sum(x.shape[0] for x in blocks)
+    width = blocks[0].shape[1]
+    return pl.pallas_call(
+        functools.partial(join_kernel, len(after), len(blocks)),
+        in_specs=[ANYWHERE] * len(after) + [WHOLE] * len(blocks),
         out_specs=WHOLE,
-        out_shape=jax.ShapeDtypeStruct(shape, BF16),
+        out_shape=jax.ShapeDtypeStruct((rows, width), BF16),
         compiler_params=params(),
-        cost_estimate=cost(2 * shape[0] * shape[1] * own.shape[0], 3 * 2**20),
-        name="pick_globals",
-    )(core, spots, own, partner)
+        cost_estimate=cost(2**20, rows * width * 4),
+        name="join_globals",
+    )(*after, *blocks)
+
+
+def settle_kernel(waits, *refs):
+    own_ref, far_keys_ref, far_values_ref = refs[waits : waits + 3]
+    refs = refs[waits + 3 : -3] + refs[-2:-1]
+    rows = far_keys_ref.shape[0]
+    for here, far_ref in ((slice(0, rows), far_keys_ref), (slice(rows, 2 * rows), far_values_ref)):
+        running = own_ref[here, :] + far_ref[...].astype(F32)
+        for ref in refs[:-1]:
+            running = running + ref[here, :].astype(F32)
+        refs[-1][here, :] = running
+
+
+def settle(own, back, far_keys, far_values, through, after=()):
+    return pl.pallas_call(
+        functools.partial(settle_kernel, len(after)),
+        in_specs=[ANYWHERE] * len(after) + [WHOLE] * (3 + len(back)) + [ANYWHERE],
+        out_specs=[WHOLE, ANYWHERE],
+        out_shape=[jax.ShapeDtypeStruct(x.shape, x.dtype) for x in (own, through)],
+        input_output_aliases={len(after) + 3 + len(back): 1},
+        compiler_params=params(),
+        cost_estimate=cost(2**20, 4 * 2**20),
+        name="settle_partner_grads",
+    )(*after, own, far_keys, far_values, *back, through)
 
 
 def finish_kernel(partners, parts, *refs):
@@ -547,33 +669,12 @@
     ]
 
 
-def reduce_level(block, masks):
-    size = block.shape[0] // len(masks)
-    running = block[:size].astype(F32)
-    for number, mask in enumerate(masks):
-        if number:
-            moved = swap(block[number * size : (number + 1) * size], "seq", mask)
-            running = running + moved.astype(F32)
-    return running.astype(BF16)
-
-
-def gather_level(block, masks):
-    return [block if mask == 0 else swap(block, "seq", mask) for mask in masks]
-
-
-def gather_parts(block, levels):
-    mine = [block]
-    for masks in reversed(levels):
-        block = mine[0] if len(mine) == 1 else jnp.concatenate(mine, 0)
-        mine = gather_level(block, masks)
-    return mine + [swap(part, "seq", 1) for part in mine]
-
-
-def reduce_parts(blocks, masks):
-    running = blocks[0].astype(F32)
-    for part, mask in zip(blocks[1:], masks[1:]):
-        running = running + swap(part, "seq", mask).astype(F32)
-    return running.astype(BF16)
+def exchange(blocks, masks):
+    return [blocks[0]] + [swap(x, "seq", mask) for x, mask in zip(blocks[1:], masks[1:])]
+
+
+def spread(block, masks):
+    return [block] + [swap(block, "seq", mask) for mask in masks[1:]]
 
 
 def per_device(queries, keys, values, key_keep, global_positions, gain, cotangent):
@@ -584,9 +685,10 @@
     global_count = global_positions.shape[0]
     keep_row = key_keep.reshape(1, rows)
     gain_row = gain.reshape(1, -1)
+    queries, cotangent = off_chip(queries), off_chip(cotangent)
 
     packed = prepare(keep_row, keys, values)
-    near = [swap(packed, "seq", 1 << bit) for bit in range(bit_count)]
+    near = [swap(packed, "seq", 1)]
 
     levels = [masks_of(level) for level in levels_of(bit_count)]
     order = [0]
@@ -599,43 +701,63 @@
     ordered = jnp.sum(jnp.where(match[:, :, None], chunks[None], 0), 1).reshape(global_count)
     spots = jnp.stack([ordered - place * rows, ordered - (place ^ 1) * rows])
 
-    picked = pick(core, spots, packed, near[0])
-    for masks in levels:
-        picked = reduce_level(picked, masks)
-    global_parts = gather_parts(picked, levels)
-
-    group_a = [(keys, values, 0)] + [(x, x, 1) for x in near[:-1]]
-    group_b = [(x, x, 1) for x in near[-1:]]
-    p_a, *state = forward_phase("forward_a", queries, group_a, keep_row=keep_row)
-    peak_a = state[1]
-    p_b, attn, peak_b, inverse, sums = forward_phase(
-        "forward_b", queries, group_b, global_parts, core, before=state, norm=(cotangent, gain_row)
+    outer, inner = levels
+    packed, *picked = pick(core, spots, packed, near[0], len(outer))
+    moved = exchange(picked, outer)
+    near += [swap(packed, "seq", 1 << bit) for bit in range(1, bit_count)]
+
+    group_1 = [(off_chip(keys), off_chip(values), 0), (near[0], near[0], 1)]
+    group_2 = [(x, x, 1) for x in near[1:-1]]
+    group_3 = [(near[-1], near[-1], 1)]
+
+    p_1, *state_1 = forward_phase("forward_own", queries, group_1, keep_row=keep_row, after=picked[-1:])
+    summed = combine(moved, len(inner), after=state_1[2:])
+    moved = exchange(summed, inner)
+    p_2, *state_2 = forward_phase(
+        "forward_partners", queries, group_2, before=state_1, after=summed[-1:]
+    )
+    (piece,) = combine(moved, 1, after=state_2[2:])
+    half = join(spread(piece, inner))
+    mine = spread(half, outer)
+    global_parts = mine + [swap(part, "seq", 1) for part in mine]
+    p_3, attn, peak_3, inverse, sums = forward_phase(
+        "forward_globals", queries, group_3, global_parts, core, before=state_2,
+        norm=(cotangent, gain_row),
     )
     head_bits = lax.axis_size("head").bit_length() - 1
+    others = jnp.zeros_like(sums)
     for bit in range(head_bits):
-        sums = sums + swap(sums, "head", 1 << bit)
-
-    back_b, *rest = backward_phase(
-        "backward_b", queries, p_b, group_b, global_parts, core, peaks=[peak_b, peak_a],
-        norm=(inverse, sums, attn, cotangent, gain_row),
+        sums = sums + others if bit else sums
+        others = swap(sums, "head", 1 << bit)
+
+    count = len(global_parts)
+    back_3, *rest = backward_phase(
+        "backward_globals", queries, p_3, group_3, global_parts, core,
+        peaks=[peak_3, state_2[1], state_1[1]], norm=(inverse, sums, others, attn, cotangent, gain_row),
     )
-    part_count = len(global_parts)
-    global_grads, (d_query, normed, grad_a, diag_a) = rest[:part_count], rest[part_count:]
-    half = part_count // 2
-    reduced = [
-        (a.astype(F32) + swap(b, "seq", 1).astype(F32)).astype(BF16)
-        for a, b in zip(global_grads[:half], global_grads[half:])
-    ]
-    total = reduce_parts(reduced, levels[0]) if levels else reduced[0]
-    for masks in levels[1:]:
-        total = reduce_level(total, masks)
-    total_parts = gather_parts(total, levels)
-
-    own, *back_a, d_query = backward_phase(
-        "backward_a", queries, p_a, group_a, own=True, grads=(grad_a, diag_a, d_query), last=True
+    global_grads, (d_query, normed, grad_2, diag_2, grad_1, diag_1) = rest[:count], rest[count:]
+    kept, given = global_grads[: count // 2], global_grads[count // 2 :]
+    reduced = [combine([a, swap(b, "seq", 1)], 1)[0] for a, b in zip(kept, given)]
+    summed = combine(exchange(reduced, outer), len(inner))
+    moved = exchange(summed, inner)
+    far_mask = 1 << (bit_count - 1)
+    far_keys = swap(back_3[:rows], "seq", far_mask)
+    *back_2, d_query = backward_phase(
+        "backward_partners", queries, p_2, group_2, grads=(grad_2, diag_2, d_query), after=summed[-1:]
     )
-    back = [swap(x, "seq", 1 << bit) for bit, x in enumerate(back_a + [back_b])]
-    key_grad, value_grad = finish(core, spots, own, back, total_parts)
+    (piece,) = combine(moved, 1, after=[d_query])
+    moved = spread(piece, inner)
+    half = join(moved)
+    mine = spread(half, outer)
+    far_values = swap(back_3[rows:], "seq", far_mask)
+    own, back_first, d_query = backward_phase(
+        "backward_own", queries, p_1, group_1, own=True, grads=(grad_1, diag_1, d_query), last=True,
+        after=[half, far_keys],
+    )
+    back_2 = [swap(x, "seq", 2 << number) for number, x in enumerate(back_2)]
+    own, back_first = settle(own, back_2, far_keys, far_values, back_first, after=mine[1:])
+    total_parts = mine + [swap(part, "seq", 1) for part in mine]
+    key_grad, value_grad = finish(core, spots, own, [swap(back_first, "seq", 1)], total_parts)
     return normed, d_query, key_grad, value_grad
 
 

time: 207 us -> 183 us (0.88)
  waiting for transfers between devices: 50.3 us -> 22.4 us
  Pallas kernels: 106 us -> 118 us
  other arithmetic: 5.71 us -> 0.84 us
  local copies, waits for them, and re-layouts: 6.67 us -> 4.25 us
    ppermute x31 -> x32, waiting for transfers between devices: 50.3 us -> 22.4 us  [swap(): return lax.ppermute(block, axis, [(i, i ^ mask) for i in range(count)])]
    pallas_call x2 -> x3, Pallas kernels: 57.2 us -> 70.1 us  [forward_phase(): pl.pallas_call(functools.partial(forward_kernel, len(near), len(parts), k...]
    pallas_call x2 -> x3, Pallas kernels: 41.7 us -> 45.2 us  [backward_phase(): pl.pallas_call(functools.partial(backward_kernel, len(near), len(parts),...]
    convert_element_type x5 -> x0, other arithmetic: 3.01 us -> none  [the longest x3 1.04 us: reduce_level(): return running.astype(BF16)]
    pallas_call x1, Pallas kernels: 3.28 us -> 1.16 us  [finish(): pl.pallas_call(functools.partial(finish_kernel, len(back), len(total)), i...]
    unnamed x36 -> x11, local copies, waits for them, and re-layouts: 4.17 us -> 3.29 us
    ppermute x31 -> x32, starting transfers between devices: 36.4 us -> 37.2 us  [swap(): return lax.ppermute(block, axis, [(i, i ^ mask) for i in range(count)])]
  transfers between devices with their start and end apart: 31 -> 32, of which waited for: 14 -> 12; matrix products, arithmetic and copies ran while one was open for 2% -> 1% of each run, Pallas kernels for 25% -> 36%
where the time goes in v3:
time: 183 us
  Pallas kernels  118 us (64%)
  starting transfers between devices  37.2 us (20%)
  waiting for transfers between devices  22.4 us (12%)
  local copies, waits for them, and re-layouts  4.25 us (2%)
    pallas_call x3, Pallas kernels, forward_phase(): pl.pallas_call(functools.partial(forward_kernel, len(near), len(parts), k...  70.1 us
    pallas_call x3, Pallas kernels, backward_phase(): pl.pallas_call(functools.partial(backward_kernel, len(near), len(parts),...  45.2 us
    ppermute x32, starting transfers between devices, swap(): return lax.ppermute(block, axis, [(i, i ^ mask) for i in range(count)])  37.2 us
    ppermute x32, waiting for transfers between devices, swap(): return lax.ppermute(block, axis, [(i, i ^ mask) for i in range(count)])  22.4 us
  transfers between devices with their start and end apart: 32, of which 12 were waited for; matrix products, arithmetic and copies ran while one was open for 1% of the time, Pallas kernels for 36%

profile of v3, /device:TPU:0, one launch (start us, length us, event | category | flops | bytes accessed | tf_op | source)
XLA Modules:
  0.0 183.0 jit_solution(1768628121773708686)
XLA Ops:
  0.6 0.0 copy-start
  0.6 0.9 copy-done
  1.6 0.9 copy-done.1
  2.5 0.7 copy-done.2
  3.2 0.1 prepare_keys_values.1.own_ref
  3.3 0.5 collective-permute-start
  3.9 0.7 broadcast_xor_fusion
  4.5 0.1 iota_compare_fusion
  4.6 0.8 broadcast_in_dim.26
  5.4 0.1 select_reduce_fusion
  5.5 0.1 sub.34
  5.6 0.1 sub.37
  5.7 0.0 collective-permute-done.partner_ref.refs_4_.refs_5_.refs_6_.refs_7_
  5.7 0.4 pick_globals.1
  6.1 2.7 %collective-permute-start.4 = (bf16[512,512]{1,0:T(8,128)(2,1)S(1)}, bf16[512,512]{1,0:T(8,128)(2,1)S(1)}, u32[]{:S(2)}, u32[]{:S(2)}) collective-permute-start(bf16[512,512]{1,0:T(8,128)(2,1)S(1)} %get-tuple-element.49), channel_id=1, source_target_pairs={{0,8},{2,10},{4,12},{6,14},{8,0},{10,2},{12,4},{14,6},{16,24},{18,... | collective-permute-start | bytes 1572872 | tf_op jit(solution)/shard_map/ppermute | solution.py:46
  8.8 1.5 collective-permute-start.3
  10.3 2.6 %collective-permute-start.1 = (bf16[512,512]{1,0:T(8,128)(2,1)S(1)}, bf16[512,512]{1,0:T(8,128)(2,1)S(1)}, u32[]{:S(2)}, u32[]{:S(2)}) collective-permute-start(bf16[512,512]{1,0:T(8,128)(2,1)S(1)} %get-tuple-element.49), channel_id=1, source_target_pairs={{0,16},{2,18},{4,20},{6,22},{8,24},{10,26},{12,28},{14,30},{16,0},... | collective-permute-start | bytes 1572872 | tf_op jit(solution)/shard_map/ppermute | solution.py:46
  12.9 0.5 collective-permute-start.2
  13.4 0.7 copy-done.3
  14.1 15.7 %forward_own.1 = (bf16[8192,512]{1,0:T(8,128)(2,1)}, f32[256,4096]{1,0:T(8,128)S(1)}, f32[256,512]{1,0:T(8,128)S(1)}, f32[256,512]{1,0:T(8,128)S(1)}) custom-call(bf16[192,512]{1,0:T(8,128)(2,1)S(1)} %get-tuple-element.50.refs_0_, bf16[256,4096]{1,0:T(8,128)(2,1)} %refs_2_.3, bf16[256,512]{1,0:T(8,128)(2,1)} %refs_4_.1, bf16[256,512]{1,0:T(8,128)(2,1)} %refs_5_.1, ...), custom_call_target="tpu_custom_call" | custom-call | flops 4294967296 | bytes 8388608 | tf_op jit(solution)/shard_map/forward_own/pallas_call | solution.py:317
  29.8 0.0 collective-permute-done.2.refs_2_
  29.9 0.5 collective-permute-start.5
  30.4 0.0 collective-permute-start.6
  30.4 0.8 collective-permute-done.4.refs_4_.refs_5_.refs_6_
  31.3 3.1 %collective-permute-start.7 = (bf16[48,512]{1,0:T(8,128)(2,1)S(1)}, bf16[48,512]{1,0:T(8,128)(2,1)S(1)}, u32[]{:S(2)}, u32[]{:S(2)}) collective-permute-start(bf16[48,512]{1,0:T(8,128)(2,1)S(1)} %get-tuple-element.53.refs_0_), channel_id=1, source_target_pairs={{0,24},{2,26},{4,28},{6,30},{8,16},{10,18},{12,20},{14,22},{16,8},... | collective-permute-start | bytes 147464 | tf_op jit(solution)/shard_map/ppermute | solution.py:46
  34.4 24.4 %forward_partners.1 = (bf16[8192,512]{1,0:T(8,128)(2,1)}, f32[256,4096]{1,0:T(8,128)S(1)}, f32[256,512]{1,0:T(8,128)S(1)}, f32[256,512]{1,0:T(8,128)S(1)}) custom-call(bf16[48,512]{1,0:T(8,128)(2,1)S(1)} %get-tuple-element.53.refs_0_, bf16[256,4096]{1,0:T(8,128)(2,1)} %refs_2_.3, bf16[512,512]{1,0:T(8,128)(2,1)S(1)} %collective-permute-done.3.refs_2_.refs_3_.refs_4_, ...), custom_call_target="tpu_custom_call" | custom-call | flops 4294967296 | bytes 8388608 | tf_op jit(solution)/shard_map/forward_partners/pallas_call | solution.py:317
  58.8 0.8 collective-permute-start.10
  59.6 0.3 collective-permute-start.9
  59.9 3.4 %collective-permute-start.8 = (bf16[48,512]{1,0:T(8,128)(2,1)S(1)}, bf16[48,512]{1,0:T(8,128)(2,1)S(1)}, u32[]{:S(2)}, u32[]{:S(2)}) collective-permute-start(bf16[48,512]{1,0:T(8,128)(2,1)S(1)} %combine_globals.7.refs_0_), channel_id=1, source_target_pairs={{0,8},{2,10},{4,12},{6,14},{8,0},{10,2},{12,4},{14,6},{16,24},{18,... | collective-permute-start | bytes 147464 | tf_op jit(solution)/shard_map/ppermute | solution.py:46
  63.3 1.6 collective-permute-done.10.refs_3_
  64.9 0.8 collective-permute-done.9.refs_2_
  65.7 2.7 %collective-permute-start.11 = (bf16[192,512]{1,0:T(8,128)(2,1)S(1)}, bf16[192,512]{1,0:T(8,128)(2,1)S(1)}, u32[]{:S(2)}, u32[]{:S(2)}) collective-permute-start(bf16[192,512]{1,0:T(8,128)(2,1)S(1)} %join_globals.2.refs_4_.refs_5_), channel_id=1, source_target_pairs={{0,4},{2,6},{4,0},{6,2},{8,12},{10,14},{12,8},{14,10},{16,20},{18,... | collective-permute-start | bytes 589832 | tf_op jit(solution)/shard_map/ppermute | solution.py:46
  68.4 3.6 %collective-permute-done.11.refs_5_.refs_6_ = bf16[192,512]{1,0:T(8,128)(2,1)S(1)} collective-permute-done((bf16[192,512]{1,0:T(8,128)(2,1)S(1)}, bf16[192,512]{1,0:T(8,128)(2,1)S(1)}, u32[]{:S(2)}, u32[]{:S(2)}) %collective-permute-start.11) | collective-permute-done | bytes 196640 | tf_op jit(solution)/shard_map/ppermute | solution.py:46
  72.1 1.4 collective-permute-done.13.refs_7_.refs_8_
  73.5 30.0 %forward_globals.1 = (bf16[8192,640]{1,0:T(8,128)(2,1)}, f32[256,4096]{1,0:T(8,128)}, f32[256,512]{1,0:T(8,128)S(1)}, f32[256,512]{1,0:T(8,128)S(1)}, f32[2,256]{1,0:T(2,128)S(1)}) custom-call(bf16[256,4096]{1,0:T(8,128)(2,1)} %refs_2_.3, bf16[512,512]{1,0:T(8,128)(2,1)S(1)} %collective-permute-done.1.refs_1_.refs_2_.refs_3_, ...), custom_call_target="tpu_custom_call" | custom-call | flops 5368709120 | bytes 10485760 | tf_op jit(solution)/shard_map/forward_globals/pallas_call | solution.py:317
  103.5 1.5 collective-permute-start.14
  105.0 2.1 %collective-permute-done.14.refs_14_ = f32[2,256]{1,0:T(2,128)S(1)} collective-permute-done((f32[2,256]{1,0:T(2,128)S(1)}, f32[2,256]{1,0:T(2,128)S(1)}, u32[]{:S(2)}, u32[]{:S(2)}) %collective-permute-start.14) | collective-permute-done | bytes 2080 | tf_op jit(solution)/shard_map/ppermute | solution.py:46
  107.1 19.3 %backward_globals.1 = (bf16[512,512]{1,0:T(8,128)(2,1)S(1)}, bf16[192,512]{1,0:T(8,128)(2,1)S(1)}, bf16[192,512]{1,0:T(8,128)(2,1)S(1)}, bf16[192,512]{1,0:T(8,1...) custom-call(bf16[256,4096]{1,0:T(8,128)(2,1)} %refs_2_.3, ...), custom_call_target="tpu_custom_call" | custom-call | flops 8053063680 | bytes 10485760 | tf_op jit(solution)/shard_map/backward_globals/pallas_call | solution.py:496
  126.3 0.5 collective-permute-start.15
  126.8 0.9 collective-permute-done.16.refs_1_
  127.8 0.1 combine_globals.9
  127.8 2.1 %collective-permute-start.17 = (bf16[192,512]{1,0:T(8,128)(2,1)S(1)}, bf16[192,512]{1,0:T(8,128)(2,1)S(1)}, u32[]{:S(2)}, u32[]{:S(2)}) collective-permute-start(bf16[192,512]{1,0:T(8,128)(2,1)S(1)} %combine_globals.9), channel_id=1, source_target_pairs={{0,4},{2,6},{4,0},{6,2},{8,12},{10,14},{12,8},{14,10},{16,20},{18,... | collective-permute-start | bytes 589832 | tf_op jit(solution)/shard_map/ppermute | solution.py:46
  130.0 1.4 collective-permute-start.24
  131.4 3.7 %collective-permute-done.17.refs_1_ = bf16[192,512]{1,0:T(8,128)(2,1)S(1)} collective-permute-done((bf16[192,512]{1,0:T(8,128)(2,1)S(1)}, bf16[192,512]{1,0:T(8,128)(2,1)S(1)}, u32[]{:S(2)}, u32[]{:S(2)}) %collective-permute-start.17) | collective-permute-done | bytes 196640 | tf_op jit(solution)/shard_map/ppermute | solution.py:46
  135.2 1.6 collective-permute-start.18
  136.7 0.9 collective-permute-start.19
  137.6 2.0 %collective-permute-start.20 = (bf16[48,512]{1,0:T(8,128)(2,1)S(1)}, bf16[48,512]{1,0:T(8,128)(2,1)S(1)}, u32[]{:S(2)}, u32[]{:S(2)}) collective-permute-start(bf16[48,512]{1,0:T(8,128)(2,1)S(1)} %get-tuple-element.72.refs_0_), channel_id=1, source_target_pairs={{0,24},{2,26},{4,28},{6,30},{8,16},{10,18},{12,20},{14,22},{16,8},... | collective-permute-start | bytes 147464 | tf_op jit(solution)/shard_map/ppermute | solution.py:46
  139.6 12.7 %backward_partners.1 = (bf16[512,512]{1,0:T(8,128)(2,1)S(1)}, bf16[512,512]{1,0:T(8,128)(2,1)S(1)}, f32[256,4096]{1,0:T(8,128)S(1)}) custom-call(bf16[48,512]{1,0:T(8,128)(2,1)S(1)} %get-tuple-element.72.refs_0_, bf16[256,4096]{1,0:T(8,128)(2,1)} %refs_2_.3, bf16[8192,512]{1,0:T(8,128)(2,1)} %get-tuple-element.73.refs_2_, ...), custom_call_target="tpu_custom_call" | custom-call | flops 6442450944 | bytes 8388608 | tf_op jit(solution)/shard_map/backward_partners/pallas_call | solution.py:496
  152.4 1.9 %collective-permute-start.23 = (bf16[48,512]{1,0:T(8,128)(2,1)S(1)}, bf16[48,512]{1,0:T(8,128)(2,1)S(1)}, u32[]{:S(2)}, u32[]{:S(2)}) collective-permute-start(bf16[48,512]{1,0:T(8,128)(2,1)S(1)} %combine_globals.11.refs_0_), channel_id=1, source_target_pairs={{0,24},{2,26},{4,28},{6,30},{8,16},{10,18},{12,20},{14,22},{16,8},... | collective-permute-start | bytes 147464 | tf_op jit(solution)/shard_map/ppermute | solution.py:46
  154.3 0.2 collective-permute-start.22
  154.5 2.3 %collective-permute-start.21 = (bf16[48,512]{1,0:T(8,128)(2,1)S(1)}, bf16[48,512]{1,0:T(8,128)(2,1)S(1)}, u32[]{:S(2)}, u32[]{:S(2)}) collective-permute-start(bf16[48,512]{1,0:T(8,128)(2,1)S(1)} %combine_globals.11.refs_0_), channel_id=1, source_target_pairs={{0,8},{2,10},{4,12},{6,14},{8,0},{10,2},{12,4},{14,6},{16,24},{18,... | collective-permute-start | bytes 147464 | tf_op jit(solution)/shard_map/ppermute | solution.py:46
  156.8 0.4 collective-permute-start.26
  157.2 1.6 collective-permute-done.23.refs_3_
  158.8 1.9 %collective-permute-start.27 = (bf16[512,512]{1,0:T(8,128)(2,1)S(1)}, bf16[512,512]{1,0:T(8,128)(2,1)S(1)}, u32[]{:S(2)}, u32[]{:S(2)}) collective-permute-start(bf16[512,512]{1,0:T(8,128)(2,1)S(1)} %get-tuple-element.87), channel_id=1, source_target_pairs={{0,4},{2,6},{4,0},{6,2},{8,12},{10,14},{12,8},{14,10},{16,20},{18,... | collective-permute-start | bytes 1572872 | tf_op jit(solution)/shard_map/ppermute | solution.py:46
  160.7 3.9 %collective-permute-done.22.refs_2_ = bf16[48,512]{1,0:T(8,128)(2,1)S(1)} collective-permute-done((bf16[48,512]{1,0:T(8,128)(2,1)S(1)}, bf16[48,512]{1,0:T(8,128)(2,1)S(1)}, u32[]{:S(2)}, u32[]{:S(2)}) %collective-permute-start.22) | collective-permute-done | bytes 49184 | tf_op jit(solution)/shard_map/ppermute | solution.py:46
  164.6 1.2 collective-permute-start.25
  165.8 13.3 %backward_own.1 = (f32[512,512]{1,0:T(8,128)S(1)}, bf16[512,512]{1,0:T(8,128)(2,1)S(1)}, bf16[256,4096]{1,0:T(8,128)(2,1)}) custom-call(bf16[192,512]{1,0:T(8,128)(2,1)S(1)} %join_globals.3.refs_0_.refs_4_, bf16[256,512]{1,0:T(8,128)(2,1)S(1)} %collective-permute-done.24.refs_1_.refs_2_, bf16[256,4096]{1,0:T(8,128)(2,1)} %refs_2_.3, ...), custom_call_target="tpu_custom_call" | custom-call | flops 6442450944 | bytes 8388608 | tf_op jit(solution)/shard_map/backward_own/pallas_call | solution.py:496
  179.1 0.2 settle_partner_grads.1
  179.3 0.1 collective-permute-start.29
  179.4 0.5 collective-permute-start.30
  179.9 0.1 collective-permute-start.31
  180.0 1.6 collective-permute-done.30.refs_6_
  181.6 0.3 collective-permute-done.31.refs_7_
  181.9 1.2 finish_key_value_grads.1
  (39 shorter events, 0.4 us)
Async XLA Ops:
  0.6 1.0 copy-start
  1.6 0.9 copy-start.1
  2.5 0.7 copy-start.2
  3.3 2.3 %collective-permute-start = (bf16[512,512]{1,0:T(8,128)(2,1)S(1)}, bf16[512,512]{1,0:T(8,128)(2,1)S(1)}, u32[]{:S(2)}, u32[]{:S(2)}) collective-permute-start(bf16[512,512]{1,0:T(8,128)(2,1)S(1)} %prepare_keys_values.1.own_ref), channel_id=1, source_target_pairs={{0,2},{2,0},{4,6},{6,4},{8,10},{10,8},{12,14},{14,12},{16,18},{18,... | collective-permute-start | bytes 1572872 | tf_op jit(solution)/shard_map/ppermute | solution.py:46
  6.1 25.1 %collective-permute-start.4 = (bf16[512,512]{1,0:T(8,128)(2,1)S(1)}, bf16[512,512]{1,0:T(8,128)(2,1)S(1)}, u32[]{:S(2)}, u32[]{:S(2)}) collective-permute-start(bf16[512,512]{1,0:T(8,128)(2,1)S(1)} %get-tuple-element.49), channel_id=1, source_target_pairs={{0,8},{2,10},{4,12},{6,14},{8,0},{10,2},{12,4},{14,6},{16,24},{18,... | collective-permute-start | bytes 1572872 | tf_op jit(solution)/shard_map/ppermute | solution.py:46
  8.8 25.5 %collective-permute-start.3 = (bf16[512,512]{1,0:T(8,128)(2,1)S(1)}, bf16[512,512]{1,0:T(8,128)(2,1)S(1)}, u32[]{:S(2)}, u32[]{:S(2)}) collective-permute-start(bf16[512,512]{1,0:T(8,128)(2,1)S(1)} %get-tuple-element.49), channel_id=1, source_target_pairs={{0,4},{2,6},{4,0},{6,2},{8,12},{10,14},{12,8},{14,10},{16,20},{18,... | collective-permute-start | bytes 1572872 | tf_op jit(solution)/shard_map/ppermute | solution.py:46
  10.3 61.8 %collective-permute-start.1 = (bf16[512,512]{1,0:T(8,128)(2,1)S(1)}, bf16[512,512]{1,0:T(8,128)(2,1)S(1)}, u32[]{:S(2)}, u32[]{:S(2)}) collective-permute-start(bf16[512,512]{1,0:T(8,128)(2,1)S(1)} %get-tuple-element.49), channel_id=1, source_target_pairs={{0,16},{2,18},{4,20},{6,22},{8,24},{10,26},{12,28},{14,30},{16,0},... | collective-permute-start | bytes 1572872 | tf_op jit(solution)/shard_map/ppermute | solution.py:46
  12.9 16.9 %collective-permute-start.2 = (bf16[192,512]{1,0:T(8,128)(2,1)S(1)}, bf16[192,512]{1,0:T(8,128)(2,1)S(1)}, u32[]{:S(2)}, u32[]{:S(2)}) collective-permute-start(bf16[192,512]{1,0:T(8,128)(2,1)S(1)} %get-tuple-element.50.refs_0_), channel_id=1, source_target_pairs={{0,4},{2,6},{4,0},{6,2},{8,12},{10,14},{12,8},{14,10},{16,20},{18,... | collective-permute-start | bytes 589832 | tf_op jit(solution)/shard_map/ppermute | solution.py:46
  13.4 0.7 copy-start.3
  29.9 28.9 %collective-permute-start.5 = (bf16[48,512]{1,0:T(8,128)(2,1)S(1)}, bf16[48,512]{1,0:T(8,128)(2,1)S(1)}, u32[]{:S(2)}, u32[]{:S(2)}) collective-permute-start(bf16[48,512]{1,0:T(8,128)(2,1)S(1)} %get-tuple-element.58), channel_id=1, source_target_pairs={{0,8},{2,10},{4,12},{6,14},{8,0},{10,2},{12,4},{14,6},{16,24},{18,... | collective-permute-start | bytes 147464 | tf_op jit(solution)/shard_map/ppermute | solution.py:46
  30.4 28.4 %collective-permute-start.6 = (bf16[48,512]{1,0:T(8,128)(2,1)S(1)}, bf16[48,512]{1,0:T(8,128)(2,1)S(1)}, u32[]{:S(2)}, u32[]{:S(2)}) collective-permute-start(bf16[48,512]{1,0:T(8,128)(2,1)S(1)} %get-tuple-element.59), channel_id=1, source_target_pairs={{0,16},{2,18},{4,20},{6,22},{8,24},{10,26},{12,28},{14,30},{16,0},... | collective-permute-start | bytes 147464 | tf_op jit(solution)/shard_map/ppermute | solution.py:46
  31.3 27.5 %collective-permute-start.7 = (bf16[48,512]{1,0:T(8,128)(2,1)S(1)}, bf16[48,512]{1,0:T(8,128)(2,1)S(1)}, u32[]{:S(2)}, u32[]{:S(2)}) collective-permute-start(bf16[48,512]{1,0:T(8,128)(2,1)S(1)} %get-tuple-element.53.refs_0_), channel_id=1, source_target_pairs={{0,24},{2,26},{4,28},{6,30},{8,16},{10,18},{12,20},{14,22},{16,8},... | collective-permute-start | bytes 147464 | tf_op jit(solution)/shard_map/ppermute | solution.py:46
  34.4 37.7 %copy-start.4 = (bf16[4096]{0:T(1024)(128)(2,1)S(1)}, bf16[4096]{0:T(1024)(128)(2,1)}, u32[]{:S(2)}) copy-start(bf16[4096]{0:T(1024)(128)(2,1)} %param.13) | copy-start | bytes 24580
  58.8 6.1 %collective-permute-start.10 = (bf16[48,512]{1,0:T(8,128)(2,1)S(1)}, bf16[48,512]{1,0:T(8,128)(2,1)S(1)}, u32[]{:S(2)}, u32[]{:S(2)}) collective-permute-start(bf16[48,512]{1,0:T(8,128)(2,1)S(1)} %combine_globals.7.refs_0_), channel_id=1, source_target_pairs={{0,24},{2,26},{4,28},{6,30},{8,16},{10,18},{12,20},{14,22},{16,8},... | collective-permute-start | bytes 147464 | tf_op jit(solution)/shard_map/ppermute | solution.py:46
  59.6 6.0 %collective-permute-start.9 = (bf16[48,512]{1,0:T(8,128)(2,1)S(1)}, bf16[48,512]{1,0:T(8,128)(2,1)S(1)}, u32[]{:S(2)}, u32[]{:S(2)}) collective-permute-start(bf16[48,512]{1,0:T(8,128)(2,1)S(1)} %combine_globals.7.refs_0_), channel_id=1, source_target_pairs={{0,16},{2,18},{4,20},{6,22},{8,24},{10,26},{12,28},{14,30},{16,0},... | collective-permute-start | bytes 147464 | tf_op jit(solution)/shard_map/ppermute | solution.py:46
  59.9 5.8 %collective-permute-start.8 = (bf16[48,512]{1,0:T(8,128)(2,1)S(1)}, bf16[48,512]{1,0:T(8,128)(2,1)S(1)}, u32[]{:S(2)}, u32[]{:S(2)}) collective-permute-start(bf16[48,512]{1,0:T(8,128)(2,1)S(1)} %combine_globals.7.refs_0_), channel_id=1, source_target_pairs={{0,8},{2,10},{4,12},{6,14},{8,0},{10,2},{12,4},{14,6},{16,24},{18,... | collective-permute-start | bytes 147464 | tf_op jit(solution)/shard_map/ppermute | solution.py:46
  65.7 6.4 %collective-permute-start.11 = (bf16[192,512]{1,0:T(8,128)(2,1)S(1)}, bf16[192,512]{1,0:T(8,128)(2,1)S(1)}, u32[]{:S(2)}, u32[]{:S(2)}) collective-permute-start(bf16[192,512]{1,0:T(8,128)(2,1)S(1)} %join_globals.2.refs_4_.refs_5_), channel_id=1, source_target_pairs={{0,4},{2,6},{4,0},{6,2},{8,12},{10,14},{12,8},{14,10},{16,20},{18,... | collective-permute-start | bytes 589832 | tf_op jit(solution)/shard_map/ppermute | solution.py:46
  68.4 3.7 %collective-permute-start.12 = (bf16[192,512]{1,0:T(8,128)(2,1)S(1)}, bf16[192,512]{1,0:T(8,128)(2,1)S(1)}, u32[]{:S(2)}, u32[]{:S(2)}) collective-permute-start(bf16[192,512]{1,0:T(8,128)(2,1)S(1)} %join_globals.2.refs_4_.refs_5_), channel_id=1, source_target_pairs={{0,2},{2,0},{4,6},{6,4},{8,10},{10,8},{12,14},{14,12},{16,18},{18,... | collective-permute-start | bytes 589832 | tf_op jit(solution)/shard_map/ppermute | solution.py:46
  72.1 1.4 collective-permute-start.13
  103.5 3.6 %collective-permute-start.14 = (f32[2,256]{1,0:T(2,128)S(1)}, f32[2,256]{1,0:T(2,128)S(1)}, u32[]{:S(2)}, u32[]{:S(2)}) collective-permute-start(f32[2,256]{1,0:T(2,128)S(1)} %get-tuple-element.65.refs_13_), channel_id=1, source_target_pairs={{0,1},{1,0},{2,3},{3,2},{4,5},{5,4},{6,7},{7,6},{8,9},{9,8},{10,11... | collective-permute-start | bytes 6152 | tf_op jit(solution)/shard_map/ppermute | solution.py:46
  126.3 1.4 collective-permute-start.16
  126.3 5.0 %collective-permute-start.15 = (bf16[192,512]{1,0:T(8,128)(2,1)S(1)}, bf16[192,512]{1,0:T(8,128)(2,1)S(1)}, u32[]{:S(2)}, u32[]{:S(2)}) collective-permute-start(bf16[192,512]{1,0:T(8,128)(2,1)S(1)} %get-tuple-element.69), channel_id=1, source_target_pairs={{0,2},{2,0},{4,6},{6,4},{8,10},{10,8},{12,14},{14,12},{16,18},{18,... | collective-permute-start | bytes 589832 | tf_op jit(solution)/shard_map/ppermute | solution.py:46
  127.8 7.3 %collective-permute-start.17 = (bf16[192,512]{1,0:T(8,128)(2,1)S(1)}, bf16[192,512]{1,0:T(8,128)(2,1)S(1)}, u32[]{:S(2)}, u32[]{:S(2)}) collective-permute-start(bf16[192,512]{1,0:T(8,128)(2,1)S(1)} %combine_globals.9), channel_id=1, source_target_pairs={{0,4},{2,6},{4,0},{6,2},{8,12},{10,14},{12,8},{14,10},{16,20},{18,... | collective-permute-start | bytes 589832 | tf_op jit(solution)/shard_map/ppermute | solution.py:46
  130.0 35.9 %collective-permute-start.24 = (bf16[256,512]{1,0:T(8,128)(2,1)S(1)}, bf16[256,512]{1,0:T(8,128)(2,1)S(1)}, u32[]{:S(2)}, u32[]{:S(2)}) collective-permute-start(bf16[256,512]{1,0:T(8,128)(2,1)S(1)} %get-tuple-element.95), channel_id=1, source_target_pairs={{0,16},{2,18},{4,20},{6,22},{8,24},{10,26},{12,28},{14,30},{16,0},... | collective-permute-start | bytes 786440 | tf_op jit(solution)/shard_map/ppermute | solution.py:46
  135.2 17.1 %collective-permute-start.18 = (bf16[48,512]{1,0:T(8,128)(2,1)S(1)}, bf16[48,512]{1,0:T(8,128)(2,1)S(1)}, u32[]{:S(2)}, u32[]{:S(2)}) collective-permute-start(bf16[48,512]{1,0:T(8,128)(2,1)S(1)} %get-tuple-element.79), channel_id=1, source_target_pairs={{0,8},{2,10},{4,12},{6,14},{8,0},{10,2},{12,4},{14,6},{16,24},{18,... | collective-permute-start | bytes 147464 | tf_op jit(solution)/shard_map/ppermute | solution.py:46
  136.7 15.6 %collective-permute-start.19 = (bf16[48,512]{1,0:T(8,128)(2,1)S(1)}, bf16[48,512]{1,0:T(8,128)(2,1)S(1)}, u32[]{:S(2)}, u32[]{:S(2)}) collective-permute-start(bf16[48,512]{1,0:T(8,128)(2,1)S(1)} %get-tuple-element.80), channel_id=1, source_target_pairs={{0,16},{2,18},{4,20},{6,22},{8,24},{10,26},{12,28},{14,30},{16,0},... | collective-permute-start | bytes 147464 | tf_op jit(solution)/shard_map/ppermute | solution.py:46
  137.6 14.7 %collective-permute-start.20 = (bf16[48,512]{1,0:T(8,128)(2,1)S(1)}, bf16[48,512]{1,0:T(8,128)(2,1)S(1)}, u32[]{:S(2)}, u32[]{:S(2)}) collective-permute-start(bf16[48,512]{1,0:T(8,128)(2,1)S(1)} %get-tuple-element.72.refs_0_), channel_id=1, source_target_pairs={{0,24},{2,26},{4,28},{6,30},{8,16},{10,18},{12,20},{14,22},{16,8},... | collective-permute-start | bytes 147464 | tf_op jit(solution)/shard_map/ppermute | solution.py:46
  152.4 6.4 %collective-permute-start.23 = (bf16[48,512]{1,0:T(8,128)(2,1)S(1)}, bf16[48,512]{1,0:T(8,128)(2,1)S(1)}, u32[]{:S(2)}, u32[]{:S(2)}) collective-permute-start(bf16[48,512]{1,0:T(8,128)(2,1)S(1)} %combine_globals.11.refs_0_), channel_id=1, source_target_pairs={{0,24},{2,26},{4,28},{6,30},{8,16},{10,18},{12,20},{14,22},{16,8},... | collective-permute-start | bytes 147464 | tf_op jit(solution)/shard_map/ppermute | solution.py:46
  154.3 10.3 %collective-permute-start.22 = (bf16[48,512]{1,0:T(8,128)(2,1)S(1)}, bf16[48,512]{1,0:T(8,128)(2,1)S(1)}, u32[]{:S(2)}, u32[]{:S(2)}) collective-permute-start(bf16[48,512]{1,0:T(8,128)(2,1)S(1)} %combine_globals.11.refs_0_), channel_id=1, source_target_pairs={{0,16},{2,18},{4,20},{6,22},{8,24},{10,26},{12,28},{14,30},{16,0},... | collective-permute-start | bytes 147464 | tf_op jit(solution)/shard_map/ppermute | solution.py:46
  154.5 10.1 %collective-permute-start.21 = (bf16[48,512]{1,0:T(8,128)(2,1)S(1)}, bf16[48,512]{1,0:T(8,128)(2,1)S(1)}, u32[]{:S(2)}, u32[]{:S(2)}) collective-permute-start(bf16[48,512]{1,0:T(8,128)(2,1)S(1)} %combine_globals.11.refs_0_), channel_id=1, source_target_pairs={{0,8},{2,10},{4,12},{6,14},{8,0},{10,2},{12,4},{14,6},{16,24},{18,... | collective-permute-start | bytes 147464 | tf_op jit(solution)/shard_map/ppermute | solution.py:46
  156.8 22.2 %collective-permute-start.26 = (bf16[256,512]{1,0:T(8,128)(2,1)S(1)}, bf16[256,512]{1,0:T(8,128)(2,1)S(1)}, u32[]{:S(2)}, u32[]{:S(2)}) collective-permute-start(bf16[256,512]{1,0:T(8,128)(2,1)S(1)} %get-tuple-element.94), channel_id=1, source_target_pairs={{0,16},{2,18},{4,20},{6,22},{8,24},{10,26},{12,28},{14,30},{16,0},... | collective-permute-start | bytes 786440 | tf_op jit(solution)/shard_map/ppermute | solution.py:46
  158.8 20.3 %collective-permute-start.27 = (bf16[512,512]{1,0:T(8,128)(2,1)S(1)}, bf16[512,512]{1,0:T(8,128)(2,1)S(1)}, u32[]{:S(2)}, u32[]{:S(2)}) collective-permute-start(bf16[512,512]{1,0:T(8,128)(2,1)S(1)} %get-tuple-element.87), channel_id=1, source_target_pairs={{0,4},{2,6},{4,0},{6,2},{8,12},{10,14},{12,8},{14,10},{16,20},{18,... | collective-permute-start | bytes 1572872 | tf_op jit(solution)/shard_map/ppermute | solution.py:46
  164.6 14.5 %collective-permute-start.28 = (bf16[512,512]{1,0:T(8,128)(2,1)S(1)}, bf16[512,512]{1,0:T(8,128)(2,1)S(1)}, u32[]{:S(2)}, u32[]{:S(2)}) collective-permute-start(bf16[512,512]{1,0:T(8,128)(2,1)S(1)} %get-tuple-element.88), channel_id=1, source_target_pairs={{0,8},{2,10},{4,12},{6,14},{8,0},{10,2},{12,4},{14,6},{16,24},{18,... | collective-permute-start | bytes 1572872 | tf_op jit(solution)/shard_map/ppermute | solution.py:46
  164.6 14.5 %collective-permute-start.25 = (bf16[192,512]{1,0:T(8,128)(2,1)S(1)}, bf16[192,512]{1,0:T(8,128)(2,1)S(1)}, u32[]{:S(2)}, u32[]{:S(2)}) collective-permute-start(bf16[192,512]{1,0:T(8,128)(2,1)S(1)} %join_globals.3.refs_0_.refs_4_), channel_id=1, source_target_pairs={{0,4},{2,6},{4,0},{6,2},{8,12},{10,14},{12,8},{14,10},{16,20},{18,... | collective-permute-start | bytes 589832 | tf_op jit(solution)/shard_map/ppermute | solution.py:46
  179.3 2.5 %collective-permute-start.29 = (bf16[512,512]{1,0:T(8,128)(2,1)S(1)}, bf16[512,512]{1,0:T(8,128)(2,1)S(1)}, u32[]{:S(2)}, u32[]{:S(2)}) collective-permute-start(bf16[512,512]{1,0:T(8,128)(2,1)S(1)} %get-tuple-element.91), channel_id=1, source_target_pairs={{0,2},{2,0},{4,6},{6,4},{8,10},{10,8},{12,14},{14,12},{16,18},{18,... | collective-permute-start | bytes 1572872 | tf_op jit(solution)/shard_map/ppermute | solution.py:46
  179.4 2.2 %collective-permute-start.30 = (bf16[192,512]{1,0:T(8,128)(2,1)S(1)}, bf16[192,512]{1,0:T(8,128)(2,1)S(1)}, u32[]{:S(2)}, u32[]{:S(2)}) collective-permute-start(bf16[192,512]{1,0:T(8,128)(2,1)S(1)} %join_globals.3.refs_0_.refs_4_), channel_id=1, source_target_pairs={{0,2},{2,0},{4,6},{6,4},{8,10},{10,8},{12,14},{14,12},{16,18},{18,... | collective-permute-start | bytes 589832 | tf_op jit(solution)/shard_map/ppermute | solution.py:46
  179.9 2.0 %collective-permute-start.31 = (bf16[192,512]{1,0:T(8,128)(2,1)S(1)}, bf16[192,512]{1,0:T(8,128)(2,1)S(1)}, u32[]{:S(2)}, u32[]{:S(2)}) collective-permute-start(bf16[192,512]{1,0:T(8,128)(2,1)S(1)} %collective-permute-done.25.refs_0_.refs_5_), channel_id=1, source_target_pairs={{0,2},{2,0},{4,6},{6,4},{8,10},{10,8},{12,14},{14,12},{16,18},{18,... | collective-permute-start | bytes 589832 | tf_op jit(solution)/shard_map/ppermute | solution.py:46

commit v4 on v3

--- a/solution.py
+++ b/solution.py
@@ -125,13 +125,14 @@
     rows, width = keys.shape
     return pl.pallas_call(
         prepare_kernel,
-        in_specs=[WHOLE] * 3,
+        grid=(1,),
+        in_specs=[fixed_block(x.shape) for x in (keep_row, keys, values)],
         out_specs=WHOLE,
         out_shape=jax.ShapeDtypeStruct((2 * rows, width), BF16),
         compiler_params=params(),
         cost_estimate=cost(2**20, 4 * rows * width * 2),
         name="prepare_keys_values",
-    )(keep_row, keys, values)
+    )(off_chip(keep_row), off_chip(keys), off_chip(values))
 
 
 def forward_kernel(near, parts, own, first, last, kept, resident, waits, *refs):

time: 183 us -> 182 us (level)
  local copies, waits for them, and re-layouts: 4.25 us -> 1.68 us
    unnamed x11 -> x5, local copies, waits for them, and re-layouts: 3.29 us -> 0.72 us
  transfers between devices with their start and end apart: 32 -> 32, of which waited for: 12 -> 12; matrix products, arithmetic and copies ran while one was open for 1% -> 1% of each run, Pallas kernels for 36% -> 37%
where the time goes in v4:
time: 182 us
  Pallas kernels  119 us (65%)
  starting transfers between devices  37.1 us (20%)
  waiting for transfers between devices  22.4 us (12%)
    pallas_call x3, Pallas kernels, forward_phase(): pl.pallas_call(functools.partial(forward_kernel, len(near), len(parts), k...  70.2 us
    pallas_call x3, Pallas kernels, backward_phase(): pl.pallas_call(functools.partial(backward_kernel, len(near), len(parts),...  45.2 us
    ppermute x32, starting transfers between devices, swap(): return lax.ppermute(block, axis, [(i, i ^ mask) for i in range(count)])  37.1 us
    ppermute x32, waiting for transfers between devices, swap(): return lax.ppermute(block, axis, [(i, i ^ mask) for i in range(count)])  22.4 us
  transfers between devices with their start and end apart: 32, of which 12 were waited for; matrix products, arithmetic and copies ran while one was open for 1% of the time, Pallas kernels for 37%

profile of v4, /device:TPU:0, one launch (start us, length us, event | category | flops | bytes accessed | tf_op | source)
XLA Modules:
  0.0 181.5 jit_solution(8732976874824164189)
XLA Ops:
  0.6 1.2 prepare_keys_values.1.own_ref
  1.8 0.5 collective-permute-start
  2.3 0.7 broadcast_xor_fusion
  3.0 0.1 iota_compare_fusion
  3.1 0.8 broadcast_in_dim.26
  3.9 0.1 select_reduce_fusion
  4.0 0.1 sub.34
  4.1 0.1 sub.37
  4.2 0.0 collective-permute-done.partner_ref.refs_4_.refs_5_.refs_6_.refs_7_
  4.2 0.4 pick_globals.1
  4.6 2.7 %collective-permute-start.4 = (bf16[512,512]{1,0:T(8,128)(2,1)S(1)}, bf16[512,512]{1,0:T(8,128)(2,1)S(1)}, u32[]{:S(2)}, u32[]{:S(2)}) collective-permute-start(bf16[512,512]{1,0:T(8,128)(2,1)S(1)} %get-tuple-element.49), channel_id=1, source_target_pairs={{0,8},{2,10},{4,12},{6,14},{8,0},{10,2},{12,4},{14,6},{16,24},{18,... | collective-permute-start | bytes 1572872 | tf_op jit(solution)/shard_map/ppermute | solution.py:46
  7.3 1.5 collective-permute-start.3
  8.8 2.6 %collective-permute-start.1 = (bf16[512,512]{1,0:T(8,128)(2,1)S(1)}, bf16[512,512]{1,0:T(8,128)(2,1)S(1)}, u32[]{:S(2)}, u32[]{:S(2)}) collective-permute-start(bf16[512,512]{1,0:T(8,128)(2,1)S(1)} %get-tuple-element.49), channel_id=1, source_target_pairs={{0,16},{2,18},{4,20},{6,22},{8,24},{10,26},{12,28},{14,30},{16,0},... | collective-permute-start | bytes 1572872 | tf_op jit(solution)/shard_map/ppermute | solution.py:46
  11.4 0.5 collective-permute-start.2
  11.9 0.7 copy-done
  12.6 15.8 %forward_own.1 = (bf16[8192,512]{1,0:T(8,128)(2,1)}, f32[256,4096]{1,0:T(8,128)S(1)}, f32[256,512]{1,0:T(8,128)S(1)}, f32[256,512]{1,0:T(8,128)S(1)}) custom-call(bf16[192,512]{1,0:T(8,128)(2,1)S(1)} %get-tuple-element.50.refs_0_, bf16[256,4096]{1,0:T(8,128)(2,1)} %refs_2_.3, bf16[256,512]{1,0:T(8,128)(2,1)} %refs_4_.1, bf16[256,512]{1,0:T(8,128)(2,1)} %refs_5_.1, ...), custom_call_target="tpu_custom_call" | custom-call | flops 4294967296 | bytes 8388608 | tf_op jit(solution)/shard_map/forward_own/pallas_call | solution.py:318
  28.3 0.0 collective-permute-done.2.refs_2_
  28.4 0.5 collective-permute-start.5
  28.9 0.8 collective-permute-done.4.refs_4_.refs_5_.refs_6_
  29.7 3.1 %collective-permute-start.7 = (bf16[48,512]{1,0:T(8,128)(2,1)S(1)}, bf16[48,512]{1,0:T(8,128)(2,1)S(1)}, u32[]{:S(2)}, u32[]{:S(2)}) collective-permute-start(bf16[48,512]{1,0:T(8,128)(2,1)S(1)} %get-tuple-element.53.refs_0_), channel_id=1, source_target_pairs={{0,24},{2,26},{4,28},{6,30},{8,16},{10,18},{12,20},{14,22},{16,8},... | collective-permute-start | bytes 147464 | tf_op jit(solution)/shard_map/ppermute | solution.py:46
  32.9 0.0 collective-permute-done.3.refs_2_.refs_3_.refs_4_
  32.9 24.4 %forward_partners.1 = (bf16[8192,512]{1,0:T(8,128)(2,1)}, f32[256,4096]{1,0:T(8,128)S(1)}, f32[256,512]{1,0:T(8,128)S(1)}, f32[256,512]{1,0:T(8,128)S(1)}) custom-call(bf16[48,512]{1,0:T(8,128)(2,1)S(1)} %get-tuple-element.53.refs_0_, bf16[256,4096]{1,0:T(8,128)(2,1)} %refs_2_.3, bf16[512,512]{1,0:T(8,128)(2,1)S(1)} %collective-permute-done.3.refs_2_.refs_3_.refs_4_, ...), custom_call_target="tpu_custom_call" | custom-call | flops 4294967296 | bytes 8388608 | tf_op jit(solution)/shard_map/forward_partners/pallas_call | solution.py:318
  57.3 0.0 collective-permute-done.6.refs_3_
  57.3 0.0 collective-permute-done.7.refs_4_
  57.4 0.7 collective-permute-start.10
  58.1 0.3 collective-permute-start.9
  58.4 3.4 %collective-permute-start.8 = (bf16[48,512]{1,0:T(8,128)(2,1)S(1)}, bf16[48,512]{1,0:T(8,128)(2,1)S(1)}, u32[]{:S(2)}, u32[]{:S(2)}) collective-permute-start(bf16[48,512]{1,0:T(8,128)(2,1)S(1)} %combine_globals.7.refs_0_), channel_id=1, source_target_pairs={{0,8},{2,10},{4,12},{6,14},{8,0},{10,2},{12,4},{14,6},{16,24},{18,... | collective-permute-start | bytes 147464 | tf_op jit(solution)/shard_map/ppermute | solution.py:46
  61.8 1.6 collective-permute-done.10.refs_3_
  63.4 0.7 collective-permute-done.9.refs_2_
  64.2 2.7 %collective-permute-start.11 = (bf16[192,512]{1,0:T(8,128)(2,1)S(1)}, bf16[192,512]{1,0:T(8,128)(2,1)S(1)}, u32[]{:S(2)}, u32[]{:S(2)}) collective-permute-start(bf16[192,512]{1,0:T(8,128)(2,1)S(1)} %join_globals.2.refs_4_.refs_5_), channel_id=1, source_target_pairs={{0,4},{2,6},{4,0},{6,2},{8,12},{10,14},{12,8},{14,10},{16,20},{18,... | collective-permute-start | bytes 589832 | tf_op jit(solution)/shard_map/ppermute | solution.py:46
  66.9 0.0 collective-permute-start.12
  66.9 3.6 %collective-permute-done.11.refs_5_.refs_6_ = bf16[192,512]{1,0:T(8,128)(2,1)S(1)} collective-permute-done((bf16[192,512]{1,0:T(8,128)(2,1)S(1)}, bf16[192,512]{1,0:T(8,128)(2,1)S(1)}, u32[]{:S(2)}, u32[]{:S(2)}) %collective-permute-start.11) | collective-permute-done | bytes 196640 | tf_op jit(solution)/shard_map/ppermute | solution.py:46
  70.5 0.0 collective-permute-start.13
  70.6 1.4 collective-permute-done.13.refs_7_.refs_8_
  72.0 30.0 %forward_globals.1 = (bf16[8192,640]{1,0:T(8,128)(2,1)}, f32[256,4096]{1,0:T(8,128)}, f32[256,512]{1,0:T(8,128)S(1)}, f32[256,512]{1,0:T(8,128)S(1)}, f32[2,256]{1,0:T(2,128)S(1)}) custom-call(bf16[256,4096]{1,0:T(8,128)(2,1)} %refs_2_.3, bf16[512,512]{1,0:T(8,128)(2,1)S(1)} %collective-permute-done.1.refs_1_.refs_2_.refs_3_, ...), custom_call_target="tpu_custom_call" | custom-call | flops 5368709120 | bytes 10485760 | tf_op jit(solution)/shard_map/forward_globals/pallas_call | solution.py:318
  102.0 1.5 collective-permute-start.14
  103.5 2.1 %collective-permute-done.14.refs_14_ = f32[2,256]{1,0:T(2,128)S(1)} collective-permute-done((f32[2,256]{1,0:T(2,128)S(1)}, f32[2,256]{1,0:T(2,128)S(1)}, u32[]{:S(2)}, u32[]{:S(2)}) %collective-permute-start.14) | collective-permute-done | bytes 2080 | tf_op jit(solution)/shard_map/ppermute | solution.py:46
  105.6 19.3 %backward_globals.1 = (bf16[512,512]{1,0:T(8,128)(2,1)S(1)}, bf16[192,512]{1,0:T(8,128)(2,1)S(1)}, bf16[192,512]{1,0:T(8,128)(2,1)S(1)}, bf16[192,512]{1,0:T(8,1...) custom-call(bf16[256,4096]{1,0:T(8,128)(2,1)} %refs_2_.3, ...), custom_call_target="tpu_custom_call" | custom-call | flops 8053063680 | bytes 10485760 | tf_op jit(solution)/shard_map/backward_globals/pallas_call | solution.py:497
  124.8 0.5 collective-permute-start.15
  125.3 0.9 collective-permute-done.16.refs_1_
  126.3 0.1 combine_globals.9
  126.3 2.1 %collective-permute-start.17 = (bf16[192,512]{1,0:T(8,128)(2,1)S(1)}, bf16[192,512]{1,0:T(8,128)(2,1)S(1)}, u32[]{:S(2)}, u32[]{:S(2)}) collective-permute-start(bf16[192,512]{1,0:T(8,128)(2,1)S(1)} %combine_globals.9), channel_id=1, source_target_pairs={{0,4},{2,6},{4,0},{6,2},{8,12},{10,14},{12,8},{14,10},{16,20},{18,... | collective-permute-start | bytes 589832 | tf_op jit(solution)/shard_map/ppermute | solution.py:46
  128.5 1.5 collective-permute-start.24
  130.0 3.7 %collective-permute-done.17.refs_1_ = bf16[192,512]{1,0:T(8,128)(2,1)S(1)} collective-permute-done((bf16[192,512]{1,0:T(8,128)(2,1)S(1)}, bf16[192,512]{1,0:T(8,128)(2,1)S(1)}, u32[]{:S(2)}, u32[]{:S(2)}) %collective-permute-start.17) | collective-permute-done | bytes 196640 | tf_op jit(solution)/shard_map/ppermute | solution.py:46
  133.7 1.6 collective-permute-start.18
  135.2 0.9 collective-permute-start.19
  136.2 2.0 %collective-permute-start.20 = (bf16[48,512]{1,0:T(8,128)(2,1)S(1)}, bf16[48,512]{1,0:T(8,128)(2,1)S(1)}, u32[]{:S(2)}, u32[]{:S(2)}) collective-permute-start(bf16[48,512]{1,0:T(8,128)(2,1)S(1)} %get-tuple-element.72.refs_0_), channel_id=1, source_target_pairs={{0,24},{2,26},{4,28},{6,30},{8,16},{10,18},{12,20},{14,22},{16,8},... | collective-permute-start | bytes 147464 | tf_op jit(solution)/shard_map/ppermute | solution.py:46
  138.1 12.7 %backward_partners.1 = (bf16[512,512]{1,0:T(8,128)(2,1)S(1)}, bf16[512,512]{1,0:T(8,128)(2,1)S(1)}, f32[256,4096]{1,0:T(8,128)S(1)}) custom-call(bf16[48,512]{1,0:T(8,128)(2,1)S(1)} %get-tuple-element.72.refs_0_, bf16[256,4096]{1,0:T(8,128)(2,1)} %refs_2_.3, bf16[8192,512]{1,0:T(8,128)(2,1)} %get-tuple-element.73.refs_2_, ...), custom_call_target="tpu_custom_call" | custom-call | flops 6442450944 | bytes 8388608 | tf_op jit(solution)/shard_map/backward_partners/pallas_call | solution.py:497
  150.9 1.9 %collective-permute-start.23 = (bf16[48,512]{1,0:T(8,128)(2,1)S(1)}, bf16[48,512]{1,0:T(8,128)(2,1)S(1)}, u32[]{:S(2)}, u32[]{:S(2)}) collective-permute-start(bf16[48,512]{1,0:T(8,128)(2,1)S(1)} %combine_globals.11.refs_0_), channel_id=1, source_target_pairs={{0,24},{2,26},{4,28},{6,30},{8,16},{10,18},{12,20},{14,22},{16,8},... | collective-permute-start | bytes 147464 | tf_op jit(solution)/shard_map/ppermute | solution.py:46
  152.8 0.2 collective-permute-start.22
  153.0 2.3 %collective-permute-start.21 = (bf16[48,512]{1,0:T(8,128)(2,1)S(1)}, bf16[48,512]{1,0:T(8,128)(2,1)S(1)}, u32[]{:S(2)}, u32[]{:S(2)}) collective-permute-start(bf16[48,512]{1,0:T(8,128)(2,1)S(1)} %combine_globals.11.refs_0_), channel_id=1, source_target_pairs={{0,8},{2,10},{4,12},{6,14},{8,0},{10,2},{12,4},{14,6},{16,24},{18,... | collective-permute-start | bytes 147464 | tf_op jit(solution)/shard_map/ppermute | solution.py:46
  155.4 0.4 collective-permute-start.26
  155.7 1.7 collective-permute-done.23.refs_3_
  157.4 1.7 collective-permute-start.27
  159.2 3.9 %collective-permute-done.22.refs_2_ = bf16[48,512]{1,0:T(8,128)(2,1)S(1)} collective-permute-done((bf16[48,512]{1,0:T(8,128)(2,1)S(1)}, bf16[48,512]{1,0:T(8,128)(2,1)S(1)}, u32[]{:S(2)}, u32[]{:S(2)}) %collective-permute-start.22) | collective-permute-done | bytes 49184 | tf_op jit(solution)/shard_map/ppermute | solution.py:46
  163.1 1.2 collective-permute-start.25
  164.3 13.2 %backward_own.1 = (f32[512,512]{1,0:T(8,128)S(1)}, bf16[512,512]{1,0:T(8,128)(2,1)S(1)}, bf16[256,4096]{1,0:T(8,128)(2,1)}) custom-call(bf16[192,512]{1,0:T(8,128)(2,1)S(1)} %join_globals.3.refs_0_.refs_4_, bf16[256,512]{1,0:T(8,128)(2,1)S(1)} %collective-permute-done.24.refs_1_.refs_2_, bf16[256,4096]{1,0:T(8,128)(2,1)} %refs_2_.3, ...), custom_call_target="tpu_custom_call" | custom-call | flops 6442450944 | bytes 8388608 | tf_op jit(solution)/shard_map/backward_own/pallas_call | solution.py:497
  177.6 0.2 settle_partner_grads.1
  177.8 0.1 collective-permute-start.29
  177.9 0.5 collective-permute-start.30
  178.4 0.1 collective-permute-start.31
  178.5 1.6 collective-permute-done.30.refs_6_
  180.1 0.3 collective-permute-done.31.refs_7_
  180.4 1.2 finish_key_value_grads.1
  (33 shorter events, 0.4 us)
Async XLA Ops:
  1.8 2.3 %collective-permute-start = (bf16[512,512]{1,0:T(8,128)(2,1)S(1)}, bf16[512,512]{1,0:T(8,128)(2,1)S(1)}, u32[]{:S(2)}, u32[]{:S(2)}) collective-permute-start(bf16[512,512]{1,0:T(8,128)(2,1)S(1)} %prepare_keys_values.1.own_ref), channel_id=1, source_target_pairs={{0,2},{2,0},{4,6},{6,4},{8,10},{10,8},{12,14},{14,12},{16,18},{18,... | collective-permute-start | bytes 1572872 | tf_op jit(solution)/shard_map/ppermute | solution.py:46
  4.6 25.1 %collective-permute-start.4 = (bf16[512,512]{1,0:T(8,128)(2,1)S(1)}, bf16[512,512]{1,0:T(8,128)(2,1)S(1)}, u32[]{:S(2)}, u32[]{:S(2)}) collective-permute-start(bf16[512,512]{1,0:T(8,128)(2,1)S(1)} %get-tuple-element.49), channel_id=1, source_target_pairs={{0,8},{2,10},{4,12},{6,14},{8,0},{10,2},{12,4},{14,6},{16,24},{18,... | collective-permute-start | bytes 1572872 | tf_op jit(solution)/shard_map/ppermute | solution.py:46
  7.3 25.6 %collective-permute-start.3 = (bf16[512,512]{1,0:T(8,128)(2,1)S(1)}, bf16[512,512]{1,0:T(8,128)(2,1)S(1)}, u32[]{:S(2)}, u32[]{:S(2)}) collective-permute-start(bf16[512,512]{1,0:T(8,128)(2,1)S(1)} %get-tuple-element.49), channel_id=1, source_target_pairs={{0,4},{2,6},{4,0},{6,2},{8,12},{10,14},{12,8},{14,10},{16,20},{18,... | collective-permute-start | bytes 1572872 | tf_op jit(solution)/shard_map/ppermute | solution.py:46
  8.8 61.8 %collective-permute-start.1 = (bf16[512,512]{1,0:T(8,128)(2,1)S(1)}, bf16[512,512]{1,0:T(8,128)(2,1)S(1)}, u32[]{:S(2)}, u32[]{:S(2)}) collective-permute-start(bf16[512,512]{1,0:T(8,128)(2,1)S(1)} %get-tuple-element.49), channel_id=1, source_target_pairs={{0,16},{2,18},{4,20},{6,22},{8,24},{10,26},{12,28},{14,30},{16,0},... | collective-permute-start | bytes 1572872 | tf_op jit(solution)/shard_map/ppermute | solution.py:46
  11.4 17.0 %collective-permute-start.2 = (bf16[192,512]{1,0:T(8,128)(2,1)S(1)}, bf16[192,512]{1,0:T(8,128)(2,1)S(1)}, u32[]{:S(2)}, u32[]{:S(2)}) collective-permute-start(bf16[192,512]{1,0:T(8,128)(2,1)S(1)} %get-tuple-element.50.refs_0_), channel_id=1, source_target_pairs={{0,4},{2,6},{4,0},{6,2},{8,12},{10,14},{12,8},{14,10},{16,20},{18,... | collective-permute-start | bytes 589832 | tf_op jit(solution)/shard_map/ppermute | solution.py:46
  11.9 0.7 copy-start
  28.4 28.9 %collective-permute-start.5 = (bf16[48,512]{1,0:T(8,128)(2,1)S(1)}, bf16[48,512]{1,0:T(8,128)(2,1)S(1)}, u32[]{:S(2)}, u32[]{:S(2)}) collective-permute-start(bf16[48,512]{1,0:T(8,128)(2,1)S(1)} %get-tuple-element.58), channel_id=1, source_target_pairs={{0,8},{2,10},{4,12},{6,14},{8,0},{10,2},{12,4},{14,6},{16,24},{18,... | collective-permute-start | bytes 147464 | tf_op jit(solution)/shard_map/ppermute | solution.py:46
  28.9 28.4 %collective-permute-start.6 = (bf16[48,512]{1,0:T(8,128)(2,1)S(1)}, bf16[48,512]{1,0:T(8,128)(2,1)S(1)}, u32[]{:S(2)}, u32[]{:S(2)}) collective-permute-start(bf16[48,512]{1,0:T(8,128)(2,1)S(1)} %get-tuple-element.59), channel_id=1, source_target_pairs={{0,16},{2,18},{4,20},{6,22},{8,24},{10,26},{12,28},{14,30},{16,0},... | collective-permute-start | bytes 147464 | tf_op jit(solution)/shard_map/ppermute | solution.py:46
  29.7 27.6 %collective-permute-start.7 = (bf16[48,512]{1,0:T(8,128)(2,1)S(1)}, bf16[48,512]{1,0:T(8,128)(2,1)S(1)}, u32[]{:S(2)}, u32[]{:S(2)}) collective-permute-start(bf16[48,512]{1,0:T(8,128)(2,1)S(1)} %get-tuple-element.53.refs_0_), channel_id=1, source_target_pairs={{0,24},{2,26},{4,28},{6,30},{8,16},{10,18},{12,20},{14,22},{16,8},... | collective-permute-start | bytes 147464 | tf_op jit(solution)/shard_map/ppermute | solution.py:46
  32.9 37.7 %copy-start.1 = (bf16[4096]{0:T(1024)(128)(2,1)S(1)}, bf16[4096]{0:T(1024)(128)(2,1)}, u32[]{:S(2)}) copy-start(bf16[4096]{0:T(1024)(128)(2,1)} %param.13) | copy-start | bytes 24580
  57.4 6.1 %collective-permute-start.10 = (bf16[48,512]{1,0:T(8,128)(2,1)S(1)}, bf16[48,512]{1,0:T(8,128)(2,1)S(1)}, u32[]{:S(2)}, u32[]{:S(2)}) collective-permute-start(bf16[48,512]{1,0:T(8,128)(2,1)S(1)} %combine_globals.7.refs_0_), channel_id=1, source_target_pairs={{0,24},{2,26},{4,28},{6,30},{8,16},{10,18},{12,20},{14,22},{16,8},... | collective-permute-start | bytes 147464 | tf_op jit(solution)/shard_map/ppermute | solution.py:46
  58.1 6.0 %collective-permute-start.9 = (bf16[48,512]{1,0:T(8,128)(2,1)S(1)}, bf16[48,512]{1,0:T(8,128)(2,1)S(1)}, u32[]{:S(2)}, u32[]{:S(2)}) collective-permute-start(bf16[48,512]{1,0:T(8,128)(2,1)S(1)} %combine_globals.7.refs_0_), channel_id=1, source_target_pairs={{0,16},{2,18},{4,20},{6,22},{8,24},{10,26},{12,28},{14,30},{16,0},... | collective-permute-start | bytes 147464 | tf_op jit(solution)/shard_map/ppermute | solution.py:46
  58.4 5.7 %collective-permute-start.8 = (bf16[48,512]{1,0:T(8,128)(2,1)S(1)}, bf16[48,512]{1,0:T(8,128)(2,1)S(1)}, u32[]{:S(2)}, u32[]{:S(2)}) collective-permute-start(bf16[48,512]{1,0:T(8,128)(2,1)S(1)} %combine_globals.7.refs_0_), channel_id=1, source_target_pairs={{0,8},{2,10},{4,12},{6,14},{8,0},{10,2},{12,4},{14,6},{16,24},{18,... | collective-permute-start | bytes 147464 | tf_op jit(solution)/shard_map/ppermute | solution.py:46
  64.2 6.4 %collective-permute-start.11 = (bf16[192,512]{1,0:T(8,128)(2,1)S(1)}, bf16[192,512]{1,0:T(8,128)(2,1)S(1)}, u32[]{:S(2)}, u32[]{:S(2)}) collective-permute-start(bf16[192,512]{1,0:T(8,128)(2,1)S(1)} %join_globals.2.refs_4_.refs_5_), channel_id=1, source_target_pairs={{0,4},{2,6},{4,0},{6,2},{8,12},{10,14},{12,8},{14,10},{16,20},{18,... | collective-permute-start | bytes 589832 | tf_op jit(solution)/shard_map/ppermute | solution.py:46
  66.9 3.7 %collective-permute-start.12 = (bf16[192,512]{1,0:T(8,128)(2,1)S(1)}, bf16[192,512]{1,0:T(8,128)(2,1)S(1)}, u32[]{:S(2)}, u32[]{:S(2)}) collective-permute-start(bf16[192,512]{1,0:T(8,128)(2,1)S(1)} %join_globals.2.refs_4_.refs_5_), channel_id=1, source_target_pairs={{0,2},{2,0},{4,6},{6,4},{8,10},{10,8},{12,14},{14,12},{16,18},{18,... | collective-permute-start | bytes 589832 | tf_op jit(solution)/shard_map/ppermute | solution.py:46
  70.5 1.4 collective-permute-start.13
  102.0 3.6 %collective-permute-start.14 = (f32[2,256]{1,0:T(2,128)S(1)}, f32[2,256]{1,0:T(2,128)S(1)}, u32[]{:S(2)}, u32[]{:S(2)}) collective-permute-start(f32[2,256]{1,0:T(2,128)S(1)} %get-tuple-element.65.refs_13_), channel_id=1, source_target_pairs={{0,1},{1,0},{2,3},{3,2},{4,5},{5,4},{6,7},{7,6},{8,9},{9,8},{10,11... | collective-permute-start | bytes 6152 | tf_op jit(solution)/shard_map/ppermute | solution.py:46
  124.8 1.4 collective-permute-start.16
  124.8 5.1 %collective-permute-start.15 = (bf16[192,512]{1,0:T(8,128)(2,1)S(1)}, bf16[192,512]{1,0:T(8,128)(2,1)S(1)}, u32[]{:S(2)}, u32[]{:S(2)}) collective-permute-start(bf16[192,512]{1,0:T(8,128)(2,1)S(1)} %get-tuple-element.69), channel_id=1, source_target_pairs={{0,2},{2,0},{4,6},{6,4},{8,10},{10,8},{12,14},{14,12},{16,18},{18,... | collective-permute-start | bytes 589832 | tf_op jit(solution)/shard_map/ppermute | solution.py:46
  126.3 7.3 %collective-permute-start.17 = (bf16[192,512]{1,0:T(8,128)(2,1)S(1)}, bf16[192,512]{1,0:T(8,128)(2,1)S(1)}, u32[]{:S(2)}, u32[]{:S(2)}) collective-permute-start(bf16[192,512]{1,0:T(8,128)(2,1)S(1)} %combine_globals.9), channel_id=1, source_target_pairs={{0,4},{2,6},{4,0},{6,2},{8,12},{10,14},{12,8},{14,10},{16,20},{18,... | collective-permute-start | bytes 589832 | tf_op jit(solution)/shard_map/ppermute | solution.py:46
  128.5 35.9 %collective-permute-start.24 = (bf16[256,512]{1,0:T(8,128)(2,1)S(1)}, bf16[256,512]{1,0:T(8,128)(2,1)S(1)}, u32[]{:S(2)}, u32[]{:S(2)}) collective-permute-start(bf16[256,512]{1,0:T(8,128)(2,1)S(1)} %get-tuple-element.95), channel_id=1, source_target_pairs={{0,16},{2,18},{4,20},{6,22},{8,24},{10,26},{12,28},{14,30},{16,0},... | collective-permute-start | bytes 786440 | tf_op jit(solution)/shard_map/ppermute | solution.py:46
  133.7 17.1 %collective-permute-start.18 = (bf16[48,512]{1,0:T(8,128)(2,1)S(1)}, bf16[48,512]{1,0:T(8,128)(2,1)S(1)}, u32[]{:S(2)}, u32[]{:S(2)}) collective-permute-start(bf16[48,512]{1,0:T(8,128)(2,1)S(1)} %get-tuple-element.79), channel_id=1, source_target_pairs={{0,8},{2,10},{4,12},{6,14},{8,0},{10,2},{12,4},{14,6},{16,24},{18,... | collective-permute-start | bytes 147464 | tf_op jit(solution)/shard_map/ppermute | solution.py:46
  135.2 15.6 %collective-permute-start.19 = (bf16[48,512]{1,0:T(8,128)(2,1)S(1)}, bf16[48,512]{1,0:T(8,128)(2,1)S(1)}, u32[]{:S(2)}, u32[]{:S(2)}) collective-permute-start(bf16[48,512]{1,0:T(8,128)(2,1)S(1)} %get-tuple-element.80), channel_id=1, source_target_pairs={{0,16},{2,18},{4,20},{6,22},{8,24},{10,26},{12,28},{14,30},{16,0},... | collective-permute-start | bytes 147464 | tf_op jit(solution)/shard_map/ppermute | solution.py:46
  136.2 14.7 %collective-permute-start.20 = (bf16[48,512]{1,0:T(8,128)(2,1)S(1)}, bf16[48,512]{1,0:T(8,128)(2,1)S(1)}, u32[]{:S(2)}, u32[]{:S(2)}) collective-permute-start(bf16[48,512]{1,0:T(8,128)(2,1)S(1)} %get-tuple-element.72.refs_0_), channel_id=1, source_target_pairs={{0,24},{2,26},{4,28},{6,30},{8,16},{10,18},{12,20},{14,22},{16,8},... | collective-permute-start | bytes 147464 | tf_op jit(solution)/shard_map/ppermute | solution.py:46
  150.9 6.5 %collective-permute-start.23 = (bf16[48,512]{1,0:T(8,128)(2,1)S(1)}, bf16[48,512]{1,0:T(8,128)(2,1)S(1)}, u32[]{:S(2)}, u32[]{:S(2)}) collective-permute-start(bf16[48,512]{1,0:T(8,128)(2,1)S(1)} %combine_globals.11.refs_0_), channel_id=1, source_target_pairs={{0,24},{2,26},{4,28},{6,30},{8,16},{10,18},{12,20},{14,22},{16,8},... | collective-permute-start | bytes 147464 | tf_op jit(solution)/shard_map/ppermute | solution.py:46
  152.8 10.3 %collective-permute-start.22 = (bf16[48,512]{1,0:T(8,128)(2,1)S(1)}, bf16[48,512]{1,0:T(8,128)(2,1)S(1)}, u32[]{:S(2)}, u32[]{:S(2)}) collective-permute-start(bf16[48,512]{1,0:T(8,128)(2,1)S(1)} %combine_globals.11.refs_0_), channel_id=1, source_target_pairs={{0,16},{2,18},{4,20},{6,22},{8,24},{10,26},{12,28},{14,30},{16,0},... | collective-permute-start | bytes 147464 | tf_op jit(solution)/shard_map/ppermute | solution.py:46
  153.0 10.1 %collective-permute-start.21 = (bf16[48,512]{1,0:T(8,128)(2,1)S(1)}, bf16[48,512]{1,0:T(8,128)(2,1)S(1)}, u32[]{:S(2)}, u32[]{:S(2)}) collective-permute-start(bf16[48,512]{1,0:T(8,128)(2,1)S(1)} %combine_globals.11.refs_0_), channel_id=1, source_target_pairs={{0,8},{2,10},{4,12},{6,14},{8,0},{10,2},{12,4},{14,6},{16,24},{18,... | collective-permute-start | bytes 147464 | tf_op jit(solution)/shard_map/ppermute | solution.py:46
  155.4 22.2 %collective-permute-start.26 = (bf16[256,512]{1,0:T(8,128)(2,1)S(1)}, bf16[256,512]{1,0:T(8,128)(2,1)S(1)}, u32[]{:S(2)}, u32[]{:S(2)}) collective-permute-start(bf16[256,512]{1,0:T(8,128)(2,1)S(1)} %get-tuple-element.94), channel_id=1, source_target_pairs={{0,16},{2,18},{4,20},{6,22},{8,24},{10,26},{12,28},{14,30},{16,0},... | collective-permute-start | bytes 786440 | tf_op jit(solution)/shard_map/ppermute | solution.py:46
  157.4 20.2 %collective-permute-start.27 = (bf16[512,512]{1,0:T(8,128)(2,1)S(1)}, bf16[512,512]{1,0:T(8,128)(2,1)S(1)}, u32[]{:S(2)}, u32[]{:S(2)}) collective-permute-start(bf16[512,512]{1,0:T(8,128)(2,1)S(1)} %get-tuple-element.87), channel_id=1, source_target_pairs={{0,4},{2,6},{4,0},{6,2},{8,12},{10,14},{12,8},{14,10},{16,20},{18,... | collective-permute-start | bytes 1572872 | tf_op jit(solution)/shard_map/ppermute | solution.py:46
  163.1 14.5 %collective-permute-start.28 = (bf16[512,512]{1,0:T(8,128)(2,1)S(1)}, bf16[512,512]{1,0:T(8,128)(2,1)S(1)}, u32[]{:S(2)}, u32[]{:S(2)}) collective-permute-start(bf16[512,512]{1,0:T(8,128)(2,1)S(1)} %get-tuple-element.88), channel_id=1, source_target_pairs={{0,8},{2,10},{4,12},{6,14},{8,0},{10,2},{12,4},{14,6},{16,24},{18,... | collective-permute-start | bytes 1572872 | tf_op jit(solution)/shard_map/ppermute | solution.py:46
  163.1 14.5 %collective-permute-start.25 = (bf16[192,512]{1,0:T(8,128)(2,1)S(1)}, bf16[192,512]{1,0:T(8,128)(2,1)S(1)}, u32[]{:S(2)}, u32[]{:S(2)}) collective-permute-start(bf16[192,512]{1,0:T(8,128)(2,1)S(1)} %join_globals.3.refs_0_.refs_4_), channel_id=1, source_target_pairs={{0,4},{2,6},{4,0},{6,2},{8,12},{10,14},{12,8},{14,10},{16,20},{18,... | collective-permute-start | bytes 589832 | tf_op jit(solution)/shard_map/ppermute | solution.py:46
  177.8 2.5 %collective-permute-start.29 = (bf16[512,512]{1,0:T(8,128)(2,1)S(1)}, bf16[512,512]{1,0:T(8,128)(2,1)S(1)}, u32[]{:S(2)}, u32[]{:S(2)}) collective-permute-start(bf16[512,512]{1,0:T(8,128)(2,1)S(1)} %get-tuple-element.91), channel_id=1, source_target_pairs={{0,2},{2,0},{4,6},{6,4},{8,10},{10,8},{12,14},{14,12},{16,18},{18,... | collective-permute-start | bytes 1572872 | tf_op jit(solution)/shard_map/ppermute | solution.py:46
  177.9 2.2 %collective-permute-start.30 = (bf16[192,512]{1,0:T(8,128)(2,1)S(1)}, bf16[192,512]{1,0:T(8,128)(2,1)S(1)}, u32[]{:S(2)}, u32[]{:S(2)}) collective-permute-start(bf16[192,512]{1,0:T(8,128)(2,1)S(1)} %join_globals.3.refs_0_.refs_4_), channel_id=1, source_target_pairs={{0,2},{2,0},{4,6},{6,4},{8,10},{10,8},{12,14},{14,12},{16,18},{18,... | collective-permute-start | bytes 589832 | tf_op jit(solution)/shard_map/ppermute | solution.py:46
  178.4 2.0 %collective-permute-start.31 = (bf16[192,512]{1,0:T(8,128)(2,1)S(1)}, bf16[192,512]{1,0:T(8,128)(2,1)S(1)}, u32[]{:S(2)}, u32[]{:S(2)}) collective-permute-start(bf16[192,512]{1,0:T(8,128)(2,1)S(1)} %collective-permute-done.25.refs_0_.refs_5_), channel_id=1, source_target_pairs={{0,2},{2,0},{4,6},{6,4},{8,10},{10,8},{12,14},{14,12},{16,18},{18,... | collective-permute-start | bytes 589832 | tf_op jit(solution)/shard_map/ppermute | solution.py:46

commit v5 on v4

--- a/solution.py
+++ b/solution.py
@@ -22,6 +22,7 @@
 VMEM_BYTES = 28 * 2**20
 FAR_STAYS = False
 GLOBALS_STAY = False
+AHEAD = 2
 TOTAL_LEAST = 2.0**-80
 TOTAL_MOST = 2.0**100
 
@@ -132,7 +133,7 @@
         compiler_params=params(),
         cost_estimate=cost(2**20, 4 * rows * width * 2),
         name="prepare_keys_values",
-    )(off_chip(keep_row), off_chip(keys), off_chip(values))
+    )(keep_row, off_chip(keys), off_chip(values))
 
 
 def forward_kernel(near, parts, own, first, last, kept, resident, waits, *refs):
@@ -185,12 +186,12 @@
 
     totals = jnp.ones((rows, HD), F32)
     order = [(head, number) for head in range(GROUP) for number in range(len(wide_keys))]
-    ahead = scores_of(*order[0])
+    ahead = [scores_of(*step) for step in order[:AHEAD]]
     mixed = None
     for place, (head, number) in enumerate(order):
-        scores = ahead
-        if place + 1 < len(order):
-            ahead = scores_of(*order[place + 1])
+        scores = ahead.pop(0)
+        if place + AHEAD < len(order):
+            ahead.append(scores_of(*order[place + AHEAD]))
         expo = jnp.exp2(scores * EXPONENT)
         if own and number == 0:
             expo = jnp.where(visible, expo, 0.0)
@@ -371,7 +372,8 @@
         diags = [jnp.zeros((rows, HD), F32)] * later
 
     gradients, diagonals = [], []
-    for head in range(GROUP):
+
+    def read_head(head):
         here = slice(head * HD, (head + 1) * HD)
         stack = slice(head * rows, (head + 1) * rows)
         if first:
@@ -393,21 +395,45 @@
             scaled_diag = diag_ref[:, head : head + 1]
         grad_stack[stack, :] = grad_bf
         q_stack[stack, :] = q_ref[:, here]
-        start = 0
-        d_query = None
-        for k, v in zip(key_list, value_list):
-            columns = slice(start, start + k.shape[0])
-            d_probs = dot_nt(grad_bf, v)
-            d_scores = (p_ref[pl.ds(base + head * rows, rows), columns].astype(F32) * (d_probs - scaled_diag)).astype(BF16)
-            ds_ref[stack, columns] = d_scores
-            part = dot_nn(d_scores, k)
-            d_query = part if d_query is None else d_query + part
-            start += k.shape[0]
-        if not first:
-            d_query = d_query + dq_ref[:, here]
-        if last:
-            d_query = d_query * SCALING
-        dq_out[:, here] = d_query.astype(dq_out.dtype)
+        gradients.append(grad_bf)
+        diagonals.append(scaled_diag)
+
+    def d_probs_of(head, number):
+        if first:
+            return dot_nt(gradients[head], value_list[number])
+        return dot_nt(grad_stack[head * rows : (head + 1) * rows, :], value_list[number])
+
+    order = [(head, number) for head in range(GROUP) for number in range(len(key_list))]
+    if not first:
+        for head in range(GROUP):
+            read_head(head)
+        ahead = [d_probs_of(*step) for step in order[:AHEAD]]
+    d_query = None
+    for place, (head, number) in enumerate(order):
+        if first:
+            if number == 0:
+                read_head(head)
+            d_probs = d_probs_of(head, number)
+        else:
+            d_probs = ahead.pop(0)
+            if place + AHEAD < len(order):
+                ahead.append(d_probs_of(*order[place + AHEAD]))
+        here = slice(head * HD, (head + 1) * HD)
+        stack = slice(head * rows, (head + 1) * rows)
+        k = key_list[number]
+        start = sum(x.shape[0] for x in key_list[:number])
+        columns = slice(start, start + k.shape[0])
+        exponentials = p_ref[pl.ds(base + head * rows, rows), columns].astype(F32)
+        d_scores = (exponentials * (d_probs - diagonals[head])).astype(BF16)
+        ds_ref[stack, columns] = d_scores
+        part = dot_nn(d_scores, k)
+        d_query = part if number == 0 else d_query + part
+        if number + 1 == len(key_list):
+            if not first:
+                d_query = d_query + dq_ref[:, here]
+            if last:
+                d_query = d_query * SCALING
+            dq_out[:, here] = d_query.astype(dq_out.dtype)
     if first:
         for (_, diag_out), diag in zip(later_outs, diags):
             diag_out[...] = diag
@@ -684,7 +710,7 @@
     place = lax.axis_index("seq")
     core = (place & 1).reshape(1)
     global_count = global_positions.shape[0]
-    keep_row = key_keep.reshape(1, rows)
+    keep_row = off_chip(key_keep.reshape(1, rows))
     gain_row = gain.reshape(1, -1)
     queries, cotangent = off_chip(queries), off_chip(cotangent)
 

time: 182 us -> 178 us (0.978)
  Pallas kernels: 119 us -> 114 us
    pallas_call x3, Pallas kernels: 45.2 us -> 40.3 us  [backward_phase(): pl.pallas_call(functools.partial(backward_kernel, len(near), len(parts),...]
  transfers between devices with their start and end apart: 32 -> 32, of which waited for: 12 -> 13; matrix products, arithmetic and copies ran while one was open for 1% -> 1% of each run, Pallas kernels for 37% -> 35%
where the time goes in v5:
time: 178 us; the launch traced here: 177 us
  Pallas kernels  114 us (64%)
  starting transfers between devices  37.5 us (21%)
  waiting for transfers between devices  23.6 us (13%)
    pallas_call x3, Pallas kernels, forward_phase(): pl.pallas_call(functools.partial(forward_kernel, len(near), len(parts), k...  70.1 us
    pallas_call x3, Pallas kernels, backward_phase(): pl.pallas_call(functools.partial(backward_kernel, len(near), len(parts),...  40.3 us
    ppermute x32, starting transfers between devices, swap(): return lax.ppermute(block, axis, [(i, i ^ mask) for i in range(count)])  37.5 us
    ppermute x32, waiting for transfers between devices, swap(): return lax.ppermute(block, axis, [(i, i ^ mask) for i in range(count)])  23.6 us
  transfers between devices with their start and end apart: 32, of which 13 were waited for; matrix products, arithmetic and copies ran while one was open for 1% of the time, Pallas kernels for 35%

profile of v5, /device:TPU:0, one launch (start us, length us, event | category | flops | bytes accessed | tf_op | source)
XLA Modules:
  0.0 177.3 jit_solution(11967558912731235723)
XLA Ops:
  0.6 1.2 prepare_keys_values.1.own_ref
  1.8 0.5 collective-permute-start
  2.3 0.7 broadcast_xor_fusion
  3.0 0.1 iota_compare_fusion
  3.1 0.8 broadcast_in_dim.26
  3.9 0.1 select_reduce_fusion
  4.0 0.1 sub.34
  4.1 0.1 sub.37
  4.2 0.0 collective-permute-done.partner_ref.refs_4_.refs_5_.refs_6_.refs_7_
  4.2 0.4 pick_globals.1
  4.6 2.7 %collective-permute-start.4 = (bf16[512,512]{1,0:T(8,128)(2,1)S(1)}, bf16[512,512]{1,0:T(8,128)(2,1)S(1)}, u32[]{:S(2)}, u32[]{:S(2)}) collective-permute-start(bf16[512,512]{1,0:T(8,128)(2,1)S(1)} %get-tuple-element.49), channel_id=1, source_target_pairs={{0,8},{2,10},{4,12},{6,14},{8,0},{10,2},{12,4},{14,6},{16,24},{18,... | collective-permute-start | bytes 1572872 | tf_op jit(solution)/shard_map/ppermute | solution.py:47
  7.3 1.5 collective-permute-start.3
  8.8 2.6 %collective-permute-start.1 = (bf16[512,512]{1,0:T(8,128)(2,1)S(1)}, bf16[512,512]{1,0:T(8,128)(2,1)S(1)}, u32[]{:S(2)}, u32[]{:S(2)}) collective-permute-start(bf16[512,512]{1,0:T(8,128)(2,1)S(1)} %get-tuple-element.49), channel_id=1, source_target_pairs={{0,16},{2,18},{4,20},{6,22},{8,24},{10,26},{12,28},{14,30},{16,0},... | collective-permute-start | bytes 1572872 | tf_op jit(solution)/shard_map/ppermute | solution.py:47
  11.4 0.5 collective-permute-start.2
  11.9 15.7 %forward_own.1 = (bf16[8192,512]{1,0:T(8,128)(2,1)}, f32[256,4096]{1,0:T(8,128)S(1)}, f32[256,512]{1,0:T(8,128)S(1)}, f32[256,512]{1,0:T(8,128)S(1)}) custom-call(bf16[192,512]{1,0:T(8,128)(2,1)S(1)} %get-tuple-element.50.refs_0_, bf16[256,4096]{1,0:T(8,128)(2,1)} %refs_2_.3, bf16[256,512]{1,0:T(8,128)(2,1)} %refs_4_.1, bf16[256,512]{1,0:T(8,128)(2,1)} %refs_5_.1, ...), custom_call_target="tpu_custom_call" | custom-call | flops 4294967296 | bytes 8388608 | tf_op jit(solution)/shard_map/forward_own/pallas_call | solution.py:319
  27.7 0.5 collective-permute-start.5
  28.2 0.5 collective-permute-start.6
  28.7 1.1 collective-permute-done.4.refs_4_.refs_5_.refs_6_
  29.7 3.1 %collective-permute-start.7 = (bf16[48,512]{1,0:T(8,128)(2,1)S(1)}, bf16[48,512]{1,0:T(8,128)(2,1)S(1)}, u32[]{:S(2)}, u32[]{:S(2)}) collective-permute-start(bf16[48,512]{1,0:T(8,128)(2,1)S(1)} %get-tuple-element.53.refs_0_), channel_id=1, source_target_pairs={{0,24},{2,26},{4,28},{6,30},{8,16},{10,18},{12,20},{14,22},{16,8},... | collective-permute-start | bytes 147464 | tf_op jit(solution)/shard_map/ppermute | solution.py:47
  32.8 24.4 %forward_partners.1 = (bf16[8192,512]{1,0:T(8,128)(2,1)}, f32[256,4096]{1,0:T(8,128)S(1)}, f32[256,512]{1,0:T(8,128)S(1)}, f32[256,512]{1,0:T(8,128)S(1)}) custom-call(bf16[48,512]{1,0:T(8,128)(2,1)S(1)} %get-tuple-element.53.refs_0_, bf16[256,4096]{1,0:T(8,128)(2,1)} %refs_2_.3, bf16[512,512]{1,0:T(8,128)(2,1)S(1)} %collective-permute-done.3.refs_2_.refs_3_.refs_4_, ...), custom_call_target="tpu_custom_call" | custom-call | flops 4294967296 | bytes 8388608 | tf_op jit(solution)/shard_map/forward_partners/pallas_call | solution.py:319
  57.2 0.0 collective-permute-done.5.refs_2_
  57.2 0.0 collective-permute-done.6.refs_3_
  57.2 0.0 collective-permute-done.7.refs_4_
  57.3 0.8 collective-permute-start.10
  58.1 0.0 collective-permute-start.9
  58.1 3.7 %collective-permute-start.8 = (bf16[48,512]{1,0:T(8,128)(2,1)S(1)}, bf16[48,512]{1,0:T(8,128)(2,1)S(1)}, u32[]{:S(2)}, u32[]{:S(2)}) collective-permute-start(bf16[48,512]{1,0:T(8,128)(2,1)S(1)} %combine_globals.7.refs_0_), channel_id=1, source_target_pairs={{0,8},{2,10},{4,12},{6,14},{8,0},{10,2},{12,4},{14,6},{16,24},{18,... | collective-permute-start | bytes 147464 | tf_op jit(solution)/shard_map/ppermute | solution.py:47
  61.7 1.6 collective-permute-done.10.refs_3_
  63.3 0.8 collective-permute-done.9.refs_2_
  64.1 2.7 %collective-permute-start.11 = (bf16[192,512]{1,0:T(8,128)(2,1)S(1)}, bf16[192,512]{1,0:T(8,128)(2,1)S(1)}, u32[]{:S(2)}, u32[]{:S(2)}) collective-permute-start(bf16[192,512]{1,0:T(8,128)(2,1)S(1)} %join_globals.2.refs_4_.refs_5_), channel_id=1, source_target_pairs={{0,4},{2,6},{4,0},{6,2},{8,12},{10,14},{12,8},{14,10},{16,20},{18,... | collective-permute-start | bytes 589832 | tf_op jit(solution)/shard_map/ppermute | solution.py:47
  66.9 3.6 %collective-permute-done.11.refs_5_.refs_6_ = bf16[192,512]{1,0:T(8,128)(2,1)S(1)} collective-permute-done((bf16[192,512]{1,0:T(8,128)(2,1)S(1)}, bf16[192,512]{1,0:T(8,128)(2,1)S(1)}, u32[]{:S(2)}, u32[]{:S(2)}) %collective-permute-start.11) | collective-permute-done | bytes 196640 | tf_op jit(solution)/shard_map/ppermute | solution.py:47
  70.5 0.0 collective-permute-done.12.refs_6_.refs_7_
  70.5 1.4 collective-permute-done.13.refs_7_.refs_8_
  71.9 30.0 %forward_globals.1 = (bf16[8192,640]{1,0:T(8,128)(2,1)}, f32[256,4096]{1,0:T(8,128)}, f32[256,512]{1,0:T(8,128)S(1)}, f32[256,512]{1,0:T(8,128)S(1)}, f32[2,256]{1,0:T(2,128)S(1)}) custom-call(bf16[256,4096]{1,0:T(8,128)(2,1)} %refs_2_.3, bf16[512,512]{1,0:T(8,128)(2,1)S(1)} %collective-permute-done.1.refs_1_.refs_2_.refs_3_, ...), custom_call_target="tpu_custom_call" | custom-call | flops 5368709120 | bytes 10485760 | tf_op jit(solution)/shard_map/forward_globals/pallas_call | solution.py:319
  101.9 1.5 collective-permute-start.14
  103.4 2.1 %collective-permute-done.14.refs_14_ = f32[2,256]{1,0:T(2,128)S(1)} collective-permute-done((f32[2,256]{1,0:T(2,128)S(1)}, f32[2,256]{1,0:T(2,128)S(1)}, u32[]{:S(2)}, u32[]{:S(2)}) %collective-permute-start.14) | collective-permute-done | bytes 2080 | tf_op jit(solution)/shard_map/ppermute | solution.py:47
  105.5 19.3 %backward_globals.1 = (bf16[512,512]{1,0:T(8,128)(2,1)S(1)}, bf16[192,512]{1,0:T(8,128)(2,1)S(1)}, bf16[192,512]{1,0:T(8,128)(2,1)S(1)}, bf16[192,512]{1,0:T(8,1...) custom-call(bf16[256,4096]{1,0:T(8,128)(2,1)} %refs_2_.3, ...), custom_call_target="tpu_custom_call" | custom-call | flops 8053063680 | bytes 10485760 | tf_op jit(solution)/shard_map/backward_globals/pallas_call | solution.py:523
  124.8 0.0 collective-permute-start.16
  124.8 0.5 collective-permute-start.15
  125.3 0.9 collective-permute-done.16.refs_1_
  126.2 0.1 combine_globals.9
  126.3 2.1 %collective-permute-start.17 = (bf16[192,512]{1,0:T(8,128)(2,1)S(1)}, bf16[192,512]{1,0:T(8,128)(2,1)S(1)}, u32[]{:S(2)}, u32[]{:S(2)}) collective-permute-start(bf16[192,512]{1,0:T(8,128)(2,1)S(1)} %combine_globals.9), channel_id=1, source_target_pairs={{0,4},{2,6},{4,0},{6,2},{8,12},{10,14},{12,8},{14,10},{16,20},{18,... | collective-permute-start | bytes 589832 | tf_op jit(solution)/shard_map/ppermute | solution.py:47
  128.4 1.5 collective-permute-start.24
  129.9 3.6 %collective-permute-done.17.refs_1_ = bf16[192,512]{1,0:T(8,128)(2,1)S(1)} collective-permute-done((bf16[192,512]{1,0:T(8,128)(2,1)S(1)}, bf16[192,512]{1,0:T(8,128)(2,1)S(1)}, u32[]{:S(2)}, u32[]{:S(2)}) %collective-permute-start.17) | collective-permute-done | bytes 196640 | tf_op jit(solution)/shard_map/ppermute | solution.py:47
  133.6 1.6 collective-permute-start.18
  135.2 0.9 collective-permute-start.19
  136.1 2.0 %collective-permute-start.20 = (bf16[48,512]{1,0:T(8,128)(2,1)S(1)}, bf16[48,512]{1,0:T(8,128)(2,1)S(1)}, u32[]{:S(2)}, u32[]{:S(2)}) collective-permute-start(bf16[48,512]{1,0:T(8,128)(2,1)S(1)} %get-tuple-element.72.refs_0_), channel_id=1, source_target_pairs={{0,24},{2,26},{4,28},{6,30},{8,16},{10,18},{12,20},{14,22},{16,8},... | collective-permute-start | bytes 147464 | tf_op jit(solution)/shard_map/ppermute | solution.py:47
  138.0 10.3 %backward_partners.1 = (bf16[512,512]{1,0:T(8,128)(2,1)S(1)}, bf16[512,512]{1,0:T(8,128)(2,1)S(1)}, f32[256,4096]{1,0:T(8,128)S(1)}) custom-call(bf16[48,512]{1,0:T(8,128)(2,1)S(1)} %get-tuple-element.72.refs_0_, bf16[256,4096]{1,0:T(8,128)(2,1)} %refs_2_.3, bf16[8192,512]{1,0:T(8,128)(2,1)} %get-tuple-element.73.refs_2_, ...), custom_call_target="tpu_custom_call" | custom-call | flops 6442450944 | bytes 8388608 | tf_op jit(solution)/shard_map/backward_partners/pallas_call | solution.py:523
  148.4 1.9 %collective-permute-start.23 = (bf16[48,512]{1,0:T(8,128)(2,1)S(1)}, bf16[48,512]{1,0:T(8,128)(2,1)S(1)}, u32[]{:S(2)}, u32[]{:S(2)}) collective-permute-start(bf16[48,512]{1,0:T(8,128)(2,1)S(1)} %combine_globals.11.refs_0_), channel_id=1, source_target_pairs={{0,24},{2,26},{4,28},{6,30},{8,16},{10,18},{12,20},{14,22},{16,8},... | collective-permute-start | bytes 147464 | tf_op jit(solution)/shard_map/ppermute | solution.py:47
  150.3 0.2 collective-permute-start.22
  150.5 2.3 %collective-permute-start.21 = (bf16[48,512]{1,0:T(8,128)(2,1)S(1)}, bf16[48,512]{1,0:T(8,128)(2,1)S(1)}, u32[]{:S(2)}, u32[]{:S(2)}) collective-permute-start(bf16[48,512]{1,0:T(8,128)(2,1)S(1)} %combine_globals.11.refs_0_), channel_id=1, source_target_pairs={{0,8},{2,10},{4,12},{6,14},{8,0},{10,2},{12,4},{14,6},{16,24},{18,... | collective-permute-start | bytes 147464 | tf_op jit(solution)/shard_map/ppermute | solution.py:47
  152.9 0.4 collective-permute-start.26
  153.2 1.7 collective-permute-done.23.refs_3_
  154.9 1.7 collective-permute-start.27
  156.6 4.0 %collective-permute-done.22.refs_2_ = bf16[48,512]{1,0:T(8,128)(2,1)S(1)} collective-permute-done((bf16[48,512]{1,0:T(8,128)(2,1)S(1)}, bf16[48,512]{1,0:T(8,128)(2,1)S(1)}, u32[]{:S(2)}, u32[]{:S(2)}) %collective-permute-start.22) | collective-permute-done | bytes 49184 | tf_op jit(solution)/shard_map/ppermute | solution.py:47
  160.6 1.2 collective-permute-start.25
  161.9 10.7 %backward_own.1 = (f32[512,512]{1,0:T(8,128)S(1)}, bf16[512,512]{1,0:T(8,128)(2,1)S(1)}, bf16[256,4096]{1,0:T(8,128)(2,1)}) custom-call(bf16[192,512]{1,0:T(8,128)(2,1)S(1)} %join_globals.3.refs_0_.refs_4_, bf16[256,512]{1,0:T(8,128)(2,1)S(1)} %collective-permute-done.24.refs_1_.refs_2_, bf16[256,4096]{1,0:T(8,128)(2,1)} %refs_2_.3, ...), custom_call_target="tpu_custom_call" | custom-call | flops 6442450944 | bytes 8388608 | tf_op jit(solution)/shard_map/backward_own/pallas_call | solution.py:523
  172.6 0.8 collective-permute-done.28.refs_5_
  173.4 0.2 settle_partner_grads.1
  173.6 0.1 collective-permute-start.29
  173.7 0.5 collective-permute-start.30
  174.2 0.1 collective-permute-start.31
  174.3 1.6 collective-permute-done.30.refs_6_
  175.9 0.3 collective-permute-done.31.refs_7_
  176.2 1.2 finish_key_value_grads.1
  (31 shorter events, 0.4 us)
Async XLA Ops:
  1.8 2.3 %collective-permute-start = (bf16[512,512]{1,0:T(8,128)(2,1)S(1)}, bf16[512,512]{1,0:T(8,128)(2,1)S(1)}, u32[]{:S(2)}, u32[]{:S(2)}) collective-permute-start(bf16[512,512]{1,0:T(8,128)(2,1)S(1)} %prepare_keys_values.1.own_ref), channel_id=1, source_target_pairs={{0,2},{2,0},{4,6},{6,4},{8,10},{10,8},{12,14},{14,12},{16,18},{18,... | collective-permute-start | bytes 1572872 | tf_op jit(solution)/shard_map/ppermute | solution.py:47
  4.6 25.2 %collective-permute-start.4 = (bf16[512,512]{1,0:T(8,128)(2,1)S(1)}, bf16[512,512]{1,0:T(8,128)(2,1)S(1)}, u32[]{:S(2)}, u32[]{:S(2)}) collective-permute-start(bf16[512,512]{1,0:T(8,128)(2,1)S(1)} %get-tuple-element.49), channel_id=1, source_target_pairs={{0,8},{2,10},{4,12},{6,14},{8,0},{10,2},{12,4},{14,6},{16,24},{18,... | collective-permute-start | bytes 1572872 | tf_op jit(solution)/shard_map/ppermute | solution.py:47
  7.3 25.5 %collective-permute-start.3 = (bf16[512,512]{1,0:T(8,128)(2,1)S(1)}, bf16[512,512]{1,0:T(8,128)(2,1)S(1)}, u32[]{:S(2)}, u32[]{:S(2)}) collective-permute-start(bf16[512,512]{1,0:T(8,128)(2,1)S(1)} %get-tuple-element.49), channel_id=1, source_target_pairs={{0,4},{2,6},{4,0},{6,2},{8,12},{10,14},{12,8},{14,10},{16,20},{18,... | collective-permute-start | bytes 1572872 | tf_op jit(solution)/shard_map/ppermute | solution.py:47
  8.8 61.7 %collective-permute-start.1 = (bf16[512,512]{1,0:T(8,128)(2,1)S(1)}, bf16[512,512]{1,0:T(8,128)(2,1)S(1)}, u32[]{:S(2)}, u32[]{:S(2)}) collective-permute-start(bf16[512,512]{1,0:T(8,128)(2,1)S(1)} %get-tuple-element.49), channel_id=1, source_target_pairs={{0,16},{2,18},{4,20},{6,22},{8,24},{10,26},{12,28},{14,30},{16,0},... | collective-permute-start | bytes 1572872 | tf_op jit(solution)/shard_map/ppermute | solution.py:47
  11.4 16.2 %collective-permute-start.2 = (bf16[192,512]{1,0:T(8,128)(2,1)S(1)}, bf16[192,512]{1,0:T(8,128)(2,1)S(1)}, u32[]{:S(2)}, u32[]{:S(2)}) collective-permute-start(bf16[192,512]{1,0:T(8,128)(2,1)S(1)} %get-tuple-element.50.refs_0_), channel_id=1, source_target_pairs={{0,4},{2,6},{4,0},{6,2},{8,12},{10,14},{12,8},{14,10},{16,20},{18,... | collective-permute-start | bytes 589832 | tf_op jit(solution)/shard_map/ppermute | solution.py:47
  27.7 29.6 %collective-permute-start.5 = (bf16[48,512]{1,0:T(8,128)(2,1)S(1)}, bf16[48,512]{1,0:T(8,128)(2,1)S(1)}, u32[]{:S(2)}, u32[]{:S(2)}) collective-permute-start(bf16[48,512]{1,0:T(8,128)(2,1)S(1)} %get-tuple-element.58), channel_id=1, source_target_pairs={{0,8},{2,10},{4,12},{6,14},{8,0},{10,2},{12,4},{14,6},{16,24},{18,... | collective-permute-start | bytes 147464 | tf_op jit(solution)/shard_map/ppermute | solution.py:47
  28.2 29.0 %collective-permute-start.6 = (bf16[48,512]{1,0:T(8,128)(2,1)S(1)}, bf16[48,512]{1,0:T(8,128)(2,1)S(1)}, u32[]{:S(2)}, u32[]{:S(2)}) collective-permute-start(bf16[48,512]{1,0:T(8,128)(2,1)S(1)} %get-tuple-element.59), channel_id=1, source_target_pairs={{0,16},{2,18},{4,20},{6,22},{8,24},{10,26},{12,28},{14,30},{16,0},... | collective-permute-start | bytes 147464 | tf_op jit(solution)/shard_map/ppermute | solution.py:47
  29.7 27.5 %collective-permute-start.7 = (bf16[48,512]{1,0:T(8,128)(2,1)S(1)}, bf16[48,512]{1,0:T(8,128)(2,1)S(1)}, u32[]{:S(2)}, u32[]{:S(2)}) collective-permute-start(bf16[48,512]{1,0:T(8,128)(2,1)S(1)} %get-tuple-element.53.refs_0_), channel_id=1, source_target_pairs={{0,24},{2,26},{4,28},{6,30},{8,16},{10,18},{12,20},{14,22},{16,8},... | collective-permute-start | bytes 147464 | tf_op jit(solution)/shard_map/ppermute | solution.py:47
  32.8 37.7 %copy-start = (bf16[4096]{0:T(1024)(128)(2,1)S(1)}, bf16[4096]{0:T(1024)(128)(2,1)}, u32[]{:S(2)}) copy-start(bf16[4096]{0:T(1024)(128)(2,1)} %param.13) | copy-start | bytes 24580
  57.3 6.1 %collective-permute-start.10 = (bf16[48,512]{1,0:T(8,128)(2,1)S(1)}, bf16[48,512]{1,0:T(8,128)(2,1)S(1)}, u32[]{:S(2)}, u32[]{:S(2)}) collective-permute-start(bf16[48,512]{1,0:T(8,128)(2,1)S(1)} %combine_globals.7.refs_0_), channel_id=1, source_target_pairs={{0,24},{2,26},{4,28},{6,30},{8,16},{10,18},{12,20},{14,22},{16,8},... | collective-permute-start | bytes 147464 | tf_op jit(solution)/shard_map/ppermute | solution.py:47
  58.1 6.0 %collective-permute-start.9 = (bf16[48,512]{1,0:T(8,128)(2,1)S(1)}, bf16[48,512]{1,0:T(8,128)(2,1)S(1)}, u32[]{:S(2)}, u32[]{:S(2)}) collective-permute-start(bf16[48,512]{1,0:T(8,128)(2,1)S(1)} %combine_globals.7.refs_0_), channel_id=1, source_target_pairs={{0,16},{2,18},{4,20},{6,22},{8,24},{10,26},{12,28},{14,30},{16,0},... | collective-permute-start | bytes 147464 | tf_op jit(solution)/shard_map/ppermute | solution.py:47
  58.1 6.0 %collective-permute-start.8 = (bf16[48,512]{1,0:T(8,128)(2,1)S(1)}, bf16[48,512]{1,0:T(8,128)(2,1)S(1)}, u32[]{:S(2)}, u32[]{:S(2)}) collective-permute-start(bf16[48,512]{1,0:T(8,128)(2,1)S(1)} %combine_globals.7.refs_0_), channel_id=1, source_target_pairs={{0,8},{2,10},{4,12},{6,14},{8,0},{10,2},{12,4},{14,6},{16,24},{18,... | collective-permute-start | bytes 147464 | tf_op jit(solution)/shard_map/ppermute | solution.py:47
  64.1 6.4 %collective-permute-start.11 = (bf16[192,512]{1,0:T(8,128)(2,1)S(1)}, bf16[192,512]{1,0:T(8,128)(2,1)S(1)}, u32[]{:S(2)}, u32[]{:S(2)}) collective-permute-start(bf16[192,512]{1,0:T(8,128)(2,1)S(1)} %join_globals.2.refs_4_.refs_5_), channel_id=1, source_target_pairs={{0,4},{2,6},{4,0},{6,2},{8,12},{10,14},{12,8},{14,10},{16,20},{18,... | collective-permute-start | bytes 589832 | tf_op jit(solution)/shard_map/ppermute | solution.py:47
  66.9 3.7 %collective-permute-start.12 = (bf16[192,512]{1,0:T(8,128)(2,1)S(1)}, bf16[192,512]{1,0:T(8,128)(2,1)S(1)}, u32[]{:S(2)}, u32[]{:S(2)}) collective-permute-start(bf16[192,512]{1,0:T(8,128)(2,1)S(1)} %join_globals.2.refs_4_.refs_5_), channel_id=1, source_target_pairs={{0,2},{2,0},{4,6},{6,4},{8,10},{10,8},{12,14},{14,12},{16,18},{18,... | collective-permute-start | bytes 589832 | tf_op jit(solution)/shard_map/ppermute | solution.py:47
  70.5 1.4 collective-permute-start.13
  101.9 3.6 %collective-permute-start.14 = (f32[2,256]{1,0:T(2,128)S(1)}, f32[2,256]{1,0:T(2,128)S(1)}, u32[]{:S(2)}, u32[]{:S(2)}) collective-permute-start(f32[2,256]{1,0:T(2,128)S(1)} %get-tuple-element.65.refs_13_), channel_id=1, source_target_pairs={{0,1},{1,0},{2,3},{3,2},{4,5},{5,4},{6,7},{7,6},{8,9},{9,8},{10,11... | collective-permute-start | bytes 6152 | tf_op jit(solution)/shard_map/ppermute | solution.py:47
  124.8 1.4 collective-permute-start.16
  124.8 5.1 %collective-permute-start.15 = (bf16[192,512]{1,0:T(8,128)(2,1)S(1)}, bf16[192,512]{1,0:T(8,128)(2,1)S(1)}, u32[]{:S(2)}, u32[]{:S(2)}) collective-permute-start(bf16[192,512]{1,0:T(8,128)(2,1)S(1)} %get-tuple-element.69), channel_id=1, source_target_pairs={{0,2},{2,0},{4,6},{6,4},{8,10},{10,8},{12,14},{14,12},{16,18},{18,... | collective-permute-start | bytes 589832 | tf_op jit(solution)/shard_map/ppermute | solution.py:47
  126.3 7.3 %collective-permute-start.17 = (bf16[192,512]{1,0:T(8,128)(2,1)S(1)}, bf16[192,512]{1,0:T(8,128)(2,1)S(1)}, u32[]{:S(2)}, u32[]{:S(2)}) collective-permute-start(bf16[192,512]{1,0:T(8,128)(2,1)S(1)} %combine_globals.9), channel_id=1, source_target_pairs={{0,4},{2,6},{4,0},{6,2},{8,12},{10,14},{12,8},{14,10},{16,20},{18,... | collective-permute-start | bytes 589832 | tf_op jit(solution)/shard_map/ppermute | solution.py:47
  128.4 33.5 %collective-permute-start.24 = (bf16[256,512]{1,0:T(8,128)(2,1)S(1)}, bf16[256,512]{1,0:T(8,128)(2,1)S(1)}, u32[]{:S(2)}, u32[]{:S(2)}) collective-permute-start(bf16[256,512]{1,0:T(8,128)(2,1)S(1)} %get-tuple-element.95), channel_id=1, source_target_pairs={{0,16},{2,18},{4,20},{6,22},{8,24},{10,26},{12,28},{14,30},{16,0},... | collective-permute-start | bytes 786440 | tf_op jit(solution)/shard_map/ppermute | solution.py:47
  133.6 14.7 %collective-permute-start.18 = (bf16[48,512]{1,0:T(8,128)(2,1)S(1)}, bf16[48,512]{1,0:T(8,128)(2,1)S(1)}, u32[]{:S(2)}, u32[]{:S(2)}) collective-permute-start(bf16[48,512]{1,0:T(8,128)(2,1)S(1)} %get-tuple-element.79), channel_id=1, source_target_pairs={{0,8},{2,10},{4,12},{6,14},{8,0},{10,2},{12,4},{14,6},{16,24},{18,... | collective-permute-start | bytes 147464 | tf_op jit(solution)/shard_map/ppermute | solution.py:47
  135.2 13.2 %collective-permute-start.19 = (bf16[48,512]{1,0:T(8,128)(2,1)S(1)}, bf16[48,512]{1,0:T(8,128)(2,1)S(1)}, u32[]{:S(2)}, u32[]{:S(2)}) collective-permute-start(bf16[48,512]{1,0:T(8,128)(2,1)S(1)} %get-tuple-element.80), channel_id=1, source_target_pairs={{0,16},{2,18},{4,20},{6,22},{8,24},{10,26},{12,28},{14,30},{16,0},... | collective-permute-start | bytes 147464 | tf_op jit(solution)/shard_map/ppermute | solution.py:47
  136.1 12.3 %collective-permute-start.20 = (bf16[48,512]{1,0:T(8,128)(2,1)S(1)}, bf16[48,512]{1,0:T(8,128)(2,1)S(1)}, u32[]{:S(2)}, u32[]{:S(2)}) collective-permute-start(bf16[48,512]{1,0:T(8,128)(2,1)S(1)} %get-tuple-element.72.refs_0_), channel_id=1, source_target_pairs={{0,24},{2,26},{4,28},{6,30},{8,16},{10,18},{12,20},{14,22},{16,8},... | collective-permute-start | bytes 147464 | tf_op jit(solution)/shard_map/ppermute | solution.py:47
  148.4 6.5 %collective-permute-start.23 = (bf16[48,512]{1,0:T(8,128)(2,1)S(1)}, bf16[48,512]{1,0:T(8,128)(2,1)S(1)}, u32[]{:S(2)}, u32[]{:S(2)}) collective-permute-start(bf16[48,512]{1,0:T(8,128)(2,1)S(1)} %combine_globals.11.refs_0_), channel_id=1, source_target_pairs={{0,24},{2,26},{4,28},{6,30},{8,16},{10,18},{12,20},{14,22},{16,8},... | collective-permute-start | bytes 147464 | tf_op jit(solution)/shard_map/ppermute | solution.py:47
  150.3 10.3 %collective-permute-start.22 = (bf16[48,512]{1,0:T(8,128)(2,1)S(1)}, bf16[48,512]{1,0:T(8,128)(2,1)S(1)}, u32[]{:S(2)}, u32[]{:S(2)}) collective-permute-start(bf16[48,512]{1,0:T(8,128)(2,1)S(1)} %combine_globals.11.refs_0_), channel_id=1, source_target_pairs={{0,16},{2,18},{4,20},{6,22},{8,24},{10,26},{12,28},{14,30},{16,0},... | collective-permute-start | bytes 147464 | tf_op jit(solution)/shard_map/ppermute | solution.py:47
  150.5 10.1 %collective-permute-start.21 = (bf16[48,512]{1,0:T(8,128)(2,1)S(1)}, bf16[48,512]{1,0:T(8,128)(2,1)S(1)}, u32[]{:S(2)}, u32[]{:S(2)}) collective-permute-start(bf16[48,512]{1,0:T(8,128)(2,1)S(1)} %combine_globals.11.refs_0_), channel_id=1, source_target_pairs={{0,8},{2,10},{4,12},{6,14},{8,0},{10,2},{12,4},{14,6},{16,24},{18,... | collective-permute-start | bytes 147464 | tf_op jit(solution)/shard_map/ppermute | solution.py:47
  152.9 19.7 %collective-permute-start.26 = (bf16[256,512]{1,0:T(8,128)(2,1)S(1)}, bf16[256,512]{1,0:T(8,128)(2,1)S(1)}, u32[]{:S(2)}, u32[]{:S(2)}) collective-permute-start(bf16[256,512]{1,0:T(8,128)(2,1)S(1)} %get-tuple-element.94), channel_id=1, source_target_pairs={{0,16},{2,18},{4,20},{6,22},{8,24},{10,26},{12,28},{14,30},{16,0},... | collective-permute-start | bytes 786440 | tf_op jit(solution)/shard_map/ppermute | solution.py:47
  154.9 17.7 %collective-permute-start.27 = (bf16[512,512]{1,0:T(8,128)(2,1)S(1)}, bf16[512,512]{1,0:T(8,128)(2,1)S(1)}, u32[]{:S(2)}, u32[]{:S(2)}) collective-permute-start(bf16[512,512]{1,0:T(8,128)(2,1)S(1)} %get-tuple-element.87), channel_id=1, source_target_pairs={{0,4},{2,6},{4,0},{6,2},{8,12},{10,14},{12,8},{14,10},{16,20},{18,... | collective-permute-start | bytes 1572872 | tf_op jit(solution)/shard_map/ppermute | solution.py:47
  160.6 12.8 %collective-permute-start.28 = (bf16[512,512]{1,0:T(8,128)(2,1)S(1)}, bf16[512,512]{1,0:T(8,128)(2,1)S(1)}, u32[]{:S(2)}, u32[]{:S(2)}) collective-permute-start(bf16[512,512]{1,0:T(8,128)(2,1)S(1)} %get-tuple-element.88), channel_id=1, source_target_pairs={{0,8},{2,10},{4,12},{6,14},{8,0},{10,2},{12,4},{14,6},{16,24},{18,... | collective-permute-start | bytes 1572872 | tf_op jit(solution)/shard_map/ppermute | solution.py:47
  160.6 11.9 %collective-permute-start.25 = (bf16[192,512]{1,0:T(8,128)(2,1)S(1)}, bf16[192,512]{1,0:T(8,128)(2,1)S(1)}, u32[]{:S(2)}, u32[]{:S(2)}) collective-permute-start(bf16[192,512]{1,0:T(8,128)(2,1)S(1)} %join_globals.3.refs_0_.refs_4_), channel_id=1, source_target_pairs={{0,4},{2,6},{4,0},{6,2},{8,12},{10,14},{12,8},{14,10},{16,20},{18,... | collective-permute-start | bytes 589832 | tf_op jit(solution)/shard_map/ppermute | solution.py:47
  173.6 2.5 %collective-permute-start.29 = (bf16[512,512]{1,0:T(8,128)(2,1)S(1)}, bf16[512,512]{1,0:T(8,128)(2,1)S(1)}, u32[]{:S(2)}, u32[]{:S(2)}) collective-permute-start(bf16[512,512]{1,0:T(8,128)(2,1)S(1)} %get-tuple-element.91), channel_id=1, source_target_pairs={{0,2},{2,0},{4,6},{6,4},{8,10},{10,8},{12,14},{14,12},{16,18},{18,... | collective-permute-start | bytes 1572872 | tf_op jit(solution)/shard_map/ppermute | solution.py:47
  173.7 2.2 %collective-permute-start.30 = (bf16[192,512]{1,0:T(8,128)(2,1)S(1)}, bf16[192,512]{1,0:T(8,128)(2,1)S(1)}, u32[]{:S(2)}, u32[]{:S(2)}) collective-permute-start(bf16[192,512]{1,0:T(8,128)(2,1)S(1)} %join_globals.3.refs_0_.refs_4_), channel_id=1, source_target_pairs={{0,2},{2,0},{4,6},{6,4},{8,10},{10,8},{12,14},{14,12},{16,18},{18,... | collective-permute-start | bytes 589832 | tf_op jit(solution)/shard_map/ppermute | solution.py:47
  174.2 2.0 %collective-permute-start.31 = (bf16[192,512]{1,0:T(8,128)(2,1)S(1)}, bf16[192,512]{1,0:T(8,128)(2,1)S(1)}, u32[]{:S(2)}, u32[]{:S(2)}) collective-permute-start(bf16[192,512]{1,0:T(8,128)(2,1)S(1)} %collective-permute-done.25.refs_0_.refs_5_), channel_id=1, source_target_pairs={{0,2},{2,0},{4,6},{6,4},{8,10},{10,8},{12,14},{14,12},{16,18},{18,... | collective-permute-start | bytes 589832 | tf_op jit(solution)/shard_map/ppermute | solution.py:47
